TPU v7x, 32 devices: a whole 2x2x4 slice. The times are simulated.
32 devices in a mesh: gz: 16 (over z, y, core), gy: 2 (over x).
Axes of the slice: x: 2, y: 2, z: 4, core: 2. Of those that a mesh axis runs over, the one named last changes fastest.
Arguments:
- measured: float32 [128, 512, 512], P('gz', 'gy'), may hold values from 0.2 to 5
- transfer_real: float32 [128, 512, 256], P('gz', 'gy'), may hold values from 0.6 to 1
- transfer_imag: float32 [128, 512, 256], P('gz', 'gy'), may hold values from -0.2 to 0.2
Outputs:
- estimate: float32 [128, 512, 512], P('gz', 'gy')
All inputs are finite; a program needn't handle non-finite values.
Results may differ from a plain program's by a relative error of at most 0.0002.
Values sent between devices are 32-bit elements; how exact they have to be, the bound alone decides.
No kernel may reach another device: no remote copies, remote signals or barrier semaphores. Data moves between devices by JAX's collectives and lax.ppermute only.
A program may use at most 128 MiB of HBM per device.

v0:
```python
import math

import jax
import jax.numpy as jnp
from jax import lax
from jax.sharding import PartitionSpec as P

ITERS = 2
RADIUS = 4


SIGMA = 1.5
FLOOR = 0.1


def product(form, left, right):
    return jnp.einsum(
        form, left, right, precision=lax.Precision.HIGHEST, preferred_element_type=jnp.float32
    )


def gauss_weights():
    offsets = jnp.arange(-RADIUS, RADIUS + 1).astype(jnp.float32)
    weights = jnp.exp(-offsets * offsets / (2.0 * SIGMA * SIGMA))
    return weights / jnp.sum(weights)


def taps_along(padded, axis, length):
    weights = gauss_weights()
    total = weights[0] * lax.slice_in_dim(padded, 0, length, axis=axis)
    for offset in range(1, 2 * RADIUS + 1):
        total = total + weights[offset] * lax.slice_in_dim(
            padded, offset, offset + length, axis=axis
        )
    return total


def blur_local(values, axis):
    length = values.shape[axis]
    widths = [(0, 0)] * values.ndim
    widths[axis] = (RADIUS, RADIUS)
    return taps_along(jnp.pad(values, widths), axis, length)


def angles(length, count):
    position = jnp.arange(length, dtype=jnp.int32)
    frequency = jnp.arange(count, dtype=jnp.int32)
    phase = position[:, None] * frequency[None, :] % length
    return phase.astype(jnp.float32) * (2.0 * math.pi / length)


def square_tables(length):
    angle = angles(length, length)
    cosine = jnp.cos(angle)
    sine = jnp.sin(angle)
    return ((cosine, sine), (cosine / length, sine / length))


def half_tables(length):
    half = length // 2
    angle = angles(length, half)
    cosine = jnp.cos(angle)
    sine = jnp.sin(angle)
    ahead = jnp.stack((cosine, -sine), axis=1)
    weight = jnp.where(jnp.arange(half) == 0, 1.0, 2.0).astype(jnp.float32) / length
    behind = jnp.stack((weight[:, None] * cosine.T, -weight[:, None] * sine.T), axis=0)
    return (ahead, behind)


def shaped(table, shape):
    return (table[0].reshape(shape), table[1].reshape(shape))


def turn(form, values, table, forward):
    first = product(form, values, table[0])
    second = product(form, values, table[1])
    if forward:
        return jnp.stack(
            (first[..., 0, :] + second[..., 1, :], first[..., 1, :] - second[..., 0, :]), axis=-2
        )
    return jnp.stack(
        (first[..., 0, :] - second[..., 1, :], first[..., 1, :] + second[..., 0, :]), axis=-2
    )


def across_z(values):
    return lax.all_to_all(values, "gz", split_axis=0, concat_axis=0, tiled=True)


def across_y(values):
    return lax.all_to_all(values, "gy", split_axis=0, concat_axis=0, tiled=True)


def forward_zfirst(field, ahead, y_fwd, z_fwd):
    z_local, y_local, x_len = field.shape
    z_devs = lax.axis_size("gz")
    y_devs = lax.axis_size("gy")
    x_share = ahead.shape[2] // z_devs
    z_len = z_local * z_devs
    y_len = y_local * y_devs
    z_share = z_len // y_devs
    values = product("zyx,xrgq->gzyrq", field, ahead.reshape(x_len, 2, z_devs, x_share))
    values = across_z(values).reshape(z_len, y_local, 2, x_share)
    values = turn("zyrq,zgk->gykrq", values, shaped(z_fwd, (z_len, y_devs, z_share)), True)
    values = across_y(values).reshape(y_len, z_share, 2, x_share)
    return turn("yjrq,yk->kjrq", values, y_fwd, True)


def inverse_zfirst(spectrum, behind, y_back, z_back, z_local, y_local):
    z_devs = lax.axis_size("gz")
    y_devs = lax.axis_size("gy")
    y_len, z_share, pair, x_share = spectrum.shape
    x_len = behind.shape[2]
    values = turn("kjrq,kgy->gyjrq", spectrum, shaped(y_back, (y_len, y_devs, y_local)), False)
    values = across_y(values)
    values = turn(
        "syjrq,sjgz->gzyrq", values, shaped(z_back, (y_devs, z_share, z_devs, z_local)), False
    )
    values = across_z(values)
    return product("szyrq,rsqx->zyx", values, behind.reshape(2, z_devs, x_share, x_len))


def gains_zfirst(transfer_real, transfer_imag):
    z_local, y_local, half = transfer_real.shape
    z_devs = lax.axis_size("gz")
    y_devs = lax.axis_size("gy")
    x_share = half // z_devs
    z_len = z_local * z_devs
    z_share = z_len // y_devs
    stacked = (
        jnp.stack((transfer_real, transfer_imag), axis=2)
        .reshape(z_local, y_local, 2, z_devs, x_share)
        .transpose(3, 0, 1, 2, 4)
    )
    stacked = (
        across_z(stacked).reshape(y_devs, z_share, y_local, 2, x_share).transpose(0, 2, 1, 3, 4)
    )
    return across_y(stacked).reshape(y_local * y_devs, z_share, 2, x_share)


def apply_gains(spectrum, gains, conjugate):
    spec_real = spectrum[..., 0, :]
    spec_imag = spectrum[..., 1, :]
    gain_real = gains[..., 0, :]
    gain_imag = gains[..., 1, :]
    if conjugate:
        return jnp.stack(
            (
                spec_real * gain_real + spec_imag * gain_imag,
                spec_imag * gain_real - spec_real * gain_imag,
            ),
            axis=-2,
        )
    return jnp.stack(
        (
            spec_real * gain_real - spec_imag * gain_imag,
            spec_real * gain_imag + spec_imag * gain_real,
        ),
        axis=-2,
    )


def on_device(measured, transfer_real, transfer_imag):
    z_local, y_local, x_len = measured.shape
    z_len = z_local * lax.axis_size("gz")
    y_len = y_local * lax.axis_size("gy")
    ahead, behind = half_tables(x_len)
    y_fwd, y_back = square_tables(y_len)
    z_fwd, z_back = square_tables(z_len)
    soft_x = blur_local(behind, 2)
    soft_y = (blur_local(y_back[0], 1), blur_local(y_back[1], 1))
    soft_z = (blur_local(z_back[0], 1), blur_local(z_back[1], 1))
    gains = gains_zfirst(transfer_real, transfer_imag)
    estimate = measured
    for iteration in range(ITERS):
        spectrum = forward_zfirst(estimate, ahead, y_fwd, z_fwd)
        blurred = inverse_zfirst(
            apply_gains(spectrum, gains, False), behind, y_back, z_back, z_local, y_local
        )
        ratio = measured / jnp.maximum(blurred, FLOOR)
        spectrum = forward_zfirst(ratio, ahead, y_fwd, z_fwd)
        correction = inverse_zfirst(
            apply_gains(spectrum, gains, True), soft_x, soft_y, soft_z, z_local, y_local
        )
        estimate = estimate * correction
    return estimate


def solution(mesh):
    return jax.shard_map(
        on_device,
        mesh=mesh,
        in_specs=(P("gz", "gy", None), P("gz", "gy", None), P("gz", "gy", None)),
        out_specs=P("gz", "gy", None),
        check_vma=False,
    )
```

profile of v0, /device:TPU:0, one launch (start us, length us, event | category | flops | bytes accessed | tf_op | source)
XLA Modules:
  0.0 1700.6 jit_solution(16490855223313157087)
XLA Ops:
  2.2 8.9 fusion.134
  13.6 7.4 all-to-all-start
  30.7 68.0 %all-to-all-done = f32[16,8,256,2,16]{2,4,1,3,0:T(8,128)} async-done(((f32[16,8,256,2,16]{2,4,1,3,0:T(8,128)}), f32[16,8,256,2,16]{2,4,1,3,0:T(8,128)}, u32[]{:S(2)}, u32[]{:S(2)}) %all-to-all-start) | async-done | bytes 4194336 | tf_op jit(solution)/shard_map/all_to_all | solution.py:87
  98.7 19.9 %all-to-all-start.2 = ((f32[16,8,256,2,16]{2,4,1,3,0:T(8,128)}), f32[16,8,256,2,16]{2,4,1,3,0:T(8,128)}, u32[]{:S(2)}, u32[]{:S(2)}) async-start(f32[16,8,256,2,16]{2,4,1,3,0:T(8,128)} %copy.83), calls=%async_computation.2 | async-start | bytes 8388608 | tf_op jit(solution)/shard_map/all_to_all | solution.py:87
  118.7 7.7 fusion.83
  126.4 7.7 fusion.80
  137.7 58.6 %all-to-all-done.2 = f32[16,8,256,2,16]{2,4,1,3,0:T(8,128)} async-done(((f32[16,8,256,2,16]{2,4,1,3,0:T(8,128)}), f32[16,8,256,2,16]{2,4,1,3,0:T(8,128)}, u32[]{:S(2)}, u32[]{:S(2)}) %all-to-all-start.2) | async-done | bytes 4194336 | tf_op jit(solution)/shard_map/all_to_all | solution.py:87
  206.8 43.7 %all-to-all-done.1 = f32[2,256,64,2,16]{1,2,4,3,0:T(8,128)} async-done(((f32[2,256,64,2,16]{1,2,4,3,0:T(8,128)}), f32[2,256,64,2,16]{1,2,4,3,0:T(8,128)}, u32[]{:S(2)}, u32[]{:S(2)}) %all-to-all-start.1) | async-done | bytes 4194336 | tf_op jit(solution)/shard_map/all_to_all | solution.py:91
  250.5 6.0 all-to-all-start.3
  259.3 12.0 fusion.174
  271.3 12.0 fusion.180
  283.4 20.9 %all-to-all-done.3 = f32[2,256,64,2,16]{1,4,3,2,0:T(8,128)} async-done(((f32[2,256,64,2,16]{1,4,3,2,0:T(8,128)}), f32[2,256,64,2,16]{1,4,3,2,0:T(8,128)}, u32[]{:S(2)}, u32[]{:S(2)}) %all-to-all-start.3) | async-done | bytes 4194336 | tf_op jit(solution)/shard_map/all_to_all | solution.py:91
  304.3 7.4 copy.85
  311.7 6.6 reshape.518
  318.3 6.2 multiply_subtract_fusion.3
  324.5 11.3 fusion.74
  335.9 10.8 fusion.75
  350.3 5.8 all-to-all-start.4
  356.1 46.9 %all-to-all-done.4 = f32[2,256,64,2,16]{1,2,4,3,0:T(8,128)} async-done(((f32[2,256,64,2,16]{1,2,4,3,0:T(8,128)}), f32[2,256,64,2,16]{1,2,4,3,0:T(8,128)}, u32[]{:S(2)}, u32[]{:S(2)}) %all-to-all-start.4) | async-done | bytes 4194336 | tf_op jit(solution)/shard_map/all_to_all | solution.py:91
  403.0 6.5 fusion.89
  409.5 6.5 fusion.86
  419.1 18.3 %all-to-all-start.5 = ((f32[16,8,256,2,16]{2,1,4,3,0:T(8,128)}), f32[16,8,256,2,16]{2,1,4,3,0:T(8,128)}, u32[]{:S(2)}, u32[]{:S(2)}) async-start(f32[16,8,256,2,16]{2,1,4,3,0:T(8,128)} %pad_maximum_fusion.2), calls=%async_computation.5 | async-start | bytes 8388608 | tf_op jit(solution)/shard_map/all_to_all | solution.py:87
  439.7 75.5 %all-to-all-done.5 = f32[16,8,256,2,16]{2,1,4,3,0:T(8,128)} async-done(((f32[16,8,256,2,16]{2,1,4,3,0:T(8,128)}), f32[16,8,256,2,16]{2,1,4,3,0:T(8,128)}, u32[]{:S(2)}, u32[]{:S(2)}) %all-to-all-start.5) | async-done | bytes 4194336 | tf_op jit(solution)/shard_map/all_to_all | solution.py:87
  515.1 9.8 fusion.50
  525.0 7.3 fusion.128
  533.0 111.7 %all_to_all.90 = f32[16,8,256,2,16]{2,4,1,3,0:T(8,128)S(1)} all-to-all(f32[16,8,256,2,16]{2,4,1,3,0:T(8,128)S(1)} %copy.89), channel_id=1, replica_groups=mesh['gz'=16,'gy'=2] {'gz'}, dimensions={0} | all-to-all | bytes 8388608 | tf_op jit(solution)/shard_map/all_to_all | solution.py:87
  644.7 6.4 fusion.95
  651.2 6.5 fusion.92
  661.3 5.6 all-to-all-start.7
  677.1 12.0 multiply_add_fusion.4
  689.2 26.4 %all-to-all-done.7 = f32[2,256,64,2,16]{1,2,4,3,0:T(8,128)} async-done(((f32[2,256,64,2,16]{1,2,4,3,0:T(8,128)}), f32[2,256,64,2,16]{1,2,4,3,0:T(8,128)}, u32[]{:S(2)}, u32[]{:S(2)}) %all-to-all-start.7) | async-done | bytes 4194336 | tf_op jit(solution)/shard_map/all_to_all | solution.py:91
  718.3 10.9 fusion.172
  729.2 11.1 fusion.182
  742.3 7.6 fusion.72
  749.9 7.6 fusion.73
  761.1 5.6 all-to-all-start.8
  773.7 40.8 %all-to-all-done.8 = f32[2,256,64,2,16]{1,2,4,3,0:T(8,128)} async-done(((f32[2,256,64,2,16]{1,2,4,3,0:T(8,128)}), f32[2,256,64,2,16]{1,2,4,3,0:T(8,128)}, u32[]{:S(2)}, u32[]{:S(2)}) %all-to-all-start.8) | async-done | bytes 4194336 | tf_op jit(solution)/shard_map/all_to_all | solution.py:91
  836.0 7.9 fusion.156
  843.9 67.4 %all-to-all-done.9 = f32[16,8,256,2,16]{2,1,4,3,0:T(8,128)} async-done(((f32[16,8,256,2,16]{2,1,4,3,0:T(8,128)}), f32[16,8,256,2,16]{2,1,4,3,0:T(8,128)}, u32[]{:S(2)}, u32[]{:S(2)}) %all-to-all-start.9) | async-done | bytes 4194336 | tf_op jit(solution)/shard_map/all_to_all | solution.py:87
  911.3 10.3 bitcast_multiply_fusion.1
  923.6 7.1 fusion.137
  931.5 111.7 %all_to_all.91 = f32[16,8,256,2,16]{2,4,1,3,0:T(8,128)S(1)} all-to-all(f32[16,8,256,2,16]{2,4,1,3,0:T(8,128)S(1)} %copy.103), channel_id=1, replica_groups=mesh['gz'=16,'gy'=2] {'gz'}, dimensions={0} | all-to-all | bytes 8388608 | tf_op jit(solution)/shard_map/all_to_all | solution.py:87
  1043.2 6.4 fusion.107
  1049.6 6.8 fusion.104
  1058.0 51.2 %all_to_all.92 = f32[2,256,64,2,16]{1,2,4,3,0:T(8,128)S(1)} all-to-all(f32[2,256,64,2,16]{1,2,4,3,0:T(8,128)S(1)} %pad_maximum_fusion.6), channel_id=1, replica_groups=mesh['gz'=16,'gy'=2] {'gy'}, dimensions={0} | all-to-all | bytes 8388608 | tf_op jit(solution)/shard_map/all_to_all | solution.py:91
  1109.8 10.9 fusion.170
  1120.7 10.9 fusion.176
  1133.6 11.2 fusion.70
  1144.8 11.2 fusion.71
  1157.1 50.6 %all_to_all.93 = f32[2,256,64,2,16]{1,2,4,3,0:T(8,128)S(1)} all-to-all(f32[2,256,64,2,16]{1,2,4,3,0:T(8,128)S(1)} %pad_maximum_fusion.7), channel_id=1, replica_groups=mesh['gz'=16,'gy'=2] {'gy'}, dimensions={0} | all-to-all | bytes 8388608 | tf_op jit(solution)/shard_map/all_to_all | solution.py:91
  1217.6 96.6 %all_to_all.94 = f32[16,8,256,2,16]{2,1,4,3,0:T(8,128)S(1)} all-to-all(f32[16,8,256,2,16]{2,1,4,3,0:T(8,128)S(1)} %pad_maximum_fusion.8), channel_id=1, replica_groups=mesh['gz'=16,'gy'=2] {'gz'}, dimensions={0} | all-to-all | bytes 8388608 | tf_op jit(solution)/shard_map/all_to_all | solution.py:87
  1314.2 7.8 fusion.46
  1322.0 7.5 fusion.131
  1330.2 97.4 %all_to_all.95 = f32[16,8,256,2,16]{2,4,1,3,0:T(8,128)S(1)} all-to-all(f32[16,8,256,2,16]{2,4,1,3,0:T(8,128)S(1)} %copy.113), channel_id=1, replica_groups=mesh['gz'=16,'gy'=2] {'gz'}, dimensions={0} | all-to-all | bytes 8388608 | tf_op jit(solution)/shard_map/all_to_all | solution.py:87
  1427.6 6.4 fusion.119
  1434.0 6.8 fusion.116
  1441.8 51.2 %all_to_all.96 = f32[2,256,64,2,16]{1,2,4,3,0:T(8,128)S(1)} all-to-all(f32[2,256,64,2,16]{1,2,4,3,0:T(8,128)S(1)} %pad_maximum_fusion.9), channel_id=1, replica_groups=mesh['gz'=16,'gy'=2] {'gy'}, dimensions={0} | all-to-all | bytes 8388608 | tf_op jit(solution)/shard_map/all_to_all | solution.py:91
  1493.6 10.9 fusion.168
  1504.5 10.9 fusion.178
  1517.4 7.6 fusion.68
  1525.0 7.8 fusion.69
  1534.2 50.5 %all_to_all.97 = f32[2,256,64,2,16]{1,2,4,3,0:T(8,128)S(1)} all-to-all(f32[2,256,64,2,16]{1,2,4,3,0:T(8,128)S(1)} %pad_maximum_fusion.10), channel_id=1, replica_groups=mesh['gz'=16,'gy'=2] {'gy'}, dimensions={0} | all-to-all | bytes 8388608 | tf_op jit(solution)/shard_map/all_to_all | solution.py:91
  1594.1 96.9 %all_to_all.98 = f32[16,8,256,2,16]{2,1,4,3,0:T(8,128)S(1)} all-to-all(f32[16,8,256,2,16]{2,1,4,3,0:T(8,128)S(1)} %pad_maximum_fusion.11), channel_id=1, replica_groups=mesh['gz'=16,'gy'=2] {'gz'}, dimensions={0} | all-to-all | bytes 8388608 | tf_op jit(solution)/shard_map/all_to_all | solution.py:87
  1691.0 9.4 bitcast_multiply_fusion
  (113 shorter events, 122.6 us)
Async XLA Ops:
  13.6 85.1 %all-to-all-start = ((f32[16,8,256,2,16]{2,4,1,3,0:T(8,128)}), f32[16,8,256,2,16]{2,4,1,3,0:T(8,128)}, u32[]{:S(2)}, u32[]{:S(2)}) async-start(f32[16,8,256,2,16]{2,4,1,3,0:T(8,128)} %copy.74), calls=%async_computation | async-start | bytes 8388608 | tf_op jit(solution)/shard_map/all_to_all | solution.py:87
  98.7 97.6 %all-to-all-start.2 = ((f32[16,8,256,2,16]{2,4,1,3,0:T(8,128)}), f32[16,8,256,2,16]{2,4,1,3,0:T(8,128)}, u32[]{:S(2)}, u32[]{:S(2)}) async-start(f32[16,8,256,2,16]{2,4,1,3,0:T(8,128)} %copy.83), calls=%async_computation.2 | async-start | bytes 8388608 | tf_op jit(solution)/shard_map/all_to_all | solution.py:87
  196.3 54.2 %all-to-all-start.1 = ((f32[2,256,64,2,16]{1,2,4,3,0:T(8,128)}), f32[2,256,64,2,16]{1,2,4,3,0:T(8,128)}, u32[]{:S(2)}, u32[]{:S(2)}) async-start(f32[2,256,64,2,16]{1,2,4,3,0:T(8,128)} %pad_maximum_fusion), calls=%async_computation.1 | async-start | bytes 8388608 | tf_op jit(solution)/shard_map/all_to_all | solution.py:91
  250.5 53.8 %all-to-all-start.3 = ((f32[2,256,64,2,16]{1,4,3,2,0:T(8,128)}), f32[2,256,64,2,16]{1,4,3,2,0:T(8,128)}, u32[]{:S(2)}, u32[]{:S(2)}) async-start(f32[2,256,64,2,16]{1,4,3,2,0:T(8,128)} %bitcast.367), calls=%async_computation.3 | async-start | bytes 8388608 | tf_op jit(solution)/shard_map/all_to_all | solution.py:91
  256.6 79.3 %copy-start.20 = (s32[2,256]{1,0:T(2,128)}, s32[2,256]{1,0:T(2,128)S(1)}, u32[]{:S(2)}) copy-start(s32[2,256]{1,0:T(2,128)S(1)} %multiply_add_fusion.10) | copy-start | bytes 6148
  350.3 52.7 %all-to-all-start.4 = ((f32[2,256,64,2,16]{1,2,4,3,0:T(8,128)}), f32[2,256,64,2,16]{1,2,4,3,0:T(8,128)}, u32[]{:S(2)}, u32[]{:S(2)}) async-start(f32[2,256,64,2,16]{1,2,4,3,0:T(8,128)} %pad_maximum_fusion.1), calls=%async_computation.4 | async-start | bytes 8388608 | tf_op jit(solution)/shard_map/all_to_all | solution.py:91
  356.1 53.3 %copy-start.14 = (s32[16,8]{1,0:T(8,128)}, s32[16,8]{1,0:T(8,128)S(1)}, u32[]{:S(2)}) copy-start(s32[16,8]{1,0:T(8,128)S(1)} %multiply_add_fusion.8) | copy-start | bytes 1540
  419.1 96.0 %all-to-all-start.5 = ((f32[16,8,256,2,16]{2,1,4,3,0:T(8,128)}), f32[16,8,256,2,16]{2,1,4,3,0:T(8,128)}, u32[]{:S(2)}, u32[]{:S(2)}) async-start(f32[16,8,256,2,16]{2,1,4,3,0:T(8,128)} %pad_maximum_fusion.2), calls=%async_computation.5 | async-start | bytes 8388608 | tf_op jit(solution)/shard_map/all_to_all | solution.py:87
  439.7 85.3 %copy-start.16 = (f32[1,16,16,512]{3,2,1,0:T(8,128)}, f32[1,16,16,512]{3,2,1,0:T(8,128)S(1)}, u32[]{:S(2)}) copy-start(f32[1,16,16,512]{3,2,1,0:T(8,128)S(1)} %get-tuple-element.37) | copy-start | bytes 1572868
  439.7 85.3 %copy-start.18 = (f32[1,16,16,512]{3,2,1,0:T(8,128)}, f32[1,16,16,512]{3,2,1,0:T(8,128)S(1)}, u32[]{:S(2)}) copy-start(f32[1,16,16,512]{3,2,1,0:T(8,128)S(1)} %get-tuple-element.38) | copy-start | bytes 1572868
  515.1 9.9 copy-start.6
  661.3 54.2 %all-to-all-start.7 = ((f32[2,256,64,2,16]{1,2,4,3,0:T(8,128)}), f32[2,256,64,2,16]{1,2,4,3,0:T(8,128)}, u32[]{:S(2)}, u32[]{:S(2)}) async-start(f32[2,256,64,2,16]{1,2,4,3,0:T(8,128)} %pad_maximum_fusion.3), calls=%async_computation.7 | async-start | bytes 8388608 | tf_op jit(solution)/shard_map/all_to_all | solution.py:91
  689.1 53.2 %copy-start.4 = (f32[512,512]{0,1:T(8,128)}, f32[512,512]{0,1:T(8,128)S(1)}, u32[]{:S(2)}) copy-start(f32[512,512]{0,1:T(8,128)S(1)} %get-tuple-element.52) | copy-start | bytes 3145732
  689.2 60.7 %copy-start.2 = (f32[512,512]{0,1:T(8,128)}, f32[512,512]{0,1:T(8,128)S(1)}, u32[]{:S(2)}) copy-start(f32[512,512]{0,1:T(8,128)S(1)} %get-tuple-element.53) | copy-start | bytes 3145732
  729.2 11.2 copy-start
  761.1 53.4 %all-to-all-start.8 = ((f32[2,256,64,2,16]{1,2,4,3,0:T(8,128)}), f32[2,256,64,2,16]{1,2,4,3,0:T(8,128)}, u32[]{:S(2)}, u32[]{:S(2)}) async-start(f32[2,256,64,2,16]{1,2,4,3,0:T(8,128)} %pad_maximum_fusion.4), calls=%async_computation.8 | async-start | bytes 8388608 | tf_op jit(solution)/shard_map/all_to_all | solution.py:91
  773.5 46.5 %copy-start.10 = (f32[2,64,16,8]{1,0,3,2:T(2,128)}, f32[2,64,16,8]{1,0,3,2:T(2,128)S(1)}, u32[]{:S(2)}) copy-start(f32[2,64,16,8]{1,0,3,2:T(2,128)S(1)} %reshape.522) | copy-start | bytes 196612
  773.7 46.3 %copy-start.12 = (f32[2,64,16,8]{1,0,3,2:T(2,128)}, f32[2,64,16,8]{1,0,3,2:T(2,128)S(1)}, u32[]{:S(2)}) copy-start(f32[2,64,16,8]{1,0,3,2:T(2,128)S(1)} %reshape.513) | copy-start | bytes 196612
  828.8 82.5 %all-to-all-start.9 = ((f32[16,8,256,2,16]{2,1,4,3,0:T(8,128)}), f32[16,8,256,2,16]{2,1,4,3,0:T(8,128)}, u32[]{:S(2)}, u32[]{:S(2)}) async-start(f32[16,8,256,2,16]{2,1,4,3,0:T(8,128)} %pad_maximum_fusion.5), calls=%async_computation.9 | async-start | bytes 8388608 | tf_op jit(solution)/shard_map/all_to_all | solution.py:87
  921.6 2.0 copy-start.8
  1120.7 10.9 copy-start.1
  1131.6 1.9 copy-start.21
  1157.0 50.6 %copy-start.15 = (s32[16,8]{1,0:T(8,128)S(1)}, s32[16,8]{1,0:T(8,128)}, u32[]{:S(2)}) copy-start(s32[16,8]{1,0:T(8,128)} %copy-done.14) | copy-start | bytes 1540
  1217.5 96.6 %copy-start.17 = (f32[1,16,16,512]{3,2,1,0:T(8,128)S(1)}, f32[1,16,16,512]{3,2,1,0:T(8,128)}, u32[]{:S(2)}) copy-start(f32[1,16,16,512]{3,2,1,0:T(8,128)} %copy-done.16) | copy-start | bytes 1572868
  1217.5 96.6 %copy-start.19 = (f32[1,16,16,512]{3,2,1,0:T(8,128)S(1)}, f32[1,16,16,512]{3,2,1,0:T(8,128)}, u32[]{:S(2)}) copy-start(f32[1,16,16,512]{3,2,1,0:T(8,128)} %copy-done.18) | copy-start | bytes 1572868
  1314.2 7.9 copy-start.7
  1515.5 2.0 copy-start.5
  1517.4 7.6 copy-start.3
  1534.2 50.5 %copy-start.11 = (f32[2,64,16,8]{1,0,3,2:T(2,128)S(1)}, f32[2,64,16,8]{1,0,3,2:T(2,128)}, u32[]{:S(2)}) copy-start(f32[2,64,16,8]{1,0,3,2:T(2,128)} %copy-done.10) | copy-start | bytes 196612
  1584.7 4.1 copy-start.13
  1594.1 96.9 %copy-start.9 = (f32[8,256,512]{2,1,0:T(8,128)S(1)}, f32[8,256,512]{2,1,0:T(8,128)}, u32[]{:S(2)}) copy-start(f32[8,256,512]{2,1,0:T(8,128)} %copy-done.8) | copy-start | bytes 12582916
where the time goes:
time: 1710 us; the launch traced here: 1700 us
  blocking collectives  718 us (42%)
  waiting for transfers between devices  448 us (26%)
  matrix products  329 us (19%)
  other arithmetic  83.4 us (5%)
  starting transfers between devices  79.3 us (5%)
  local copies, waits for them, and re-layouts  40.6 us (2%)
    all_to_all x5, blocking collectives, across_z(): return lax.all_to_all(values, 'gz', split_axis=0, concat_axis=0, tiled=True)  514 us
    dot_general x40, matrix products, product(): jnp.einsum(form, left, right, precision=lax.Precision.HIGHEST, preferred_...  329 us
    all_to_all x4, waiting for transfers between devices, across_z(): return lax.all_to_all(values, 'gz', split_axis=0, concat_axis=0, tiled=True)  269 us
    all_to_all x4, blocking collectives, across_y(): return lax.all_to_all(values, 'gy', split_axis=0, concat_axis=0, tiled=True)  204 us
    all_to_all x5, waiting for transfers between devices, across_y(): return lax.all_to_all(values, 'gy', split_axis=0, concat_axis=0, tiled=True)  179 us
    all_to_all x4, starting transfers between devices, across_z(): return lax.all_to_all(values, 'gz', split_axis=0, concat_axis=0, tiled=True)  50.6 us
  transfers between devices with their start and end apart: 9, of which 9 were waited for; matrix products, arithmetic and copies ran while one was open for 6% of the time, Pallas kernels for 0%

commit v1 on v0

--- a/solution.py
+++ b/solution.py
@@ -1,8 +1,12 @@
+import functools
 import math
 
 import jax
 import jax.numpy as jnp
+import numpy as np
 from jax import lax
+from jax.experimental import pallas as pl
+from jax.experimental.pallas import tpu as pltpu
 from jax.sharding import PartitionSpec as P
 
 ITERS = 2
@@ -160,7 +164,7 @@
     )
 
 
-def on_device(measured, transfer_real, transfer_imag):
+def on_device_rows(measured, transfer_real, transfer_imag):
     z_local, y_local, x_len = measured.shape
     z_len = z_local * lax.axis_size("gz")
     y_len = y_local * lax.axis_size("gy")
@@ -186,11 +190,382 @@
     return estimate
 
 
+LANES = 128
+SUBLANES = 8
+
+
+def gauss_weights_np():
+    offsets = np.arange(-RADIUS, RADIUS + 1).astype(np.float64)
+    weights = np.exp(-offsets * offsets / (2.0 * SIGMA * SIGMA))
+    return weights / weights.sum()
+
+
+def smooth_np(table, axis):
+    weights = gauss_weights_np()
+    widths = [(0, 0)] * table.ndim
+    widths[axis] = (RADIUS, RADIUS)
+    padded = np.pad(table, widths)
+    length = table.shape[axis]
+    return sum(
+        weights[j] * np.take(padded, np.arange(j, j + length), axis=axis)
+        for j in range(2 * RADIUS + 1)
+    )
+
+
+def two_terms(table):
+    high = table.astype(np.float32).astype(jnp.bfloat16)
+    low = (table - high.astype(np.float64)).astype(np.float32).astype(jnp.bfloat16)
+    return np.stack((high, low))
+
+
+def phase_np(first, second, length):
+    return 2.0 * np.pi * ((first[:, None] * second[None, :]) % length) / length
+
+
+def x_tables(length):
+    half = length // 2
+    where = np.arange(length)
+    ahead, behind = [], []
+    for odd in range(2):
+        k = 2 * np.arange(half // 2) + odd
+        angle = phase_np(where, k, length)
+        ahead.append(np.concatenate((np.cos(angle), -np.sin(angle)), axis=1)[:half])
+        weight = (np.where(k == 0, 1.0, 2.0) / length)[:, None]
+        behind.append(np.concatenate((weight * np.cos(angle).T, -weight * np.sin(angle).T), axis=0))
+    sharp = np.stack([table[:, :half] for table in behind])
+    soft = smooth_np(np.concatenate(behind, axis=0), 1)
+    return two_terms(np.stack(ahead)), two_terms(sharp), two_terms(soft)
+
+
+def y_tables(length):
+    half = length // 2
+    where = np.arange(length)
+    ahead, sharp, soft = [], [], []
+    for odd in range(2):
+        k = 2 * np.arange(half) + odd
+        angle = phase_np(k, where, length)
+        cosine, sine = np.cos(angle), np.sin(angle)
+        ahead.append(np.concatenate((cosine[:, :half], sine[:, :half]), axis=0))
+        cosine, sine = cosine.T / length, sine.T / length
+        sharp.append(np.concatenate((cosine[:half], sine[:half]), axis=0))
+        soft.append(np.concatenate((smooth_np(cosine, 0), smooth_np(sine, 0)), axis=0))
+    return two_terms(np.stack(ahead)), two_terms(np.stack(sharp)), two_terms(np.stack(soft))
+
+
+def z_tables(length):
+    where = np.arange(length)
+    angle = phase_np(where, where, length)
+    cosine, sine = np.cos(angle), np.sin(angle)
+    ahead = np.block([[cosine, sine], [-sine, cosine]])
+    cosine, sine = cosine / length, sine / length
+    sharp = np.block([[cosine, -sine], [sine, cosine]])
+    cosine, sine = smooth_np(cosine, 0), smooth_np(sine, 0)
+    soft = np.block([[cosine, -sine], [sine, cosine]])
+    return two_terms(ahead), two_terms(sharp), two_terms(soft)
+
+
+def dot(left, right):
+    return jnp.dot(left, right, preferred_element_type=jnp.float32)
+
+
+def split_terms(values):
+    high = values.astype(jnp.bfloat16)
+    return high, (values - high.astype(jnp.float32)).astype(jnp.bfloat16)
+
+
+def table_times(high, low, values):
+    first, second = split_terms(values)
+    return dot(high, first) + dot(high, second) + dot(low, first)
+
+
+def times_table(values, high, low):
+    first, second = split_terms(values)
+    return dot(first, high) + dot(second, high) + dot(first, low)
+
+
+def quarters(values):
+    return [values[:, LANES * i : LANES * (i + 1)] for i in range(4)]
+
+
+def load_spectrum(got_ref, odd):
+    y_devs = got_ref.shape[1]
+    rows = got_ref.shape[4] // 2
+    part = []
+    for lane in range(4):
+        pieces = [
+            got_ref[:, g, 0, lane, odd * rows : (odd + 1) * rows, :].reshape(-1, LANES)
+            for g in range(y_devs)
+        ]
+        part.append(jnp.concatenate(pieces, axis=0))
+    return jnp.concatenate(part, axis=1)
+
+
+def store_spectrum(send_ref, odd, parts):
+    z_devs, y_devs = send_ref.shape[0], send_ref.shape[1]
+    rows = send_ref.shape[4] // 2
+    for lane in range(4):
+        for g in range(y_devs):
+            piece = parts[lane][g * z_devs * rows : (g + 1) * z_devs * rows]
+            send_ref[:, g, 0, lane, odd * rows : (odd + 1) * rows, :] = piece.reshape(
+                z_devs, rows, LANES
+            )
+
+
+def turned_back(both):
+    rows = both.shape[0] // 2
+    cosine, sine = quarters(both[:rows]), quarters(both[rows:])
+    return [
+        cosine[0] - sine[1],
+        cosine[1] + sine[0],
+        cosine[2] - sine[3],
+        cosine[3] + sine[2],
+    ]
+
+
+def turned_ahead(both):
+    rows = both.shape[0] // 2
+    cosine, sine = quarters(both[:rows]), quarters(both[rows:])
+    return [
+        cosine[0] + sine[1],
+        cosine[1] - sine[0],
+        cosine[2] + sine[3],
+        cosine[3] - sine[2],
+    ]
+
+
+def plane_back_sharp(got_ref, y_ref, x_ref):
+    even = turned_back(table_times(y_ref[0, 0], y_ref[1, 0], load_spectrum(got_ref, 0)))
+    odd = turned_back(table_times(y_ref[0, 1], y_ref[1, 1], load_spectrum(got_ref, 1)))
+    upper = [a + b for a, b in zip(even, odd)]
+    lower = [a - b for a, b in zip(even, odd)]
+    spans = []
+    for parity in range(2):
+        values = jnp.concatenate(
+            (
+                jnp.concatenate(upper[2 * parity : 2 * parity + 2], axis=1),
+                jnp.concatenate(lower[2 * parity : 2 * parity + 2], axis=1),
+            ),
+            axis=0,
+        )
+        spans.append(times_table(values, x_ref[0, parity], x_ref[1, parity]))
+    return spans[0] + spans[1], spans[0] - spans[1]
+
+
+def plane_back_soft(got_ref, y_ref, x_ref):
+    both = table_times(y_ref[0, 0], y_ref[1, 0], load_spectrum(got_ref, 0)) + table_times(
+        y_ref[0, 1], y_ref[1, 1], load_spectrum(got_ref, 1)
+    )
+    values = jnp.concatenate(turned_back(both), axis=1)
+    plane = times_table(values, x_ref[0], x_ref[1])
+    half = plane.shape[1] // 2
+    return plane[:, :half], plane[:, half:]
+
+
+def plane_ahead(left, right, send_ref, y_ref, x_ref):
+    even = times_table(left + right, x_ref[0, 0], x_ref[1, 0])
+    odd = times_table(left - right, x_ref[0, 1], x_ref[1, 1])
+    values = jnp.concatenate((even, odd), axis=1)
+    half = values.shape[0] // 2
+    upper, lower = values[:half], values[half:]
+    for parity, part in enumerate((upper + lower, upper - lower)):
+        both = table_times(y_ref[0, parity], y_ref[1, parity], part)
+        store_spectrum(send_ref, parity, turned_ahead(both))
+
+
+def first_kernel(volume_ref, ya_ref, xa_ref, send_ref):
+    half = volume_ref.shape[2] // 2
+    plane_ahead(volume_ref[0, :, :half], volume_ref[0, :, half:], send_ref, ya_ref, xa_ref)
+
+
+def ratio_kernel(got_ref, measured_ref, yb_ref, xb_ref, ya_ref, xa_ref, send_ref):
+    half = measured_ref.shape[2] // 2
+    left, right = plane_back_sharp(got_ref, yb_ref, xb_ref)
+    left = measured_ref[0, :, :half] / jnp.maximum(left, FLOOR)
+    right = measured_ref[0, :, half:] / jnp.maximum(right, FLOOR)
+    plane_ahead(left, right, send_ref, ya_ref, xa_ref)
+
+
+def correct_kernel(got_ref, estimate_ref, yb_ref, xb_ref, ya_ref, xa_ref, send_ref, out_ref):
+    half = estimate_ref.shape[2] // 2
+    left, right = plane_back_soft(got_ref, yb_ref, xb_ref)
+    left = estimate_ref[0, :, :half] * left
+    right = estimate_ref[0, :, half:] * right
+    out_ref[0, :, :half] = left
+    out_ref[0, :, half:] = right
+    plane_ahead(left, right, send_ref, ya_ref, xa_ref)
+
+
+def last_kernel(got_ref, estimate_ref, yb_ref, xb_ref, out_ref):
+    half = estimate_ref.shape[2] // 2
+    left, right = plane_back_soft(got_ref, yb_ref, xb_ref)
+    out_ref[0, :, :half] = estimate_ref[0, :, :half] * left
+    out_ref[0, :, half:] = estimate_ref[0, :, half:] * right
+
+
+def gain_kernel(conjugate, got_ref, gain_ref, za_ref, zb_ref, send_ref):
+    z_len, _, rows, _ = got_ref.shape
+    flat = got_ref.reshape(z_len * 2 * rows, LANES)
+    sent = send_ref.reshape(z_len * 2 * rows, LANES)
+
+    def column(part):
+        pieces = [flat[pl.ds(part * rows + i, z_len, 2 * rows), :] for i in range(rows)]
+        return jnp.concatenate(pieces, axis=1)
+
+    values = jnp.concatenate((column(0), column(1)), axis=0)
+    spectrum = table_times(za_ref[0], za_ref[1], values)
+    real, imag = spectrum[:z_len], spectrum[z_len:]
+    gain_real, gain_imag = gain_ref[0, 0], gain_ref[0, 1]
+    if conjugate:
+        turned = (real * gain_real + imag * gain_imag, imag * gain_real - real * gain_imag)
+    else:
+        turned = (real * gain_real - imag * gain_imag, real * gain_imag + imag * gain_real)
+    values = table_times(zb_ref[0], zb_ref[1], jnp.concatenate(turned, axis=0))
+    for part in range(2):
+        for i in range(rows):
+            sent[pl.ds(part * rows + i, z_len, 2 * rows), :] = values[
+                part * z_len : (part + 1) * z_len, i * LANES : (i + 1) * LANES
+            ]
+
+
+VMEM_BYTES = 58 * 2**20
+
+
+def whole(table):
+    return pl.BlockSpec(table.shape, lambda *_: (0,) * table.ndim)
+
+
+def call(kernel, grid, arrays, specs, tables, outs, out_specs, flops, name):
+    moved = sum(math.prod(a.shape) * a.dtype.itemsize for a in (*arrays, *tables, *jax.tree.leaves(outs)))
+    return pl.pallas_call(
+        kernel,
+        grid=grid,
+        in_specs=list(specs) + [whole(t) for t in tables],
+        out_specs=out_specs,
+        out_shape=outs,
+        compiler_params=pltpu.CompilerParams(vmem_limit_bytes=VMEM_BYTES),
+        cost_estimate=pl.CostEstimate(flops=flops, bytes_accessed=moved, transcendentals=0),
+        name=name,
+    )(*arrays, *tables)
+
+
+def exchange(values):
+    z_devs, y_devs = values.shape[:2]
+    flat = values.reshape(z_devs * y_devs, *values.shape[2:])
+    flat = lax.all_to_all(flat, ("gz", "gy"), split_axis=0, concat_axis=0, tiled=True)
+    return flat.reshape(values.shape)
+
+
+def to_planes(volume):
+    return lax.all_to_all(volume, "gy", split_axis=0, concat_axis=1, tiled=True)
+
+
+def from_planes(volume):
+    return lax.all_to_all(volume, "gy", split_axis=1, concat_axis=0, tiled=True)
+
+
+def gains_planes(transfer_real, transfer_imag):
+    half = transfer_real.shape[2]
+    both = jnp.stack((transfer_real, transfer_imag))
+    both = lax.all_to_all(both, "gz", split_axis=2, concat_axis=1, tiled=True)
+    _, z_len, rows, _ = both.shape
+    both = both.reshape(2, z_len, rows // 2, 2, half // 2, 2).transpose(3, 5, 0, 1, 2, 4)
+    return both.reshape(4, 2, z_len, rows // 2 * (half // 2))
+
+
+def on_device_planes(measured, transfer_real, transfer_imag):
+    z_devs, y_devs = lax.axis_size("gz"), lax.axis_size("gy")
+    devs = z_devs * y_devs
+    z_local, y_local, x_len = measured.shape
+    z_len, y_len = z_local * z_devs, y_local * y_devs
+    planes, rows = z_len // devs, y_len // devs
+    xa, xb, xs = (jnp.asarray(t) for t in x_tables(x_len))
+    ya, yb, ys = (jnp.asarray(t) for t in y_tables(y_len))
+    za, zb, zs = (jnp.asarray(t) for t in z_tables(z_len))
+
+    spectrum = jax.ShapeDtypeStruct((z_devs, y_devs, planes, 4, rows, LANES), jnp.float32)
+    volume = jax.ShapeDtypeStruct((planes, y_len, x_len), jnp.float32)
+    spectrum_spec = pl.BlockSpec(
+        (z_devs, y_devs, 1, 4, rows, LANES), lambda p: (0, 0, p, 0, 0, 0)
+    )
+    volume_spec = pl.BlockSpec((1, y_len, x_len), lambda p: (p, 0, 0))
+    ahead_flops = 3 * planes * y_len * x_len * (x_len + 2 * y_len)
+    sharp_flops = ahead_flops
+    soft_flops = 2 * ahead_flops
+
+    def first(values):
+        return call(
+            first_kernel, (planes,), (values,), (volume_spec,), (ya, xa),
+            spectrum, spectrum_spec, ahead_flops, "first",
+        )
+
+    def ratio(got, values):
+        return call(
+            ratio_kernel, (planes,), (got, values), (spectrum_spec, volume_spec), (yb, xb, ya, xa),
+            spectrum, spectrum_spec, ahead_flops + sharp_flops, "ratio",
+        )
+
+    def correct(got, values):
+        return call(
+            correct_kernel, (planes,), (got, values), (spectrum_spec, volume_spec),
+            (ys, xs, ya, xa), (spectrum, volume), (spectrum_spec, volume_spec),
+            ahead_flops + soft_flops, "correct",
+        )
+
+    def last(got, values):
+        return call(
+            last_kernel, (planes,), (got, values), (spectrum_spec, volume_spec), (ys, xs),
+            volume, volume_spec, soft_flops, "last",
+        )
+
+    columns = jax.ShapeDtypeStruct((z_len, 4, rows, LANES), jnp.float32)
+    columns_spec = pl.BlockSpec((z_len, 2, rows // 2, LANES), lambda s: (0, s % 2, s // 2, 0))
+
+    def filtered(got, gains, conjugate):
+        gains_spec = pl.BlockSpec((1, *gains.shape[1:]), lambda s: (s, 0, 0, 0))
+        return call(
+            functools.partial(gain_kernel, conjugate), (4,),
+            (got.reshape(columns.shape), gains), (columns_spec, gains_spec),
+            (za, zs if conjugate else zb), columns, columns_spec,
+            3 * 2 * 2 * 4 * z_len * z_len * rows * x_len, "adjoint" if conjugate else "blur",
+        ).reshape(spectrum.shape)
+
+    measured = to_planes(measured)
+    gains = gains_planes(transfer_real, transfer_imag)
+    estimate = measured
+    send = first(measured)
+    for iteration in range(ITERS):
+        send = filtered(exchange(send), gains, False)
+        send = ratio(exchange(send), measured)
+        send = filtered(exchange(send), gains, True)
+        got = exchange(send)
+        if iteration < ITERS - 1:
+            send, estimate = correct(got, estimate)
+        else:
+            estimate = last(got, estimate)
+    return from_planes(estimate)
+
+
+def planes_fit(mesh, shape):
+    devs = mesh.shape["gz"] * mesh.shape["gy"]
+    z_len, y_len, x_len = shape
+    return (
+        z_len % devs == 0
+        and z_len % LANES == 0
+        and y_len % (2 * SUBLANES * devs) == 0
+        and x_len == 4 * LANES
+    )
+
+
 def solution(mesh):
-    return jax.shard_map(
-        on_device,
-        mesh=mesh,
-        in_specs=(P("gz", "gy", None), P("gz", "gy", None), P("gz", "gy", None)),
-        out_specs=P("gz", "gy", None),
-        check_vma=False,
-    )
+    def run(measured, transfer_real, transfer_imag):
+        spec = P("gz", "gy", None)
+        fits = planes_fit(mesh, measured.shape)
+        return jax.shard_map(
+            on_device_planes if fits else on_device_rows,
+            mesh=mesh,
+            in_specs=(spec, spec, spec),
+            out_specs=spec,
+            check_vma=False,
+        )(measured, transfer_real, transfer_imag)
+
+    return run

time: 1710 us -> 1110 us (0.65)
  waiting for transfers between devices: 448 us -> 107 us
  matrix products: 329 us -> 0 us
  Pallas kernels: 0 us -> 114 us
  other arithmetic: 83.4 us -> 2.27 us
  local copies, waits for them, and re-layouts: 40.6 us -> 115 us
  starting transfers between devices: 79.3 us -> 30.7 us
    all_to_all x9 -> x3, waiting for transfers between devices: 448 us -> 107 us  [the longest x1 64 us: gains_planes(): both = lax.all_to_all(both, 'gz', split_axis=2, concat_axis=1, tiled=True)]
    dot_general x40 -> x0, matrix products: 329 us -> none  [product(): jnp.einsum(form, left, right, precision=lax.Precision.HIGHEST, preferred_...]
    pallas_call x0 -> x9, Pallas kernels: none -> 114 us  [call(): pl.pallas_call(kernel, grid=grid, in_specs=list(specs) + [whole(t) for t...]
    all_to_all x9 -> x3, starting transfers between devices: 79.3 us -> 30.7 us  [the longest x1 18.8 us: exchange(): lax.all_to_all(flat, ('gz', 'gy'), split_axis=0, concat_axis=0, tiled=True)]
    reshape x7 -> x2, local copies, waits for them, and re-layouts: 13.4 us -> 52.9 us  [the longest x1 48 us: gains_planes(): both.reshape(2, z_len, rows // 2, 2, half // 2, 2)]
    all_to_all x2 -> x3, local copies, waits for them, and re-layouts: 12.3 us -> 48.4 us  [the longest x1 40.5 us: gains_planes(): both = lax.all_to_all(both, 'gz', split_axis=2, concat_axis=1, tiled=True)]
    add x9 -> x0, other arithmetic: 33.3 us -> none  [the longest x3 25.5 us: taps_along(): total + weights[offset] * lax.slice_in_dim(padded, offset, offset + lengt...]
    all_to_all x9 -> x8, blocking collectives: 718 us -> 735 us  [the longest x7 684 us: exchange(): lax.all_to_all(flat, ('gz', 'gy'), split_axis=0, concat_axis=0, tiled=True)]
  transfers between devices with their start and end apart: 9 -> 3, of which waited for: 9 -> 2; matrix products, arithmetic and copies ran while one was open for 6% -> 10% of each run, Pallas kernels for 0% -> 1%
where the time goes in v1:
time: 1110 us; the launch traced here: 1100 us
  blocking collectives  735 us (66%)
  local copies, waits for them, and re-layouts  115 us (10%)
  Pallas kernels  114 us (10%)
  waiting for transfers between devices  107 us (10%)
  starting transfers between devices  30.7 us (3%)
    all_to_all x7, blocking collectives, exchange(): lax.all_to_all(flat, ('gz', 'gy'), split_axis=0, concat_axis=0, tiled=True)  684 us
    pallas_call x9, Pallas kernels, call(): pl.pallas_call(kernel, grid=grid, in_specs=list(specs) + [whole(t) for t...  114 us
    all_to_all x1, waiting for transfers between devices, gains_planes(): both = lax.all_to_all(both, 'gz', split_axis=2, concat_axis=1, tiled=True)  64 us
    all_to_all x1, blocking collectives, from_planes(): return lax.all_to_all(volume, 'gy', split_axis=1, concat_axis=0, tiled=True)  50.5 us
    reshape x1, local copies, waits for them, and re-layouts, gains_planes(): both.reshape(2, z_len, rows // 2, 2, half // 2, 2)  48 us
    all_to_all x1, waiting for transfers between devices, to_planes(): return lax.all_to_all(volume, 'gy', split_axis=0, concat_axis=1, tiled=True)  42.6 us
    all_to_all x1, local copies, waits for them, and re-layouts, gains_planes(): both = lax.all_to_all(both, 'gz', split_axis=2, concat_axis=1, tiled=True)  40.5 us
  transfers between devices with their start and end apart: 3, of which 2 were waited for; matrix products, arithmetic and copies ran while one was open for 10% of the time, Pallas kernels for 1%

profile of v1, /device:TPU:0, one launch (start us, length us, event | category | flops | bytes accessed | tf_op | source)
XLA Modules:
  0.0 1103.7 jit_solution(14817907040013687501)
XLA Ops:
  0.0 0.0 copy-start
  0.0 5.7 all-to-all-start
  5.7 0.0 copy-done
  5.7 4.0 copy_bitcast_fusion
  9.8 2.3 pad_maximum_fusion
  12.0 42.6 %all-to-all-done = f32[8,256,512]{2,1,0:T(8,128)} async-done(((f32[8,256,512]{2,1,0:T(8,128)}), f32[8,256,512]{2,1,0:T(8,128)}, u32[]{:S(2)}, u32[]{:S(2)}) %all-to-all-start) | async-done | bytes 4194336 | tf_op jit(solution)/shard_map/all_to_all | solution.py:459
  54.6 6.2 all-to-all-start.2
  60.8 4.6 copy.19
  65.5 9.0 first.1
  74.5 64.0 %all-to-all-done.2 = f32[2,8,256,256]{3,1,0,2:T(8,128)} async-done(((f32[2,8,256,256]{3,1,0,2:T(8,128)}), f32[2,8,256,256]{3,1,0,2:T(8,128)}, u32[]{:S(2)}, u32[]{:S(2)}) %all-to-all-start.2) | async-done | bytes 4194336 | tf_op jit(solution)/shard_map/all_to_all | solution.py:469
  138.5 18.8 %all-to-all-start.1 = ((f32[32,4,4,16,128]{4,3,2,1,0:T(8,128)}), f32[32,4,4,16,128]{4,3,2,1,0:T(8,128)}, u32[]{:S(2)}, u32[]{:S(2)}) async-start(f32[32,4,4,16,128]{4,3,2,1,0:T(8,128)} %bitcast.43), calls=%async_computation.1 | async-start | bytes 8388608 | tf_op jit(solution)/shard_map/all_to_all | solution.py:454
  157.3 40.5 %copy.22 = f32[2,8,16,16,256]{1,2,4,3,0:T(8,128)} copy(f32[2,8,16,16,256]{4,1,0,3,2:T(8,128)} %bitcast.7) | data formatting | bytes 8388608 | tf_op jit(solution)/shard_map/all_to_all | solution.py:469
  197.8 48.0 %reshape.32 = f32[2,128,8,2,128,2]{1,5,4,3,2,0:T(2,128)} reshape(f32[2,16,8,16,256]{2,1,4,3,0:T(8,128)} %bitcast.8) | data formatting | bytes 8388608 | tf_op jit(solution)/shard_map/reshape | solution.py:471
  245.8 5.3 copy.23
  251.0 4.9 reshape.33.gain_ref
  255.9 0.0 all-to-all-done.1
  255.9 9.7 blur.2
  265.6 99.5 %all_to_all.91 = f32[32,4,4,16,128]{4,3,2,1,0:T(8,128)} all-to-all(f32[32,4,4,16,128]{4,3,2,1,0:T(8,128)} %bitcast.53), channel_id=1, replica_groups=mesh['gz'=16,'gy'=2] {'gz','gy'}, dimensions={0} | all-to-all | bytes 8388608 | tf_op jit(solution)/shard_map/all_to_all | solution.py:454
  365.1 15.7 %ratio.2 = f32[16,2,4,4,16,128]{5,4,3,2,1,0:T(8,128)} custom-call(f32[16,2,4,4,16,128]{5,4,3,2,1,0:T(8,128)} %bitcast.54, f32[4,512,512]{2,1,0:T(8,128)} %bitcast.40, bf16[2,2,512,256]{3,2,1,0:T(8,128)(2,1)} %constant.22.clone.yb_ref, bf16[2,2,256,256]{3,2,1,0:T(8,128)(2,1)} %constant.19.clone.xb_ref, bf16[2,2,512,256]{3,2,1,0:T(8,128)(2,1)} %constant.21.clone.ya_ref, ...), custom_call_target="tpu_custom_call" | custom-call | flops 9663676416 | bytes 15728640 | tf_op jit(solution)/shard_map/ratio/pallas_call | solution.py:439
  380.9 97.5 %all_to_all.92 = f32[32,4,4,16,128]{4,3,2,1,0:T(8,128)} all-to-all(f32[32,4,4,16,128]{4,3,2,1,0:T(8,128)} %bitcast.55), channel_id=1, replica_groups=mesh['gz'=16,'gy'=2] {'gz','gy'}, dimensions={0} | all-to-all | bytes 8388608 | tf_op jit(solution)/shard_map/all_to_all | solution.py:454
  478.3 9.6 adjoint.2
  488.0 97.5 %all_to_all.93 = f32[32,4,4,16,128]{4,3,2,1,0:T(8,128)} all-to-all(f32[32,4,4,16,128]{4,3,2,1,0:T(8,128)} %bitcast.57), channel_id=1, replica_groups=mesh['gz'=16,'gy'=2] {'gz','gy'}, dimensions={0} | all-to-all | bytes 8388608 | tf_op jit(solution)/shard_map/all_to_all | solution.py:454
  585.4 20.7 %correct.1 = (f32[16,2,4,4,16,128]{5,4,3,2,1,0:T(8,128)}, f32[4,512,512]{2,1,0:T(8,128)}) custom-call(f32[16,2,4,4,16,128]{5,4,3,2,1,0:T(8,128)} %bitcast.49, f32[4,512,512]{2,1,0:T(8,128)} %bitcast.41, bf16[2,2,1024,256]{3,2,1,0:T(8,128)(2,1)} %constant.23.clone.yb_ref, bf16[2,512,512]{2,1,0:T(8,128)(2,1)} %constant.20.clone.xb_ref, ...), custom_call_target="tpu_custom_call" | custom-call | flops 14495514624 | bytes 21495808 | tf_op jit(solution)/shard_map/correct/pallas_call | solution.py:439
  606.1 97.5 %all_to_all.94 = f32[32,4,4,16,128]{4,3,2,1,0:T(8,128)} all-to-all(f32[32,4,4,16,128]{4,3,2,1,0:T(8,128)} %bitcast.50), channel_id=1, replica_groups=mesh['gz'=16,'gy'=2] {'gz','gy'}, dimensions={0} | all-to-all | bytes 8388608 | tf_op jit(solution)/shard_map/all_to_all | solution.py:454
  703.6 9.6 blur.3
  713.2 97.5 %all_to_all.95 = f32[32,4,4,16,128]{4,3,2,1,0:T(8,128)} all-to-all(f32[32,4,4,16,128]{4,3,2,1,0:T(8,128)} %bitcast.52), channel_id=1, replica_groups=mesh['gz'=16,'gy'=2] {'gz','gy'}, dimensions={0} | all-to-all | bytes 8388608 | tf_op jit(solution)/shard_map/all_to_all | solution.py:454
  810.7 15.8 %ratio.3 = f32[16,2,4,4,16,128]{5,4,3,2,1,0:T(8,128)} custom-call(f32[16,2,4,4,16,128]{5,4,3,2,1,0:T(8,128)} %bitcast.44, f32[4,512,512]{2,1,0:T(8,128)} %bitcast.42, bf16[2,2,512,256]{3,2,1,0:T(8,128)(2,1)} %constant.22.clone.yb_ref, bf16[2,2,256,256]{3,2,1,0:T(8,128)(2,1)} %constant.19.clone.xb_ref, bf16[2,2,512,256]{3,2,1,0:T(8,128)(2,1)} %constant.21.clone.ya_ref, ...), custom_call_target="tpu_custom_call" | custom-call | flops 9663676416 | bytes 15728640 | tf_op jit(solution)/shard_map/ratio/pallas_call | solution.py:439
  826.5 97.5 %all_to_all.96 = f32[32,4,4,16,128]{4,3,2,1,0:T(8,128)} all-to-all(f32[32,4,4,16,128]{4,3,2,1,0:T(8,128)} %bitcast.45), channel_id=1, replica_groups=mesh['gz'=16,'gy'=2] {'gz','gy'}, dimensions={0} | all-to-all | bytes 8388608 | tf_op jit(solution)/shard_map/all_to_all | solution.py:454
  924.0 9.6 adjoint.3
  933.5 97.5 %all_to_all.97 = f32[32,4,4,16,128]{4,3,2,1,0:T(8,128)} all-to-all(f32[32,4,4,16,128]{4,3,2,1,0:T(8,128)} %bitcast.48), channel_id=1, replica_groups=mesh['gz'=16,'gy'=2] {'gz','gy'}, dimensions={0} | all-to-all | bytes 8388608 | tf_op jit(solution)/shard_map/all_to_all | solution.py:454
  1031.0 14.0 %last.1 = f32[4,512,512]{2,1,0:T(8,128)} custom-call(f32[16,2,4,4,16,128]{5,4,3,2,1,0:T(8,128)} %bitcast.46, f32[4,512,512]{2,1,0:T(8,128)} %get-tuple-element.8.estimate_ref, bf16[2,2,1024,256]{3,2,1,0:T(8,128)(2,1)} %constant.23.clone.yb_ref, bf16[2,512,512]{2,1,0:T(8,128)(2,1)} %constant.20.clone.xb_ref), custom_call_target="tpu_custom_call" | custom-call | flops 9663676416 | bytes 15728640 | tf_op jit(solution)/shard_map/last/pallas_call | solution.py:439
  1045.1 4.9 copy.24
  1050.0 50.5 %all_to_all.98 = f32[4,512,512]{2,0,1:T(4,128)S(1)} all-to-all(f32[4,512,512]{2,0,1:T(4,128)S(1)} %copy.24), channel_id=1, replica_groups=mesh['gz'=16,'gy'=2] {'gy'}, dimensions={1} | all-to-all | bytes 8388608 | tf_op jit(solution)/shard_map/all_to_all | solution.py:463
  1100.4 3.3 copy.25
Async XLA Ops:
  0.0 5.7 copy-start
  0.0 54.6 %all-to-all-start = ((f32[8,256,512]{2,1,0:T(8,128)}), f32[8,256,512]{2,1,0:T(8,128)}, u32[]{:S(2)}, u32[]{:S(2)}) async-start(f32[8,256,512]{2,1,0:T(8,128)} %param.12), calls=%async_computation | async-start | bytes 8388608 | tf_op jit(solution)/shard_map/all_to_all | solution.py:459
  54.6 83.9 %all-to-all-start.2 = ((f32[2,8,256,256]{3,1,0,2:T(8,128)}), f32[2,8,256,256]{3,1,0,2:T(8,128)}, u32[]{:S(2)}, u32[]{:S(2)}) async-start(f32[2,8,256,256]{3,1,0,2:T(8,128)} %pad_maximum_fusion), calls=%async_computation.2 | async-start | bytes 8388608 | tf_op jit(solution)/shard_map/all_to_all | solution.py:469
  138.5 117.4 %all-to-all-start.1 = ((f32[32,4,4,16,128]{4,3,2,1,0:T(8,128)}), f32[32,4,4,16,128]{4,3,2,1,0:T(8,128)}, u32[]{:S(2)}, u32[]{:S(2)}) async-start(f32[32,4,4,16,128]{4,3,2,1,0:T(8,128)} %bitcast.43), calls=%async_computation.1 | async-start | bytes 8388608 | tf_op jit(solution)/shard_map/all_to_all | solution.py:454

commit v2 on v1

--- a/solution.py
+++ b/solution.py
@@ -252,7 +252,7 @@
     return two_terms(np.stack(ahead)), two_terms(np.stack(sharp)), two_terms(np.stack(soft))
 
 
-def z_tables(length):
+def z_tables(length, order):
     where = np.arange(length)
     angle = phase_np(where, where, length)
     cosine, sine = np.cos(angle), np.sin(angle)
@@ -261,7 +261,9 @@
     sharp = np.block([[cosine, -sine], [sine, cosine]])
     cosine, sine = smooth_np(cosine, 0), smooth_np(sine, 0)
     soft = np.block([[cosine, -sine], [sine, cosine]])
-    return two_terms(ahead), two_terms(sharp), two_terms(soft)
+    cosine, sine = cosine[order], sine[order]
+    parted = np.block([[cosine, -sine], [sine, cosine]])
+    return two_terms(ahead), two_terms(sharp), two_terms(soft), two_terms(parted)
 
 
 def dot(left, right):
@@ -402,10 +404,9 @@
     out_ref[0, :, half:] = estimate_ref[0, :, half:] * right
 
 
-def gain_kernel(conjugate, got_ref, gain_ref, za_ref, zb_ref, send_ref):
+def gain_kernel(conjugate, got_ref, gain_ref, za_ref, zb_ref, *send_refs):
     z_len, _, rows, _ = got_ref.shape
     flat = got_ref.reshape(z_len * 2 * rows, LANES)
-    sent = send_ref.reshape(z_len * 2 * rows, LANES)
 
     def column(part):
         pieces = [flat[pl.ds(part * rows + i, z_len, 2 * rows), :] for i in range(rows)]
@@ -420,11 +421,17 @@
     else:
         turned = (real * gain_real - imag * gain_imag, real * gain_imag + imag * gain_real)
     values = table_times(zb_ref[0], zb_ref[1], jnp.concatenate(turned, axis=0))
-    for part in range(2):
-        for i in range(rows):
-            sent[pl.ds(part * rows + i, z_len, 2 * rows), :] = values[
-                part * z_len : (part + 1) * z_len, i * LANES : (i + 1) * LANES
-            ]
+    start = 0
+    for send_ref in send_refs:
+        count = send_ref.shape[0]
+        sent = send_ref.reshape(count * 2 * rows, LANES)
+        for part in range(2):
+            low = part * z_len + start
+            for i in range(rows):
+                sent[pl.ds(part * rows + i, count, 2 * rows), :] = values[
+                    low : low + count, i * LANES : (i + 1) * LANES
+                ]
+        start += count
 
 
 VMEM_BYTES = 58 * 2**20
@@ -455,12 +462,35 @@
     return flat.reshape(values.shape)
 
 
+def swap(pieces):
+    devs = pieces.shape[0]
+    me = lax.axis_index("gy")
+    got = lax.dynamic_update_index_in_dim(
+        jnp.zeros_like(pieces), lax.dynamic_index_in_dim(pieces, me, 0), me, 0
+    )
+    for step in range(1, devs):
+        to, source = lax.rem(me + step, devs), lax.rem(me + devs - step, devs)
+        piece = lax.dynamic_index_in_dim(pieces, to, 0)
+        piece = lax.ppermute(piece, "gy", [(i, (i + step) % devs) for i in range(devs)])
+        got = lax.dynamic_update_index_in_dim(got, piece, source, 0)
+    return got
+
+
 def to_planes(volume):
-    return lax.all_to_all(volume, "gy", split_axis=0, concat_axis=1, tiled=True)
-
-
-def from_planes(volume):
-    return lax.all_to_all(volume, "gy", split_axis=1, concat_axis=0, tiled=True)
+    devs = lax.axis_size("gy")
+    z_local, y_local, x_len = volume.shape
+    got = swap(volume.reshape(devs, z_local // devs, y_local, x_len))
+    return got.transpose(1, 0, 2, 3).reshape(z_local // devs, devs * y_local, x_len)
+
+
+def from_planes(groups):
+    devs = lax.axis_size("gy")
+    parts = []
+    for group in groups:
+        count, y_len, x_len = group.shape
+        parts.append(swap(group.reshape(count, devs, y_len // devs, x_len).transpose(1, 0, 2, 3)))
+    whole_part = jnp.concatenate(parts, axis=1)
+    return whole_part.reshape(-1, *whole_part.shape[2:])
 
 
 def gains_planes(transfer_real, transfer_imag):
@@ -480,7 +510,13 @@
     planes, rows = z_len // devs, y_len // devs
     xa, xb, xs = (jnp.asarray(t) for t in x_tables(x_len))
     ya, yb, ys = (jnp.asarray(t) for t in y_tables(y_len))
-    za, zb, zs = (jnp.asarray(t) for t in z_tables(z_len))
+    groups = (planes - 1, 1) if planes > 1 else (planes,)
+    starts = [sum(groups[:i]) for i in range(len(groups))]
+    by_plane = np.arange(z_len).reshape(devs, planes)
+    order = np.concatenate(
+        [by_plane[:, s : s + n].reshape(-1) for s, n in zip(starts, groups)]
+    )
+    za, zb, zs, zp = (jnp.asarray(t) for t in z_tables(z_len, order))
 
     spectrum = jax.ShapeDtypeStruct((z_devs, y_devs, planes, 4, rows, LANES), jnp.float32)
     volume = jax.ShapeDtypeStruct((planes, y_len, x_len), jnp.float32)
@@ -511,38 +547,44 @@
             ahead_flops + soft_flops, "correct",
         )
 
-    def last(got, values):
+    def last(got, values, start):
+        count = got.shape[2]
         return call(
-            last_kernel, (planes,), (got, values), (spectrum_spec, volume_spec), (ys, xs),
-            volume, volume_spec, soft_flops, "last",
-        )
-
-    columns = jax.ShapeDtypeStruct((z_len, 4, rows, LANES), jnp.float32)
-    columns_spec = pl.BlockSpec((z_len, 2, rows // 2, LANES), lambda s: (0, s % 2, s // 2, 0))
-
-    def filtered(got, gains, conjugate):
+            last_kernel, (count,), (got, values),
+            (spectrum_spec, pl.BlockSpec((1, y_len, x_len), lambda p: (p + start, 0, 0))),
+            (ys, xs), jax.ShapeDtypeStruct((count, y_len, x_len), jnp.float32), volume_spec,
+            soft_flops * count // planes, "last",
+        )
+
+    columns = (z_len, 4, rows, LANES)
+
+    def columns_spec(count):
+        return pl.BlockSpec((count, 2, rows // 2, LANES), lambda s: (0, s % 2, s // 2, 0))
+
+    def filtered(got, gains, conjugate, back, parts):
         gains_spec = pl.BlockSpec((1, *gains.shape[1:]), lambda s: (s, 0, 0, 0))
-        return call(
+        sent = call(
             functools.partial(gain_kernel, conjugate), (4,),
-            (got.reshape(columns.shape), gains), (columns_spec, gains_spec),
-            (za, zs if conjugate else zb), columns, columns_spec,
+            (got.reshape(columns), gains), (columns_spec(z_len), gains_spec),
+            (za, back),
+            [jax.ShapeDtypeStruct((devs * n, *columns[1:]), jnp.float32) for n in parts],
+            [columns_spec(devs * n) for n in parts],
             3 * 2 * 2 * 4 * z_len * z_len * rows * x_len, "adjoint" if conjugate else "blur",
-        ).reshape(spectrum.shape)
-
+        )
+        return [v.reshape(z_devs, y_devs, n, *columns[1:]) for v, n in zip(sent, parts)]
+
+    gains = gains_planes(transfer_real, transfer_imag)
     measured = to_planes(measured)
-    gains = gains_planes(transfer_real, transfer_imag)
     estimate = measured
     send = first(measured)
     for iteration in range(ITERS):
-        send = filtered(exchange(send), gains, False)
+        (send,) = filtered(exchange(send), gains, False, zb, (planes,))
         send = ratio(exchange(send), measured)
-        send = filtered(exchange(send), gains, True)
-        got = exchange(send)
         if iteration < ITERS - 1:
-            send, estimate = correct(got, estimate)
-        else:
-            estimate = last(got, estimate)
-    return from_planes(estimate)
+            (send,) = filtered(exchange(send), gains, True, zs, (planes,))
+            send, estimate = correct(exchange(send), estimate)
+    sends = filtered(exchange(send), gains, True, zp, groups)
+    return from_planes([last(exchange(v), estimate, s) for v, s in zip(sends, starts)])
 
 
 def planes_fit(mesh, shape):

time: 1110 us -> 1040 us (0.937)
  blocking collectives: 735 us -> 662 us
  waiting for transfers between devices: 107 us -> 95.1 us
    ppermute x0 -> x3, waiting for transfers between devices: none -> 71.2 us  [swap(): lax.ppermute(piece, 'gy', [(i, (i + step) % devs) for i in range(devs)])]
    all_to_all x1, waiting for transfers between devices: 64 us -> 13.5 us  [gains_planes(): both = lax.all_to_all(both, 'gz', split_axis=2, concat_axis=1, tiled=True)]
    all_to_all x1 -> x0, blocking collectives: 50.5 us -> none  [from_planes(): return lax.all_to_all(volume, 'gy', split_axis=1, concat_axis=0, tiled=True)]
    all_to_all x1 -> x0, waiting for transfers between devices: 42.6 us -> none  [to_planes(): return lax.all_to_all(volume, 'gy', split_axis=0, concat_axis=1, tiled=True)]
    all_to_all x7, blocking collectives: 684 us -> 662 us  [exchange(): lax.all_to_all(flat, ('gz', 'gy'), split_axis=0, concat_axis=0, tiled=True)]
    all_to_all x1 -> x2, starting transfers between devices: 18.8 us -> 23.3 us  [exchange(): lax.all_to_all(flat, ('gz', 'gy'), split_axis=0, concat_axis=0, tiled=True)]
    pallas_call x9 -> x10, Pallas kernels: 114 us -> 117 us  [call(): pl.pallas_call(kernel, grid=grid, in_specs=list(specs) + [whole(t) for t...]
  transfers between devices with their start and end apart: 3 -> 6, of which waited for: 2 -> 4; matrix products, arithmetic and copies ran while one was open for 10% -> 11% of each run, Pallas kernels for 1% -> 3%
where the time goes in v2:
time: 1040 us; the launch traced here: 1030 us
  blocking collectives  662 us (64%)
  local copies, waits for them, and re-layouts  120 us (12%)
  Pallas kernels  117 us (11%)
  waiting for transfers between devices  95.1 us (9%)
  starting transfers between devices  35.6 us (3%)
    all_to_all x7, blocking collectives, exchange(): lax.all_to_all(flat, ('gz', 'gy'), split_axis=0, concat_axis=0, tiled=True)  662 us
    pallas_call x10, Pallas kernels, call(): pl.pallas_call(kernel, grid=grid, in_specs=list(specs) + [whole(t) for t...  117 us
    ppermute x3, waiting for transfers between devices, swap(): lax.ppermute(piece, 'gy', [(i, (i + step) % devs) for i in range(devs)])  71.2 us
    reshape x1, local copies, waits for them, and re-layouts, gains_planes(): both.reshape(2, z_len, rows // 2, 2, half // 2, 2)  48 us
    all_to_all x1, local copies, waits for them, and re-layouts, gains_planes(): both = lax.all_to_all(both, 'gz', split_axis=2, concat_axis=1, tiled=True)  40.6 us
    all_to_all x2, starting transfers between devices, exchange(): lax.all_to_all(flat, ('gz', 'gy'), split_axis=0, concat_axis=0, tiled=True)  23.3 us
  transfers between devices with their start and end apart: 6, of which 4 were waited for; matrix products, arithmetic and copies ran while one was open for 11% of the time, Pallas kernels for 3%

profile of v2, /device:TPU:0, one launch (start us, length us, event | category | flops | bytes accessed | tf_op | source)
XLA Modules:
  0.0 1034.4 jit_solution(5106395883070672893)
XLA Ops:
  0.0 4.7 copy_bitcast_fusion
  4.7 2.3 pad_maximum_fusion
  6.9 7.4 all-to-all-start.1
  14.4 3.1 dynamic-slice_bitcast_fusion
  17.5 1.5 collective-permute-start
  19.0 0.0 copy-start.1
  19.0 0.5 broadcast_in_dim.10
  19.5 1.7 copy-done.1
  21.2 0.2 bitcast_dynamic-update-slice_fusion
  21.4 44.3 %collective-permute-done = f32[1,4,256,512]{3,2,0,1:T(8,128)} collective-permute-done((f32[1,4,256,512]{3,2,0,1:T(8,128)}, f32[1,4,256,512]{3,2,0,1:T(8,128)}, u32[]{:S(2)}, u32[]{:S(2)}) %collective-permute-start) | collective-permute-done | bytes 2097184 | tf_op jit(solution)/shard_map/ppermute | solution.py:474
  65.7 1.8 constant_dynamic-update-slice_fusion.1
  67.5 0.0 copy-start.2
  67.5 2.0 copy-done.2
  69.5 9.0 first.1
  78.5 13.5 %all-to-all-done.1 = f32[2,8,256,256]{3,1,0,2:T(8,128)} async-done(((f32[2,8,256,256]{3,1,0,2:T(8,128)}), f32[2,8,256,256]{3,1,0,2:T(8,128)}, u32[]{:S(2)}, u32[]{:S(2)}) %all-to-all-start.1) | async-done | bytes 4194336 | tf_op jit(solution)/shard_map/all_to_all | solution.py:499
  92.1 19.7 %all-to-all-start = ((f32[32,4,4,16,128]{4,3,2,1,0:T(8,128)}), f32[32,4,4,16,128]{4,3,2,1,0:T(8,128)}, u32[]{:S(2)}, u32[]{:S(2)}) async-start(f32[32,4,4,16,128]{4,3,2,1,0:T(8,128)} %bitcast.56), calls=%async_computation | async-start | bytes 8388608 | tf_op jit(solution)/shard_map/all_to_all | solution.py:461
  111.8 40.6 %copy.28 = f32[2,8,16,16,256]{1,2,4,3,0:T(8,128)} copy(f32[2,8,16,16,256]{4,1,0,3,2:T(8,128)} %bitcast.7) | data formatting | bytes 8388608 | tf_op jit(solution)/shard_map/all_to_all | solution.py:499
  152.3 48.0 %reshape.51 = f32[2,128,8,2,128,2]{1,5,4,3,2,0:T(2,128)} reshape(f32[2,16,8,16,256]{2,1,4,3,0:T(8,128)} %bitcast.8) | data formatting | bytes 8388608 | tf_op jit(solution)/shard_map/reshape | solution.py:501
  200.3 5.3 copy.29
  205.6 4.9 reshape.52.gain_ref
  210.5 0.0 all-to-all-done
  210.5 9.7 blur.2
  220.2 99.5 %all_to_all.60 = f32[32,4,4,16,128]{4,3,2,1,0:T(8,128)} all-to-all(f32[32,4,4,16,128]{4,3,2,1,0:T(8,128)} %bitcast.66), channel_id=1, replica_groups=mesh['gz'=16,'gy'=2] {'gz','gy'}, dimensions={0} | all-to-all | bytes 8388608 | tf_op jit(solution)/shard_map/all_to_all | solution.py:461
  319.7 15.7 %ratio.2 = f32[16,2,4,4,16,128]{5,4,3,2,1,0:T(8,128)} custom-call(f32[16,2,4,4,16,128]{5,4,3,2,1,0:T(8,128)} %bitcast.67, f32[4,512,512]{2,1,0:T(8,128)} %bitcast.70, bf16[2,2,512,256]{3,2,1,0:T(8,128)(2,1)} %constant.79.clone.yb_ref, bf16[2,2,256,256]{3,2,1,0:T(8,128)(2,1)} %constant.76.clone.xb_ref, bf16[2,2,512,256]{3,2,1,0:T(8,128)(2,1)} %constant.78.clone.ya_ref, ...), custom_call_target="tpu_custom_call" | custom-call | flops 9663676416 | bytes 15728640 | tf_op jit(solution)/shard_map/ratio/pallas_call | solution.py:446
  335.4 97.5 %all_to_all.61 = f32[32,4,4,16,128]{4,3,2,1,0:T(8,128)} all-to-all(f32[32,4,4,16,128]{4,3,2,1,0:T(8,128)} %bitcast.68), channel_id=1, replica_groups=mesh['gz'=16,'gy'=2] {'gz','gy'}, dimensions={0} | all-to-all | bytes 8388608 | tf_op jit(solution)/shard_map/all_to_all | solution.py:461
  432.9 9.7 adjoint.2
  442.5 97.5 %all_to_all.62 = f32[32,4,4,16,128]{4,3,2,1,0:T(8,128)} all-to-all(f32[32,4,4,16,128]{4,3,2,1,0:T(8,128)} %bitcast.63), channel_id=1, replica_groups=mesh['gz'=16,'gy'=2] {'gz','gy'}, dimensions={0} | all-to-all | bytes 8388608 | tf_op jit(solution)/shard_map/all_to_all | solution.py:461
  540.0 20.6 %correct.1 = (f32[16,2,4,4,16,128]{5,4,3,2,1,0:T(8,128)}, f32[4,512,512]{2,1,0:T(8,128)}) custom-call(f32[16,2,4,4,16,128]{5,4,3,2,1,0:T(8,128)} %bitcast.60, f32[4,512,512]{2,1,0:T(8,128)} %bitcast.71, bf16[2,2,1024,256]{3,2,1,0:T(8,128)(2,1)} %constant.80.clone.yb_ref, bf16[2,512,512]{2,1,0:T(8,128)(2,1)} %constant.77.clone.xb_ref, ...), custom_call_target="tpu_custom_call" | custom-call | flops 14495514624 | bytes 21495808 | tf_op jit(solution)/shard_map/correct/pallas_call | solution.py:446
  560.6 97.5 %all_to_all.63 = f32[32,4,4,16,128]{4,3,2,1,0:T(8,128)} all-to-all(f32[32,4,4,16,128]{4,3,2,1,0:T(8,128)} %bitcast.61), channel_id=1, replica_groups=mesh['gz'=16,'gy'=2] {'gz','gy'}, dimensions={0} | all-to-all | bytes 8388608 | tf_op jit(solution)/shard_map/all_to_all | solution.py:461
  658.1 9.6 blur.3
  667.7 97.5 %all_to_all.64 = f32[32,4,4,16,128]{4,3,2,1,0:T(8,128)} all-to-all(f32[32,4,4,16,128]{4,3,2,1,0:T(8,128)} %bitcast.65), channel_id=1, replica_groups=mesh['gz'=16,'gy'=2] {'gz','gy'}, dimensions={0} | all-to-all | bytes 8388608 | tf_op jit(solution)/shard_map/all_to_all | solution.py:461
  765.2 15.7 %ratio.3 = f32[16,2,4,4,16,128]{5,4,3,2,1,0:T(8,128)} custom-call(f32[16,2,4,4,16,128]{5,4,3,2,1,0:T(8,128)} %bitcast.57, f32[4,512,512]{2,1,0:T(8,128)} %bitcast.72, bf16[2,2,512,256]{3,2,1,0:T(8,128)(2,1)} %constant.79.clone.yb_ref, bf16[2,2,256,256]{3,2,1,0:T(8,128)(2,1)} %constant.76.clone.xb_ref, bf16[2,2,512,256]{3,2,1,0:T(8,128)(2,1)} %constant.78.clone.ya_ref, ...), custom_call_target="tpu_custom_call" | custom-call | flops 9663676416 | bytes 15728640 | tf_op jit(solution)/shard_map/ratio/pallas_call | solution.py:446
  780.9 97.5 %all_to_all.65 = f32[32,4,4,16,128]{4,3,2,1,0:T(8,128)} all-to-all(f32[32,4,4,16,128]{4,3,2,1,0:T(8,128)} %bitcast.58), channel_id=1, replica_groups=mesh['gz'=16,'gy'=2] {'gz','gy'}, dimensions={0} | all-to-all | bytes 8388608 | tf_op jit(solution)/shard_map/all_to_all | solution.py:461
  878.4 9.6 adjoint.3
  888.0 75.0 %all_to_all.66 = f32[32,3,4,16,128]{4,3,2,1,0:T(8,128)} all-to-all(f32[32,3,4,16,128]{4,3,2,1,0:T(8,128)} %bitcast.76), channel_id=1, replica_groups=mesh['gz'=16,'gy'=2] {'gz','gy'}, dimensions={0} | all-to-all | bytes 6291456 | tf_op jit(solution)/shard_map/all_to_all | solution.py:461
  963.0 3.6 all-to-all-start.9
  966.7 11.4 %last.2 = f32[3,512,512]{2,1,0:T(8,128)} custom-call(f32[16,2,3,4,16,128]{5,4,3,2,1,0:T(8,128)} %bitcast.75, f32[4,512,512]{2,1,0:T(8,128)} %get-tuple-element.11.estimate_ref, bf16[2,2,1024,256]{3,2,1,0:T(8,128)(2,1)} %constant.80.clone.yb_ref, bf16[2,512,512]{2,1,0:T(8,128)(2,1)} %constant.77.clone.xb_ref), custom_call_target="tpu_custom_call" | custom-call | flops 7247757312 | bytes 13631488 | tf_op jit(solution)/shard_map/last/pallas_call | solution.py:446
  978.1 2.7 dynamic-slice_bitcast_fusion.1
  980.8 1.8 collective-permute-start.1
  982.6 10.4 %all-to-all-done.9 = f32[32,1,4,16,128]{4,3,2,1,0:T(8,128)S(1)} async-done(((f32[32,1,4,16,128]{4,3,2,1,0:T(8,128)}), f32[32,1,4,16,128]{4,3,2,1,0:T(8,128)S(1)}, u32[]{:S(2)}, u32[]{:S(2)}) %all-to-all-start.9) | async-done | bytes 1048608 | tf_op jit(solution)/shard_map/all_to_all | solution.py:461
  992.9 0.0 copy-start
  992.9 1.0 copy-done
  993.9 6.1 last.3
  1000.0 0.0 copy-start.3
  1000.0 1.2 constant_dynamic-slice_fusion
  1001.2 1.5 collective-permute-start.2
  1002.7 0.1 broadcast_in_dim.11
  1002.9 1.1 bitcast_dynamic-update-slice_fusion.3
  1004.0 26.9 %collective-permute-done.2 = f32[1,1,256,512]{3,2,0,1:T(8,128)S(1)} collective-permute-done((f32[1,1,256,512]{3,2,0,1:T(8,128)S(1)}, f32[1,1,256,512]{3,2,0,1:T(8,128)S(1)}, u32[]{:S(2)}, u32[]{:S(2)}) %collective-permute-start.2) | collective-permute-done | bytes 524320 | tf_op jit(solution)/shard_map/ppermute | solution.py:474
  1030.9 0.4 broadcast_in_dim.9
  1031.3 0.0 copy-done.3
  1031.3 0.1 bitcast_dynamic-update-slice_fusion.1
  1031.4 0.0 collective-permute-done.1
  1031.5 0.1 constant_dynamic-update-slice_fusion
  1031.6 2.8 pad_maximum_fusion.1
  (1 shorter events, 0.0 us)
Async XLA Ops:
  6.9 85.1 %all-to-all-start.1 = ((f32[2,8,256,256]{3,1,0,2:T(8,128)}), f32[2,8,256,256]{3,1,0,2:T(8,128)}, u32[]{:S(2)}, u32[]{:S(2)}) async-start(f32[2,8,256,256]{3,1,0,2:T(8,128)} %pad_maximum_fusion), calls=%async_computation.1 | async-start | bytes 8388608 | tf_op jit(solution)/shard_map/all_to_all | solution.py:499
  17.5 48.2 %collective-permute-start = (f32[1,4,256,512]{3,2,0,1:T(8,128)}, f32[1,4,256,512]{3,2,0,1:T(8,128)}, u32[]{:S(2)}, u32[]{:S(2)}) collective-permute-start(f32[1,4,256,512]{3,2,0,1:T(8,128)} %dynamic-slice_bitcast_fusion), channel_id=1, source_target_pairs={{0,1},{1,0},{2,3},{3,2},{4,5},{5,4},{6,7},{7,6},{8,9},{9,8},{10,11... | collective-permute-start | bytes 6291464 | tf_op jit(solution)/shard_map/ppermute | solution.py:474
  19.0 2.2 copy-start.1
  67.5 2.0 copy-start.2
  92.1 118.4 %all-to-all-start = ((f32[32,4,4,16,128]{4,3,2,1,0:T(8,128)}), f32[32,4,4,16,128]{4,3,2,1,0:T(8,128)}, u32[]{:S(2)}, u32[]{:S(2)}) async-start(f32[32,4,4,16,128]{4,3,2,1,0:T(8,128)} %bitcast.56), calls=%async_computation | async-start | bytes 8388608 | tf_op jit(solution)/shard_map/all_to_all | solution.py:461
  963.0 29.9 %all-to-all-start.9 = ((f32[32,1,4,16,128]{4,3,2,1,0:T(8,128)}), f32[32,1,4,16,128]{4,3,2,1,0:T(8,128)S(1)}, u32[]{:S(2)}, u32[]{:S(2)}) async-start(f32[32,1,4,16,128]{4,3,2,1,0:T(8,128)} %bitcast.28), calls=%async_computation.9 | async-start | bytes 2097152 | tf_op jit(solution)/shard_map/all_to_all | solution.py:461
  980.8 50.7 %collective-permute-start.1 = (f32[1,3,256,512]{3,2,1,0:T(8,128)}, f32[1,3,256,512]{3,2,1,0:T(8,128)S(1)}, u32[]{:S(2)}, u32[]{:S(2)}) collective-permute-start(f32[1,3,256,512]{3,2,1,0:T(8,128)} %dynamic-slice_bitcast_fusion.1), channel_id=1, source_target_pairs={{0,1},{1,0},{2,3},{3,2},{4,5},{5,4},{6,7},{7,6},{8,9},{9,8},{10,11... | collective-permute-start | bytes 4718600 | tf_op jit(solution)/shard_map/ppermute | solution.py:474
  992.9 1.0 copy-start
  1000.0 31.3 %copy-start.3 = (f32[3,512,512]{2,1,0:T(8,128)S(1)}, f32[3,512,512]{2,1,0:T(8,128)}, u32[]{:S(2)}) copy-start(f32[3,512,512]{2,1,0:T(8,128)} %last.2) | copy-start | bytes 9437188
  1001.2 29.6 %collective-permute-start.2 = (f32[1,1,256,512]{3,2,0,1:T(8,128)S(1)}, f32[1,1,256,512]{3,2,0,1:T(8,128)S(1)}, u32[]{:S(2)}, u32[]{:S(2)}) collective-permute-start(f32[1,1,256,512]{3,2,0,1:T(8,128)S(1)} %constant_dynamic-slice_fusion), channel_id=1, source_target_pairs={{0,1},{1,0},{2,3},{3,2},{4,5},{5,4},{6,7},{7,6},{8,9},{9,8},{10,11... | collective-permute-start | bytes 1572872 | tf_op jit(solution)/shard_map/ppermute | solution.py:474

commit v3 on v0

--- a/solution.py
+++ b/solution.py
@@ -1,8 +1,12 @@
+import functools
 import math
 
 import jax
 import jax.numpy as jnp
+import numpy as np
 from jax import lax
+from jax.experimental import pallas as pl
+from jax.experimental.pallas import tpu as pltpu
 from jax.sharding import PartitionSpec as P
 
 ITERS = 2
@@ -160,7 +164,7 @@
     )
 
 
-def on_device(measured, transfer_real, transfer_imag):
+def on_device_rows(measured, transfer_real, transfer_imag):
     z_local, y_local, x_len = measured.shape
     z_len = z_local * lax.axis_size("gz")
     y_len = y_local * lax.axis_size("gy")
@@ -186,11 +190,439 @@
     return estimate
 
 
+LANES = 128
+SUBLANES = 8
+
+
+def gauss_weights_np():
+    offsets = np.arange(-RADIUS, RADIUS + 1).astype(np.float64)
+    weights = np.exp(-offsets * offsets / (2.0 * SIGMA * SIGMA))
+    return weights / weights.sum()
+
+
+def smooth_np(table, axis):
+    weights = gauss_weights_np()
+    widths = [(0, 0)] * table.ndim
+    widths[axis] = (RADIUS, RADIUS)
+    padded = np.pad(table, widths)
+    length = table.shape[axis]
+    return sum(
+        weights[j] * np.take(padded, np.arange(j, j + length), axis=axis)
+        for j in range(2 * RADIUS + 1)
+    )
+
+
+def two_terms(table):
+    high = table.astype(np.float32).astype(jnp.bfloat16)
+    low = (table - high.astype(np.float64)).astype(np.float32).astype(jnp.bfloat16)
+    return np.stack((high, low))
+
+
+def phase_np(first, second, length):
+    return 2.0 * np.pi * ((first[:, None] * second[None, :]) % length) / length
+
+
+def x_tables(length):
+    half = length // 2
+    where = np.arange(length)
+    ahead, behind = [], []
+    for odd in range(2):
+        k = 2 * np.arange(half // 2) + odd
+        angle = phase_np(k, where, length)
+        ahead.append(np.concatenate((np.cos(angle), -np.sin(angle)), axis=0)[:, :half])
+        weight = (np.where(k == 0, 1.0, 2.0) / length)[:, None]
+        behind.append(np.concatenate((weight * np.cos(angle), -weight * np.sin(angle)), axis=0))
+    sharp = np.stack([table[:, :half] for table in behind])
+    soft = smooth_np(np.concatenate(behind, axis=0), 1)
+    return two_terms(np.stack(ahead)), two_terms(sharp), two_terms(soft)
+
+
+def y_tables(length):
+    half = length // 2
+    where = np.arange(length)
+    ahead, sharp, soft = [], [], []
+    for odd in range(2):
+        k = 2 * np.arange(half) + odd
+        angle = phase_np(where, k, length)
+        cosine, sine = np.cos(angle), np.sin(angle)
+        ahead.append(np.concatenate((cosine[:half], sine[:half]), axis=1))
+        cosine, sine = cosine.T / length, sine.T / length
+        sharp.append(np.concatenate((cosine[:, :half], sine[:, :half]), axis=1))
+        soft.append(np.concatenate((smooth_np(cosine, 1), smooth_np(sine, 1)), axis=1))
+    return two_terms(np.stack(ahead)), two_terms(np.stack(sharp)), two_terms(np.concatenate(soft))
+
+
+def z_tables(length):
+    where = np.arange(length)
+    angle = phase_np(where, where, length)
+    cosine, sine = np.cos(angle), np.sin(angle)
+    ahead = np.block([[cosine, sine], [-sine, cosine]])
+    cosine, sine = cosine / length, sine / length
+    sharp = np.block([[cosine, -sine], [sine, cosine]])
+    cosine, sine = smooth_np(cosine, 0), smooth_np(sine, 0)
+    soft = np.block([[cosine, -sine], [sine, cosine]])
+    return two_terms(ahead), two_terms(sharp), two_terms(soft)
+
+
+def dot(left, right):
+    return jnp.dot(left, right, preferred_element_type=jnp.float32)
+
+
+def split_terms(values):
+    high = values.astype(jnp.bfloat16)
+    return high, (values - high.astype(jnp.float32)).astype(jnp.bfloat16)
+
+
+def table_times(high, low, values):
+    first, second = split_terms(values)
+    return dot(
+        jnp.concatenate((high, high, low), axis=1), jnp.concatenate((first, second, first), axis=0)
+    )
+
+
+def times_table(values, high, low):
+    first, second = split_terms(values)
+    return dot(
+        jnp.concatenate((first, second, first), axis=1), jnp.concatenate((high, high, low), axis=0)
+    )
+
+
+def table_times_lines(high, low, values):
+    first, second = split_terms(values)
+    return lax.dot_general(
+        jnp.concatenate((high, high, low), axis=1),
+        jnp.concatenate((first, second, first), axis=1),
+        (((1,), (1,)), ((), ())),
+        preferred_element_type=jnp.float32,
+    )
+
+
+def lines_of(values, high, low):
+    return times_table(values.T, high, low)
+
+
+def load_lines(got_ref):
+    kx_len = got_ref.shape[0] * got_ref.shape[1]
+    z_len = got_ref.shape[4]
+    flat = got_ref.reshape(kx_len * 2 * z_len, LANES)
+    parities = []
+    for odd in range(2):
+        parts = []
+        for part in range(2):
+            pieces = [
+                flat[pl.ds((odd * 2 + part) * z_len + z, kx_len // 2, 4 * z_len), :]
+                for z in range(z_len)
+            ]
+            parts.append(jnp.concatenate(pieces, axis=1))
+        parities.append(jnp.concatenate(parts, axis=0))
+    return parities
+
+
+def store_lines(send_ref, odd, values):
+    kx_len = send_ref.shape[0] * send_ref.shape[1]
+    z_len = send_ref.shape[4]
+    flat = send_ref.reshape(kx_len * 2 * z_len, LANES)
+    half = kx_len // 2
+    for part in range(2):
+        for z in range(z_len):
+            flat[pl.ds((odd * 2 + part) * z_len + z, half, 4 * z_len), :] = values[
+                part * half : (part + 1) * half, z * LANES : (z + 1) * LANES
+            ]
+
+
+def lines_back_sharp(got_ref, x_ref):
+    even, odd = load_lines(got_ref)
+    even = lines_of(even, x_ref[0, 0], x_ref[1, 0])
+    odd = lines_of(odd, x_ref[0, 1], x_ref[1, 1])
+    return even + odd, even - odd
+
+
+def lines_back_soft(got_ref, x_ref):
+    both = lines_of(jnp.concatenate(load_lines(got_ref), axis=0), x_ref[0], x_ref[1])
+    half = both.shape[1] // 2
+    return both[:, :half], both[:, half:]
+
+
+def lines_ahead(left, right, send_ref, x_ref):
+    store_lines(send_ref, 0, table_times_lines(x_ref[0, 0], x_ref[1, 0], left + right))
+    store_lines(send_ref, 1, table_times_lines(x_ref[0, 1], x_ref[1, 1], left - right))
+
+
+def halves(volume_ref):
+    half = volume_ref.shape[2] // 2
+    return (
+        volume_ref[:, :, :half].reshape(-1, half),
+        volume_ref[:, :, half:].reshape(-1, half),
+    )
+
+
+def store_halves(volume_ref, left, right):
+    half = volume_ref.shape[2] // 2
+    shape = (*volume_ref.shape[:2], half)
+    volume_ref[:, :, :half] = left.reshape(shape)
+    volume_ref[:, :, half:] = right.reshape(shape)
+
+
+def first_kernel(volume_ref, xa_ref, send_ref):
+    left, right = halves(volume_ref)
+    lines_ahead(left, right, send_ref, xa_ref)
+
+
+def ratio_kernel(got_ref, measured_ref, xb_ref, xa_ref, send_ref):
+    left, right = lines_back_sharp(got_ref, xb_ref)
+    over_left, over_right = halves(measured_ref)
+    left = over_left / jnp.maximum(left, FLOOR)
+    right = over_right / jnp.maximum(right, FLOOR)
+    lines_ahead(left, right, send_ref, xa_ref)
+
+
+def correct_kernel(got_ref, estimate_ref, xb_ref, xa_ref, send_ref, out_ref):
+    left, right = lines_back_soft(got_ref, xb_ref)
+    old_left, old_right = halves(estimate_ref)
+    left, right = old_left * left, old_right * right
+    store_halves(out_ref, left, right)
+    lines_ahead(left, right, send_ref, xa_ref)
+
+
+def last_kernel(got_ref, estimate_ref, xb_ref, out_ref):
+    left, right = lines_back_soft(got_ref, xb_ref)
+    old_left, old_right = halves(estimate_ref)
+    store_halves(out_ref, old_left * left, old_right * right)
+
+
+def arrange_kernel(real_ref, imag_ref, pick_ref, send_ref):
+    z_len, _, kx_len = real_ref.shape
+    tiles = send_ref.shape[2]
+    flat = send_ref.reshape(kx_len * 2 * tiles * z_len, LANES)
+    for part, ref in enumerate((real_ref, imag_ref)):
+        for z in range(z_len):
+            values = ref[z].T
+            first, second = split_terms(values)
+            rest = values - first.astype(jnp.float32) - second.astype(jnp.float32)
+            pick = pick_ref[...]
+            values = dot(first, pick) + dot(second, pick) + dot(rest.astype(jnp.bfloat16), pick)
+            for tile in range(tiles):
+                start = (part * tiles + tile) * z_len + z
+                flat[pl.ds(start, kx_len, 2 * tiles * z_len), :] = values[
+                    :, tile * LANES : (tile + 1) * LANES
+                ]
+
+
+def plane_of(ref, k, part, tiles):
+    pieces = [
+        ref[:, g, k, part, tile].reshape(-1, LANES) for g in range(ref.shape[1]) for tile in tiles
+    ]
+    return jnp.concatenate(pieces, axis=1)
+
+
+def turned_ahead(both):
+    rows, half = both.shape[0] // 2, both.shape[1] // 2
+    return (
+        both[:rows, :half] + both[rows:, half:],
+        both[rows:, :half] - both[:rows, half:],
+    )
+
+
+def turned_back(both):
+    rows, half = both.shape[0] // 2, both.shape[1] // 2
+    return (
+        both[:rows, :half] - both[rows:, half:],
+        both[rows:, :half] + both[:rows, half:],
+    )
+
+
+def gain_kernel(adjoint, got_ref, gain_ref, ya_ref, za_ref, zb_ref, yb_ref, send_ref):
+    z_devs, y_devs, share, _, tiles, z_local, _ = got_ref.shape
+    rows = 2 * z_devs * z_local
+    half = y_devs * tiles * LANES // 2
+
+    def by_kx(values):
+        return [values[k * rows : (k + 1) * rows] for k in range(share)]
+
+    values = jnp.concatenate(
+        [plane_of(got_ref, k, part, range(tiles)) for k in range(share) for part in range(2)],
+        axis=0,
+    )
+    left, right = values[:, :half], values[:, half:]
+    evens = by_kx(times_table(left + right, ya_ref[0, 0], ya_ref[1, 0]))
+    odds = by_kx(times_table(left - right, ya_ref[0, 1], ya_ref[1, 1]))
+    planes = []
+    for k in range(share):
+        even, odd = turned_ahead(evens[k]), turned_ahead(odds[k])
+        values = jnp.concatenate(
+            [jnp.concatenate((even[part], odd[part]), axis=1) for part in range(2)], axis=0
+        )
+        values = table_times(za_ref[0], za_ref[1], values)
+        real, imag = values[: rows // 2], values[rows // 2 :]
+        gain_real, gain_imag = [
+            jnp.concatenate(
+                (
+                    plane_of(gain_ref, k, part, range(tiles // 2)),
+                    plane_of(gain_ref, k, part, range(tiles // 2, tiles)),
+                ),
+                axis=1,
+            )
+            for part in range(2)
+        ]
+        if adjoint:
+            turned = (real * gain_real + imag * gain_imag, imag * gain_real - real * gain_imag)
+        else:
+            turned = (real * gain_real - imag * gain_imag, real * gain_imag + imag * gain_real)
+        planes.append(table_times(zb_ref[0], zb_ref[1], jnp.concatenate(turned, axis=0)))
+    values = jnp.concatenate(planes, axis=0)
+    if adjoint:
+        boths = by_kx(times_table(values, yb_ref[0], yb_ref[1]))
+    else:
+        evens = by_kx(times_table(values[:, :half], yb_ref[0, 0], yb_ref[1, 0]))
+        odds = by_kx(times_table(values[:, half:], yb_ref[0, 1], yb_ref[1, 1]))
+    for k in range(share):
+        if adjoint:
+            parts = turned_back(boths[k])
+        else:
+            even, odd = turned_back(evens[k]), turned_back(odds[k])
+            parts = [jnp.concatenate((a + b, a - b), axis=1) for a, b in zip(even, odd)]
+        for part in range(2):
+            for g in range(y_devs):
+                for tile in range(tiles):
+                    low = (g * tiles + tile) * LANES
+                    send_ref[:, g, k, part, tile] = parts[part][:, low : low + LANES].reshape(
+                        z_devs, z_local, LANES
+                    )
+
+
+KX_AT_ONCE = 2
+VMEM_BYTES = 32 * 2**20
+
+
+def whole(table):
+    return pl.BlockSpec(table.shape, lambda *_: (0,) * table.ndim)
+
+
+def call(kernel, grid, arrays, specs, tables, outs, out_specs, flops, name):
+    leaves = (*arrays, *tables, *jax.tree.leaves(outs))
+    moved = sum(math.prod(a.shape) * a.dtype.itemsize for a in leaves)
+    return pl.pallas_call(
+        kernel,
+        grid=grid,
+        in_specs=list(specs) + [whole(t) for t in tables],
+        out_specs=out_specs,
+        out_shape=outs,
+        compiler_params=pltpu.CompilerParams(vmem_limit_bytes=VMEM_BYTES),
+        cost_estimate=pl.CostEstimate(flops=flops, bytes_accessed=moved, transcendentals=0),
+        name=name,
+    )(*arrays, *tables)
+
+
+def exchange(values):
+    return lax.all_to_all(values, ("gz", "gy"), split_axis=0, concat_axis=0, tiled=True)
+
+
+def on_device_lines(measured, transfer_real, transfer_imag):
+    z_devs, y_devs = lax.axis_size("gz"), lax.axis_size("gy")
+    devs = z_devs * y_devs
+    z_local, y_local, x_len = measured.shape
+    z_len, y_len, kx_len = z_local * z_devs, y_local * y_devs, x_len // 2
+    tiles, share = y_local // LANES, kx_len // devs
+    xa, xb, xs = (jnp.asarray(t) for t in x_tables(x_len))
+    ya, yb, ys = (jnp.asarray(t) for t in y_tables(y_len))
+    za, zb, zs = (jnp.asarray(t) for t in z_tables(z_len))
+    picked = np.concatenate((np.arange(0, y_local, 2), np.arange(1, y_local, 2)))
+    pick = jnp.asarray(np.eye(y_local, dtype=np.float32)[:, picked].astype(jnp.bfloat16))
+
+    spectrum = jax.ShapeDtypeStruct((devs, share, 2, tiles, z_local, LANES), jnp.float32)
+    volume = jax.ShapeDtypeStruct(measured.shape, jnp.float32)
+    lines_spec = pl.BlockSpec(
+        (devs, share, 2, 1, z_local, LANES), lambda t: (0, 0, 0, t, 0, 0)
+    )
+    volume_spec = pl.BlockSpec((z_local, LANES, x_len), lambda t: (0, t, 0))
+    line_flops = 3 * z_local * y_local * x_len * x_len
+
+    def first(values):
+        return call(
+            first_kernel, (tiles,), (values,), (volume_spec,), (xa,),
+            spectrum, lines_spec, line_flops, "first",
+        )
+
+    def ratio(got, values):
+        return call(
+            ratio_kernel, (tiles,), (got, values), (lines_spec, volume_spec), (xb, xa),
+            spectrum, lines_spec, 2 * line_flops, "ratio",
+        )
+
+    def correct(got, values):
+        return call(
+            correct_kernel, (tiles,), (got, values), (lines_spec, volume_spec), (xs, xa),
+            (spectrum, volume), (lines_spec, volume_spec), 3 * line_flops, "correct",
+        )
+
+    def last(got, values):
+        return call(
+            last_kernel, (tiles,), (got, values), (lines_spec, volume_spec), (xs,),
+            volume, volume_spec, 2 * line_flops, "last",
+        )
+
+    planes = (z_devs, y_devs, *spectrum.shape[1:])
+    at_once = KX_AT_ONCE if share % KX_AT_ONCE == 0 else 1
+    plane_spec = pl.BlockSpec(
+        (z_devs, y_devs, at_once, 2, tiles, z_local, LANES), lambda k: (0, 0, k, 0, 0, 0, 0)
+    )
+
+    def filtered(got, gains, adjoint):
+        return call(
+            functools.partial(gain_kernel, adjoint), (share // at_once,),
+            (got.reshape(planes), gains.reshape(planes)), (plane_spec, plane_spec),
+            (ya, za, zs, ys) if adjoint else (ya, za, zb, yb),
+            jax.ShapeDtypeStruct(planes, jnp.float32), plane_spec,
+            3 * 8 * share * z_len * y_len * (2 * z_len + y_len), "adjoint" if adjoint else "blur",
+        ).reshape(spectrum.shape)
+
+    def arranged(transfer_real, transfer_imag):
+        in_spec = pl.BlockSpec((z_local, y_local, LANES), lambda k: (0, 0, k))
+        out_spec = pl.BlockSpec((LANES, 2, tiles, z_local, LANES), lambda k: (k, 0, 0, 0, 0))
+        return call(
+            arrange_kernel, (kx_len // LANES,), (transfer_real, transfer_imag), (in_spec, in_spec),
+            (pick,), jax.ShapeDtypeStruct((kx_len, *spectrum.shape[2:]), jnp.float32), out_spec,
+            3 * 4 * z_local * y_local * y_local * kx_len, "arrange",
+        ).reshape(spectrum.shape)
+
+    send = first(measured)
+    send, transfer_real, transfer_imag = lax.optimization_barrier(
+        (send, transfer_real, transfer_imag)
+    )
+    send = exchange(send)
+    gains = exchange(arranged(transfer_real, transfer_imag))
+    estimate = measured
+    for iteration in range(ITERS):
+        send = ratio(exchange(filtered(send, gains, False)), measured)
+        send = exchange(filtered(exchange(send), gains, True))
+        if iteration < ITERS - 1:
+            send, estimate = correct(send, estimate)
+            send = exchange(send)
+    return last(send, estimate)
+
+
+def lines_fit(mesh, shape):
+    z_devs, y_devs = mesh.shape["gz"], mesh.shape["gy"]
+    z_len, y_len, x_len = shape
+    return (
+        z_len % LANES == 0
+        and z_len // z_devs == SUBLANES
+        and y_len % (2 * LANES * y_devs) == 0
+        and x_len % (4 * LANES) == 0
+        and x_len // 2 % (z_devs * y_devs) == 0
+    )
+
+
 def solution(mesh):
-    return jax.shard_map(
-        on_device,
-        mesh=mesh,
-        in_specs=(P("gz", "gy", None), P("gz", "gy", None), P("gz", "gy", None)),
-        out_specs=P("gz", "gy", None),
-        check_vma=False,
-    )
+    def run(measured, transfer_real, transfer_imag):
+        spec = P("gz", "gy", None)
+        fits = lines_fit(mesh, measured.shape)
+        return jax.shard_map(
+            on_device_lines if fits else on_device_rows,
+            mesh=mesh,
+            in_specs=(spec, spec, spec),
+            out_specs=spec,
+            check_vma=False,
+        )(measured, transfer_real, transfer_imag)
+
+    return run

time: 1710 us -> 987 us (0.58)
  waiting for transfers between devices: 448 us -> 85.4 us
  matrix products: 329 us -> 0 us
  Pallas kernels: 0 us -> 106 us
  other arithmetic: 83.4 us -> 0 us
  starting transfers between devices: 79.3 us -> 7.43 us
  blocking collectives: 718 us -> 779 us
  local copies, waits for them, and re-layouts: 40.6 us -> 8.86 us
    all_to_all x9 -> x1, waiting for transfers between devices: 448 us -> 85.4 us  [exchange(): lax.all_to_all(values, ('gz', 'gy'), split_axis=0, concat_axis=0, tiled=T...]
    dot_general x40 -> x0, matrix products: 329 us -> none  [product(): jnp.einsum(form, left, right, precision=lax.Precision.HIGHEST, preferred_...]
    pallas_call x0 -> x10, Pallas kernels: none -> 106 us  [call(): pl.pallas_call(kernel, grid=grid, in_specs=list(specs) + [whole(t) for t...]
    all_to_all x9 -> x1, starting transfers between devices: 79.3 us -> 7.43 us  [exchange(): lax.all_to_all(values, ('gz', 'gy'), split_axis=0, concat_axis=0, tiled=T...]
    all_to_all x9 -> x8, blocking collectives: 718 us -> 779 us  [exchange(): lax.all_to_all(values, ('gz', 'gy'), split_axis=0, concat_axis=0, tiled=T...]
    add x9 -> x0, other arithmetic: 33.3 us -> none  [the longest x3 25.5 us: taps_along(): total + weights[offset] * lax.slice_in_dim(padded, offset, offset + lengt...]
    another operation x13 -> x0, other arithmetic: 17.2 us -> none  [the longest x8 11.2 us: turn(): jnp.stack((first[..., 0, :] - second[..., 1, :], first[..., 1, :] + secon...]
  transfers between devices with their start and end apart: 9 -> 1, of which waited for: 9 -> 1; matrix products, arithmetic and copies ran while one was open for 6% -> 0% of each run, Pallas kernels for 0% -> 0%
where the time goes in v3:
time: 987 us; the launch traced here: 986 us
  blocking collectives  779 us (79%)
  Pallas kernels  106 us (11%)
  waiting for transfers between devices  85.4 us (9%)
    all_to_all x8, blocking collectives, exchange(): lax.all_to_all(values, ('gz', 'gy'), split_axis=0, concat_axis=0, tiled=T...  779 us
    pallas_call x10, Pallas kernels, call(): pl.pallas_call(kernel, grid=grid, in_specs=list(specs) + [whole(t) for t...  106 us
    all_to_all x1, waiting for transfers between devices, exchange(): lax.all_to_all(values, ('gz', 'gy'), split_axis=0, concat_axis=0, tiled=T...  85.4 us
  transfers between devices with their start and end apart: 1, of which 1 were waited for; matrix products, arithmetic and copies ran while one was open for 0% of the time, Pallas kernels for 0%

profile of v3, /device:TPU:0, one launch (start us, length us, event | category | flops | bytes accessed | tf_op | source)
XLA Modules:
  0.0 986.3 jit_solution(11563077428296938389)
XLA Ops:
  0.0 0.0 copy-start
  0.0 2.2 copy-done
  2.2 0.0 copy-start.4
  2.2 1.0 copy-done.4
  3.2 4.8 first.1
  8.0 0.0 copy-start.2
  8.1 2.0 copy-done.2
  10.1 0.0 copy-start.6
  10.1 0.0 copy-start.10
  10.1 7.4 all-to-all-start
  17.5 0.0 copy-done.6
  17.5 0.0 copy-done.10
  17.5 0.0 copy-start.7
  17.5 1.6 copy-done.7
  19.1 4.7 arrange.1
  23.8 0.0 copy-start.3
  23.8 2.0 copy-done.3
  25.8 85.4 %all-to-all-done = f32[32,8,2,2,8,128]{5,4,3,2,1,0:T(8,128)} async-done(((f32[32,8,2,2,8,128]{5,4,3,2,1,0:T(8,128)}), f32[32,8,2,2,8,128]{5,4,3,2,1,0:T(8,128)}, u32[]{:S(2)}, u32[]{:S(2)}) %all-to-all-start) | async-done | bytes 4194336 | tf_op jit(solution)/shard_map/all_to_all | solution.py:517
  111.2 0.0 copy-start.12
  111.2 0.0 copy-start.14
  111.2 0.0 copy-start.15
  111.2 0.0 copy-start.17
  111.2 98.4 %all_to_all.45 = f32[32,8,2,2,8,128]{5,4,3,2,1,0:T(8,128)S(1)} all-to-all(f32[32,8,2,2,8,128]{5,4,3,2,1,0:T(8,128)} %bitcast.10), channel_id=1, replica_groups=mesh['gz'=16,'gy'=2] {'gz','gy'}, dimensions={0} | all-to-all | bytes 8388608 | tf_op jit(solution)/shard_map/all_to_all | solution.py:517
  209.7 0.0 copy-done.12
  209.7 0.0 copy-done.14
  209.7 0.0 copy-done.15
  209.7 0.0 copy-done.17
  209.7 14.0 %blur.2 = f32[16,2,8,2,2,8,128]{6,5,4,3,2,1,0:T(8,128)S(1)} custom-call(f32[16,2,8,2,2,8,128]{6,5,4,3,2,1,0:T(8,128)} %bitcast.got_ref, f32[16,2,8,2,2,8,128]{6,5,4,3,2,1,0:T(8,128)S(1)} %bitcast.11, bf16[2,2,256,512]{3,2,1,0:T(8,128)(2,1)S(1)} %copy-done.12, bf16[2,256,256]{2,1,0:T(8,128)(2,1)S(1)} %copy-done.15, bf16[2,256,256]{2,1,0:T(8,128)(2,1)S(1)} %copy-done.17, ...), custom_call_target="tpu_custom_call" | custom-call | flops 9663676416 | bytes 15204352 | tf_op jit(solution)/shard_map/blur/pallas_call | solution.py:504
  223.7 0.0 copy-start.1
  223.7 0.0 copy-start.5
  223.7 0.0 copy-start.8
  223.7 97.2 %all_to_all.46.got_ref = f32[32,8,2,2,8,128]{5,4,3,2,1,0:T(8,128)S(1)} all-to-all(f32[32,8,2,2,8,128]{5,4,3,2,1,0:T(8,128)S(1)} %bitcast.19), channel_id=1, replica_groups=mesh['gz'=16,'gy'=2] {'gz','gy'}, dimensions={0} | all-to-all | bytes 8388608 | tf_op jit(solution)/shard_map/all_to_all | solution.py:517
  320.9 0.0 copy-done.1
  320.9 0.0 copy-done.5
  320.9 0.0 copy-done.8
  320.9 9.2 ratio.2
  330.1 0.0 copy-start.11
  330.1 0.0 copy-start.16
  330.2 97.2 %all_to_all.47 = f32[32,8,2,2,8,128]{5,4,3,2,1,0:T(8,128)S(1)} all-to-all(f32[32,8,2,2,8,128]{5,4,3,2,1,0:T(8,128)S(1)} %ratio.2), channel_id=1, replica_groups=mesh['gz'=16,'gy'=2] {'gz','gy'}, dimensions={0} | all-to-all | bytes 8388608 | tf_op jit(solution)/shard_map/all_to_all | solution.py:517
  427.3 0.0 copy-done.11
  427.3 0.0 copy-done.16
  427.3 16.5 %adjoint.2 = f32[16,2,8,2,2,8,128]{6,5,4,3,2,1,0:T(8,128)S(1)} custom-call(f32[16,2,8,2,2,8,128]{6,5,4,3,2,1,0:T(8,128)S(1)} %bitcast.20, f32[16,2,8,2,2,8,128]{6,5,4,3,2,1,0:T(8,128)S(1)} %bitcast.12, bf16[2,2,256,512]{3,2,1,0:T(8,128)(2,1)S(1)} %copy-done.12, bf16[2,256,256]{2,1,0:T(8,128)(2,1)S(1)} %copy-done.15, bf16[2,256,256]{2,1,0:T(8,128)(2,1)S(1)} %copy-done.16, ...), custom_call_target="tpu_custom_call" | custom-call | flops 9663676416 | bytes 16252928 | tf_op jit(solution)/shard_map/adjoint/pallas_call | solution.py:504
  443.8 0.0 copy-start.9
  443.8 97.2 %all_to_all.48.got_ref = f32[32,8,2,2,8,128]{5,4,3,2,1,0:T(8,128)S(1)} all-to-all(f32[32,8,2,2,8,128]{5,4,3,2,1,0:T(8,128)S(1)} %bitcast.21), channel_id=1, replica_groups=mesh['gz'=16,'gy'=2] {'gz','gy'}, dimensions={0} | all-to-all | bytes 8388608 | tf_op jit(solution)/shard_map/all_to_all | solution.py:517
  541.0 0.0 copy-done.9
  541.0 10.3 %correct.1 = (f32[32,8,2,2,8,128]{5,4,3,2,1,0:T(8,128)S(1)}, f32[8,256,512]{2,1,0:T(8,128)S(1)}) custom-call(f32[32,8,2,2,8,128]{5,4,3,2,1,0:T(8,128)S(1)} %all_to_all.48.got_ref, f32[8,256,512]{2,1,0:T(8,128)S(1)} %copy-done.1, bf16[2,512,512]{2,1,0:T(8,128)(2,1)S(1)} %copy-done.9, bf16[2,2,256,256]{3,2,1,0:T(8,128)(2,1)S(1)} %copy-done.5), custom_call_target="tpu_custom_call" | custom-call | flops 4831838208 | bytes 18350080 | tf_op jit(solution)/shard_map/correct/pallas_call | solution.py:504
  551.3 97.2 %all_to_all.49 = f32[32,8,2,2,8,128]{5,4,3,2,1,0:T(8,128)S(1)} all-to-all(f32[32,8,2,2,8,128]{5,4,3,2,1,0:T(8,128)S(1)} %get-tuple-element.13), channel_id=1, replica_groups=mesh['gz'=16,'gy'=2] {'gz','gy'}, dimensions={0} | all-to-all | bytes 8388608 | tf_op jit(solution)/shard_map/all_to_all | solution.py:517
  648.5 13.2 %blur.3 = f32[16,2,8,2,2,8,128]{6,5,4,3,2,1,0:T(8,128)S(1)} custom-call(f32[16,2,8,2,2,8,128]{6,5,4,3,2,1,0:T(8,128)S(1)} %bitcast.17, f32[16,2,8,2,2,8,128]{6,5,4,3,2,1,0:T(8,128)S(1)} %bitcast.13, bf16[2,2,256,512]{3,2,1,0:T(8,128)(2,1)S(1)} %copy-done.12, bf16[2,256,256]{2,1,0:T(8,128)(2,1)S(1)} %copy-done.15, bf16[2,256,256]{2,1,0:T(8,128)(2,1)S(1)} %copy-done.17, ...), custom_call_target="tpu_custom_call" | custom-call | flops 9663676416 | bytes 15204352 | tf_op jit(solution)/shard_map/blur/pallas_call | solution.py:504
  661.7 97.2 %all_to_all.50.got_ref = f32[32,8,2,2,8,128]{5,4,3,2,1,0:T(8,128)S(1)} all-to-all(f32[32,8,2,2,8,128]{5,4,3,2,1,0:T(8,128)S(1)} %bitcast.18), channel_id=1, replica_groups=mesh['gz'=16,'gy'=2] {'gz','gy'}, dimensions={0} | all-to-all | bytes 8388608 | tf_op jit(solution)/shard_map/all_to_all | solution.py:517
  758.8 9.2 ratio.3
  768.0 0.0 copy-start.13
  768.0 97.2 %all_to_all.51 = f32[32,8,2,2,8,128]{5,4,3,2,1,0:T(8,128)S(1)} all-to-all(f32[32,8,2,2,8,128]{5,4,3,2,1,0:T(8,128)S(1)} %ratio.3), channel_id=1, replica_groups=mesh['gz'=16,'gy'=2] {'gz','gy'}, dimensions={0} | all-to-all | bytes 8388608 | tf_op jit(solution)/shard_map/all_to_all | solution.py:517
  865.2 0.0 copy-done.13
  865.2 16.5 %adjoint.3 = f32[16,2,8,2,2,8,128]{6,5,4,3,2,1,0:T(8,128)S(1)} custom-call(f32[16,2,8,2,2,8,128]{6,5,4,3,2,1,0:T(8,128)S(1)} %bitcast.15, f32[16,2,8,2,2,8,128]{6,5,4,3,2,1,0:T(8,128)S(1)} %bitcast.14, bf16[2,2,256,512]{3,2,1,0:T(8,128)(2,1)S(1)} %copy-done.13, bf16[2,256,256]{2,1,0:T(8,128)(2,1)S(1)} %copy-done.15, bf16[2,256,256]{2,1,0:T(8,128)(2,1)S(1)} %copy-done.16, ...), custom_call_target="tpu_custom_call" | custom-call | flops 9663676416 | bytes 16252928 | tf_op jit(solution)/shard_map/adjoint/pallas_call | solution.py:504
  881.7 97.2 %all_to_all.52.got_ref = f32[32,8,2,2,8,128]{5,4,3,2,1,0:T(8,128)S(1)} all-to-all(f32[32,8,2,2,8,128]{5,4,3,2,1,0:T(8,128)S(1)} %bitcast.16), channel_id=1, replica_groups=mesh['gz'=16,'gy'=2] {'gz','gy'}, dimensions={0} | all-to-all | bytes 8388608 | tf_op jit(solution)/shard_map/all_to_all | solution.py:517
  978.9 7.4 last.1
Async XLA Ops:
  0.0 2.2 copy-start
  2.2 1.0 copy-start.4
  8.0 2.0 copy-start.2
  10.1 7.4 copy-start.6
  10.1 7.4 copy-start.10
  10.1 101.2 %all-to-all-start = ((f32[32,8,2,2,8,128]{5,4,3,2,1,0:T(8,128)}), f32[32,8,2,2,8,128]{5,4,3,2,1,0:T(8,128)}, u32[]{:S(2)}, u32[]{:S(2)}) async-start(f32[32,8,2,2,8,128]{5,4,3,2,1,0:T(8,128)} %copy-done.2), calls=%async_computation | async-start | bytes 8388608 | tf_op jit(solution)/shard_map/all_to_all | solution.py:517
  17.5 1.6 copy-start.7
  23.8 2.0 copy-start.3
  111.2 98.4 %copy-start.12 = (bf16[2,2,256,512]{3,2,1,0:T(8,128)(2,1)S(1)}, bf16[2,2,256,512]{3,2,1,0:T(8,128)(2,1)}, u32[]{:S(2)}) copy-start(bf16[2,2,256,512]{3,2,1,0:T(8,128)(2,1)} %constant.23.clone.ya_ref) | copy-start | bytes 3145732
  111.2 98.4 %copy-start.14 = (bf16[2,2,256,512]{3,2,1,0:T(8,128)(2,1)S(1)}, bf16[2,2,256,512]{3,2,1,0:T(8,128)(2,1)}, u32[]{:S(2)}) copy-start(bf16[2,2,256,512]{3,2,1,0:T(8,128)(2,1)} %constant.24.clone.yb_ref) | copy-start | bytes 3145732
  111.2 98.4 %copy-start.15 = (bf16[2,256,256]{2,1,0:T(8,128)(2,1)S(1)}, bf16[2,256,256]{2,1,0:T(8,128)(2,1)}, u32[]{:S(2)}) copy-start(bf16[2,256,256]{2,1,0:T(8,128)(2,1)} %constant.26.clone.za_ref) | copy-start | bytes 786436
  111.2 98.4 %copy-start.17 = (bf16[2,256,256]{2,1,0:T(8,128)(2,1)S(1)}, bf16[2,256,256]{2,1,0:T(8,128)(2,1)}, u32[]{:S(2)}) copy-start(bf16[2,256,256]{2,1,0:T(8,128)(2,1)} %constant.27.clone.zb_ref) | copy-start | bytes 786436
  223.7 97.2 %copy-start.1 = (f32[8,256,512]{2,1,0:T(8,128)S(1)}, f32[8,256,512]{2,1,0:T(8,128)}, u32[]{:S(2)}) copy-start(f32[8,256,512]{2,1,0:T(8,128)} %measured_ref.3) | copy-start | bytes 12582916
  223.7 97.2 %copy-start.5 = (bf16[2,2,256,256]{3,2,1,0:T(8,128)(2,1)S(1)}, bf16[2,2,256,256]{3,2,1,0:T(8,128)(2,1)}, u32[]{:S(2)}) copy-start(bf16[2,2,256,256]{3,2,1,0:T(8,128)(2,1)} %constant.20.clone.xa_ref) | copy-start | bytes 1572868
  223.7 97.2 %copy-start.8 = (bf16[2,2,256,256]{3,2,1,0:T(8,128)(2,1)S(1)}, bf16[2,2,256,256]{3,2,1,0:T(8,128)(2,1)}, u32[]{:S(2)}) copy-start(bf16[2,2,256,256]{3,2,1,0:T(8,128)(2,1)} %constant.21.clone.xb_ref) | copy-start | bytes 1572868
  330.1 97.2 %copy-start.11 = (bf16[2,512,1024]{2,1,0:T(8,128)(2,1)S(1)}, bf16[2,512,1024]{2,1,0:T(8,128)(2,1)}, u32[]{:S(2)}) copy-start(bf16[2,512,1024]{2,1,0:T(8,128)(2,1)} %constant.25.clone.yb_ref) | copy-start | bytes 6291460
  330.1 97.2 %copy-start.16 = (bf16[2,256,256]{2,1,0:T(8,128)(2,1)S(1)}, bf16[2,256,256]{2,1,0:T(8,128)(2,1)}, u32[]{:S(2)}) copy-start(bf16[2,256,256]{2,1,0:T(8,128)(2,1)} %constant.28.clone.zb_ref) | copy-start | bytes 786436
  443.8 97.2 %copy-start.9 = (bf16[2,512,512]{2,1,0:T(8,128)(2,1)S(1)}, bf16[2,512,512]{2,1,0:T(8,128)(2,1)}, u32[]{:S(2)}) copy-start(bf16[2,512,512]{2,1,0:T(8,128)(2,1)} %constant.22.clone.xb_ref) | copy-start | bytes 3145732
  768.0 97.2 %copy-start.13 = (bf16[2,2,256,512]{3,2,1,0:T(8,128)(2,1)S(1)}, bf16[2,2,256,512]{3,2,1,0:T(8,128)(2,1)}, u32[]{:S(2)}) copy-start(bf16[2,2,256,512]{3,2,1,0:T(8,128)(2,1)} %constant.23.clone.ya_ref) | copy-start | bytes 3145732

commit v4 on v3

--- a/solution.py
+++ b/solution.py
@@ -264,6 +264,11 @@
     return two_terms(ahead), two_terms(sharp), two_terms(soft)
 
 
+def parity_pick(length):
+    order = np.concatenate((np.arange(0, length, 2), np.arange(1, length, 2)))
+    return np.eye(length, dtype=np.float32)[:, order].astype(jnp.bfloat16)
+
+
 def dot(left, right):
     return jnp.dot(left, right, preferred_element_type=jnp.float32)
 
@@ -301,106 +306,124 @@
     return times_table(values.T, high, low)
 
 
-def load_lines(got_ref):
-    kx_len = got_ref.shape[0] * got_ref.shape[1]
-    z_len = got_ref.shape[4]
-    flat = got_ref.reshape(kx_len * 2 * z_len, LANES)
-    parities = []
-    for odd in range(2):
-        parts = []
-        for part in range(2):
-            pieces = [
-                flat[pl.ds((odd * 2 + part) * z_len + z, kx_len // 2, 4 * z_len), :]
-                for z in range(z_len)
-            ]
-            parts.append(jnp.concatenate(pieces, axis=1))
-        parities.append(jnp.concatenate(parts, axis=0))
-    return parities
-
-
-def store_lines(send_ref, odd, values):
-    kx_len = send_ref.shape[0] * send_ref.shape[1]
-    z_len = send_ref.shape[4]
-    flat = send_ref.reshape(kx_len * 2 * z_len, LANES)
-    half = kx_len // 2
+def swapped(blocks):
+    row = lax.broadcasted_iota(jnp.int32, blocks[0].shape, 1)
+    blocks = list(blocks)
+    for step in (1, 2, 4):
+        upper = (row & step) == 0
+        for i in range(SUBLANES):
+            if i & step == 0:
+                a, b = blocks[i], blocks[i + step]
+                blocks[i] = jnp.where(upper, a, pltpu.roll(b, step, 1))
+                blocks[i + step] = jnp.where(upper, pltpu.roll(a, SUBLANES - step, 1), b)
+    return blocks
+
+
+def load_lines(got_ref, tile):
+    half = got_ref.shape[0] * got_ref.shape[1] // 2
+    parts = []
     for part in range(2):
-        for z in range(z_len):
-            flat[pl.ds((odd * 2 + part) * z_len + z, half, 4 * z_len), :] = values[
-                part * half : (part + 1) * half, z * LANES : (z + 1) * LANES
-            ]
-
-
-def lines_back_sharp(got_ref, x_ref):
-    even, odd = load_lines(got_ref)
+        blocks = swapped([got_ref[:, i, part, tile] for i in range(SUBLANES)])
+        parts.append(jnp.concatenate([b.reshape(-1, LANES) for b in blocks], axis=1))
+    return [
+        jnp.concatenate([p[odd * half : (odd + 1) * half] for p in parts], axis=0)
+        for odd in range(2)
+    ]
+
+
+def store_lines(send_ref, tile, parities):
+    devs = send_ref.shape[0]
+    half = devs * send_ref.shape[1] // 2
+    for part in range(2):
+        values = jnp.concatenate([p[part * half : (part + 1) * half] for p in parities], axis=0)
+        blocks = [
+            values[:, z * LANES : (z + 1) * LANES].reshape(devs, SUBLANES, LANES)
+            for z in range(SUBLANES)
+        ]
+        for i, block in enumerate(swapped(blocks)):
+            send_ref[:, i, part, tile] = block
+
+
+def lines_back_sharp(got_ref, tile, x_ref):
+    even, odd = load_lines(got_ref, tile)
     even = lines_of(even, x_ref[0, 0], x_ref[1, 0])
     odd = lines_of(odd, x_ref[0, 1], x_ref[1, 1])
     return even + odd, even - odd
 
 
-def lines_back_soft(got_ref, x_ref):
-    both = lines_of(jnp.concatenate(load_lines(got_ref), axis=0), x_ref[0], x_ref[1])
+def lines_back_soft(got_ref, tile, x_ref):
+    both = lines_of(jnp.concatenate(load_lines(got_ref, tile), axis=0), x_ref[0], x_ref[1])
     half = both.shape[1] // 2
     return both[:, :half], both[:, half:]
 
 
-def lines_ahead(left, right, send_ref, x_ref):
-    store_lines(send_ref, 0, table_times_lines(x_ref[0, 0], x_ref[1, 0], left + right))
-    store_lines(send_ref, 1, table_times_lines(x_ref[0, 1], x_ref[1, 1], left - right))
-
-
-def halves(volume_ref):
+def lines_ahead(left, right, send_ref, tile, x_ref):
+    even = table_times_lines(x_ref[0, 0], x_ref[1, 0], left + right)
+    odd = table_times_lines(x_ref[0, 1], x_ref[1, 1], left - right)
+    store_lines(send_ref, tile, (even, odd))
+
+
+def halves(volume_ref, tile):
     half = volume_ref.shape[2] // 2
+    rows = slice(tile * LANES, (tile + 1) * LANES)
     return (
-        volume_ref[:, :, :half].reshape(-1, half),
-        volume_ref[:, :, half:].reshape(-1, half),
-    )
-
-
-def store_halves(volume_ref, left, right):
+        volume_ref[:, rows, :half].reshape(-1, half),
+        volume_ref[:, rows, half:].reshape(-1, half),
+    )
+
+
+def store_halves(volume_ref, tile, left, right):
     half = volume_ref.shape[2] // 2
-    shape = (*volume_ref.shape[:2], half)
-    volume_ref[:, :, :half] = left.reshape(shape)
-    volume_ref[:, :, half:] = right.reshape(shape)
+    rows = slice(tile * LANES, (tile + 1) * LANES)
+    shape = (volume_ref.shape[0], LANES, half)
+    volume_ref[:, rows, :half] = left.reshape(shape)
+    volume_ref[:, rows, half:] = right.reshape(shape)
 
 
 def first_kernel(volume_ref, xa_ref, send_ref):
-    left, right = halves(volume_ref)
-    lines_ahead(left, right, send_ref, xa_ref)
+    for tile in range(send_ref.shape[3]):
+        left, right = halves(volume_ref, tile)
+        lines_ahead(left, right, send_ref, tile, xa_ref)
 
 
 def ratio_kernel(got_ref, measured_ref, xb_ref, xa_ref, send_ref):
-    left, right = lines_back_sharp(got_ref, xb_ref)
-    over_left, over_right = halves(measured_ref)
-    left = over_left / jnp.maximum(left, FLOOR)
-    right = over_right / jnp.maximum(right, FLOOR)
-    lines_ahead(left, right, send_ref, xa_ref)
+    for tile in range(got_ref.shape[3]):
+        left, right = lines_back_sharp(got_ref, tile, xb_ref)
+        over_left, over_right = halves(measured_ref, tile)
+        left = over_left / jnp.maximum(left, FLOOR)
+        right = over_right / jnp.maximum(right, FLOOR)
+        lines_ahead(left, right, send_ref, tile, xa_ref)
 
 
 def correct_kernel(got_ref, estimate_ref, xb_ref, xa_ref, send_ref, out_ref):
-    left, right = lines_back_soft(got_ref, xb_ref)
-    old_left, old_right = halves(estimate_ref)
-    left, right = old_left * left, old_right * right
-    store_halves(out_ref, left, right)
-    lines_ahead(left, right, send_ref, xa_ref)
+    for tile in range(got_ref.shape[3]):
+        left, right = lines_back_soft(got_ref, tile, xb_ref)
+        old_left, old_right = halves(estimate_ref, tile)
+        left, right = old_left * left, old_right * right
+        store_halves(out_ref, tile, left, right)
+        lines_ahead(left, right, send_ref, tile, xa_ref)
 
 
 def last_kernel(got_ref, estimate_ref, xb_ref, out_ref):
-    left, right = lines_back_soft(got_ref, xb_ref)
-    old_left, old_right = halves(estimate_ref)
-    store_halves(out_ref, old_left * left, old_right * right)
-
-
-def arrange_kernel(real_ref, imag_ref, pick_ref, send_ref):
+    for tile in range(got_ref.shape[3]):
+        left, right = lines_back_soft(got_ref, tile, xb_ref)
+        old_left, old_right = halves(estimate_ref, tile)
+        store_halves(out_ref, tile, old_left * left, old_right * right)
+
+
+def picked(values, pick):
+    first, second = split_terms(values)
+    rest = values - first.astype(jnp.float32) - second.astype(jnp.float32)
+    return dot(first, pick) + dot(second, pick) + dot(rest.astype(jnp.bfloat16), pick)
+
+
+def arrange_kernel(real_ref, imag_ref, pick_x_ref, pick_y_ref, send_ref):
     z_len, _, kx_len = real_ref.shape
     tiles = send_ref.shape[2]
     flat = send_ref.reshape(kx_len * 2 * tiles * z_len, LANES)
     for part, ref in enumerate((real_ref, imag_ref)):
         for z in range(z_len):
-            values = ref[z].T
-            first, second = split_terms(values)
-            rest = values - first.astype(jnp.float32) - second.astype(jnp.float32)
-            pick = pick_ref[...]
-            values = dot(first, pick) + dot(second, pick) + dot(rest.astype(jnp.bfloat16), pick)
+            values = picked(picked(ref[z], pick_x_ref[...]).T, pick_y_ref[...])
             for tile in range(tiles):
                 start = (part * tiles + tile) * z_len + z
                 flat[pl.ds(start, kx_len, 2 * tiles * z_len), :] = values[
@@ -431,8 +454,16 @@
     )
 
 
-def gain_kernel(adjoint, got_ref, gain_ref, ya_ref, za_ref, zb_ref, yb_ref, send_ref):
-    z_devs, y_devs, share, _, tiles, z_local, _ = got_ref.shape
+def gain_kernel(adjoint, at_once, got_ref, *refs):
+    @pl.loop(0, got_ref.shape[2] // at_once)
+    def _(step):
+        gain_planes(adjoint, at_once, step * at_once, got_ref, *refs)
+
+
+def gain_planes(
+    adjoint, share, base, got_ref, gain_ref, ya_ref, za_ref, zb_ref, yb_ref, send_ref
+):
+    z_devs, y_devs, _, _, tiles, z_local, _ = got_ref.shape
     rows = 2 * z_devs * z_local
     half = y_devs * tiles * LANES // 2
 
@@ -440,7 +471,7 @@
         return [values[k * rows : (k + 1) * rows] for k in range(share)]
 
     values = jnp.concatenate(
-        [plane_of(got_ref, k, part, range(tiles)) for k in range(share) for part in range(2)],
+        [plane_of(got_ref, base + k, part, range(tiles)) for k in range(share) for part in range(2)],
         axis=0,
     )
     left, right = values[:, :half], values[:, half:]
@@ -457,8 +488,8 @@
         gain_real, gain_imag = [
             jnp.concatenate(
                 (
-                    plane_of(gain_ref, k, part, range(tiles // 2)),
-                    plane_of(gain_ref, k, part, range(tiles // 2, tiles)),
+                    plane_of(gain_ref, base + k, part, range(tiles // 2)),
+                    plane_of(gain_ref, base + k, part, range(tiles // 2, tiles)),
                 ),
                 axis=1,
             )
@@ -485,32 +516,28 @@
             for g in range(y_devs):
                 for tile in range(tiles):
                     low = (g * tiles + tile) * LANES
-                    send_ref[:, g, k, part, tile] = parts[part][:, low : low + LANES].reshape(
+                    send_ref[:, g, base + k, part, tile] = parts[part][:, low : low + LANES].reshape(
                         z_devs, z_local, LANES
                     )
 
 
-KX_AT_ONCE = 2
+KX_AT_ONCE = 4
 VMEM_BYTES = 32 * 2**20
 
 
-def whole(table):
-    return pl.BlockSpec(table.shape, lambda *_: (0,) * table.ndim)
-
-
-def call(kernel, grid, arrays, specs, tables, outs, out_specs, flops, name):
-    leaves = (*arrays, *tables, *jax.tree.leaves(outs))
+def call(kernel, arrays, outs, flops, name):
+    leaves = (*arrays, *jax.tree.leaves(outs))
     moved = sum(math.prod(a.shape) * a.dtype.itemsize for a in leaves)
+    spec = pl.BlockSpec(memory_space=pltpu.VMEM)
     return pl.pallas_call(
         kernel,
-        grid=grid,
-        in_specs=list(specs) + [whole(t) for t in tables],
-        out_specs=out_specs,
+        in_specs=[spec] * len(arrays),
+        out_specs=jax.tree.map(lambda _: spec, outs),
         out_shape=outs,
         compiler_params=pltpu.CompilerParams(vmem_limit_bytes=VMEM_BYTES),
         cost_estimate=pl.CostEstimate(flops=flops, bytes_accessed=moved, transcendentals=0),
         name=name,
-    )(*arrays, *tables)
+    )(*arrays)
 
 
 def exchange(values):
@@ -526,63 +553,43 @@
     xa, xb, xs = (jnp.asarray(t) for t in x_tables(x_len))
     ya, yb, ys = (jnp.asarray(t) for t in y_tables(y_len))
     za, zb, zs = (jnp.asarray(t) for t in z_tables(z_len))
-    picked = np.concatenate((np.arange(0, y_local, 2), np.arange(1, y_local, 2)))
-    pick = jnp.asarray(np.eye(y_local, dtype=np.float32)[:, picked].astype(jnp.bfloat16))
+    pick_x, pick_y = (jnp.asarray(parity_pick(n)) for n in (kx_len, y_local))
 
     spectrum = jax.ShapeDtypeStruct((devs, share, 2, tiles, z_local, LANES), jnp.float32)
     volume = jax.ShapeDtypeStruct(measured.shape, jnp.float32)
-    lines_spec = pl.BlockSpec(
-        (devs, share, 2, 1, z_local, LANES), lambda t: (0, 0, 0, t, 0, 0)
-    )
-    volume_spec = pl.BlockSpec((z_local, LANES, x_len), lambda t: (0, t, 0))
     line_flops = 3 * z_local * y_local * x_len * x_len
 
     def first(values):
-        return call(
-            first_kernel, (tiles,), (values,), (volume_spec,), (xa,),
-            spectrum, lines_spec, line_flops, "first",
-        )
+        return call(first_kernel, (values, xa), spectrum, line_flops, "first")
 
     def ratio(got, values):
-        return call(
-            ratio_kernel, (tiles,), (got, values), (lines_spec, volume_spec), (xb, xa),
-            spectrum, lines_spec, 2 * line_flops, "ratio",
-        )
+        return call(ratio_kernel, (got, values, xb, xa), spectrum, 2 * line_flops, "ratio")
 
     def correct(got, values):
         return call(
-            correct_kernel, (tiles,), (got, values), (lines_spec, volume_spec), (xs, xa),
-            (spectrum, volume), (lines_spec, volume_spec), 3 * line_flops, "correct",
+            correct_kernel, (got, values, xs, xa), (spectrum, volume), 3 * line_flops, "correct"
         )
 
     def last(got, values):
-        return call(
-            last_kernel, (tiles,), (got, values), (lines_spec, volume_spec), (xs,),
-            volume, volume_spec, 2 * line_flops, "last",
-        )
+        return call(last_kernel, (got, values, xs), volume, 2 * line_flops, "last")
 
     planes = (z_devs, y_devs, *spectrum.shape[1:])
     at_once = KX_AT_ONCE if share % KX_AT_ONCE == 0 else 1
-    plane_spec = pl.BlockSpec(
-        (z_devs, y_devs, at_once, 2, tiles, z_local, LANES), lambda k: (0, 0, k, 0, 0, 0, 0)
-    )
 
     def filtered(got, gains, adjoint):
         return call(
-            functools.partial(gain_kernel, adjoint), (share // at_once,),
-            (got.reshape(planes), gains.reshape(planes)), (plane_spec, plane_spec),
-            (ya, za, zs, ys) if adjoint else (ya, za, zb, yb),
-            jax.ShapeDtypeStruct(planes, jnp.float32), plane_spec,
-            3 * 8 * share * z_len * y_len * (2 * z_len + y_len), "adjoint" if adjoint else "blur",
+            functools.partial(gain_kernel, adjoint, at_once),
+            (got.reshape(planes), gains.reshape(planes), ya, za, *((zs, ys) if adjoint else (zb, yb))),
+            jax.ShapeDtypeStruct(planes, jnp.float32),
+            3 * 8 * share * z_len * y_len * (2 * z_len + y_len),
+            "adjoint" if adjoint else "blur",
         ).reshape(spectrum.shape)
 
     def arranged(transfer_real, transfer_imag):
-        in_spec = pl.BlockSpec((z_local, y_local, LANES), lambda k: (0, 0, k))
-        out_spec = pl.BlockSpec((LANES, 2, tiles, z_local, LANES), lambda k: (k, 0, 0, 0, 0))
         return call(
-            arrange_kernel, (kx_len // LANES,), (transfer_real, transfer_imag), (in_spec, in_spec),
-            (pick,), jax.ShapeDtypeStruct((kx_len, *spectrum.shape[2:]), jnp.float32), out_spec,
-            3 * 4 * z_local * y_local * y_local * kx_len, "arrange",
+            arrange_kernel, (transfer_real, transfer_imag, pick_x, pick_y),
+            jax.ShapeDtypeStruct((kx_len, *spectrum.shape[2:]), jnp.float32),
+            3 * 4 * z_local * y_local * kx_len * (y_local + kx_len), "arrange",
         ).reshape(spectrum.shape)
 
     send = first(measured)
@@ -609,7 +616,7 @@
         and z_len // z_devs == SUBLANES
         and y_len % (2 * LANES * y_devs) == 0
         and x_len % (4 * LANES) == 0
-        and x_len // 2 % (z_devs * y_devs) == 0
+        and x_len // 2 == SUBLANES * z_devs * y_devs
     )
 
 

time: 987 us -> 974 us (0.987)
  Pallas kernels: 106 us -> 87.2 us
    pallas_call x10, Pallas kernels: 106 us -> 87.2 us  [call(): pl.pallas_call(kernel, in_specs=[spec] * len(arrays), out_specs=jax.tree....]
  transfers between devices with their start and end apart: 1 -> 1, of which waited for: 1 -> 1; matrix products, arithmetic and copies ran while one was open for 0% -> 0% of each run, Pallas kernels for 0% -> 1%
where the time goes in v4:
time: 974 us; the launch traced here: 968 us
  blocking collectives  780 us (80%)
  Pallas kernels  87.2 us (9%)
  waiting for transfers between devices  84.1 us (9%)
    all_to_all x8, blocking collectives, exchange(): lax.all_to_all(values, ('gz', 'gy'), split_axis=0, concat_axis=0, tiled=T...  780 us
    pallas_call x10, Pallas kernels, call(): pl.pallas_call(kernel, in_specs=[spec] * len(arrays), out_specs=jax.tree....  87.2 us
    all_to_all x1, waiting for transfers between devices, exchange(): lax.all_to_all(values, ('gz', 'gy'), split_axis=0, concat_axis=0, tiled=T...  84.1 us
  transfers between devices with their start and end apart: 1, of which 1 were waited for; matrix products, arithmetic and copies ran while one was open for 0% of the time, Pallas kernels for 1%

profile of v4, /device:TPU:0, one launch (start us, length us, event | category | flops | bytes accessed | tf_op | source)
XLA Modules:
  0.0 967.6 jit_solution(9940192398908766608)
XLA Ops:
  0.0 0.0 copy-start
  0.0 2.2 copy-done
  2.2 0.0 copy-start.3
  2.2 1.0 copy-done.3
  3.2 2.4 first.1
  5.6 0.0 copy-start.2
  5.6 2.0 copy-done.2
  7.6 0.0 copy-start.8
  7.6 0.0 copy-start.16
  7.6 7.4 all-to-all-start
  15.1 0.0 copy-done.8
  15.1 0.0 copy-done.16
  15.1 0.0 copy-start.9
  15.1 1.6 copy-done.9
  16.7 6.0 arrange.1
  22.7 0.0 copy-start.5
  22.7 2.0 copy-done.5
  24.7 84.1 %all-to-all-done = f32[32,8,2,2,8,128]{5,4,3,2,1,0:T(8,128)} async-done(((f32[32,8,2,2,8,128]{5,4,3,2,1,0:T(8,128)}), f32[32,8,2,2,8,128]{5,4,3,2,1,0:T(8,128)}, u32[]{:S(2)}, u32[]{:S(2)}) %all-to-all-start) | async-done | bytes 4194336 | tf_op jit(solution)/shard_map/all_to_all | solution.py:544
  108.8 0.0 copy-start.11
  108.8 0.0 copy-start.12
  108.8 0.0 copy-start.13
  108.8 0.0 copy-start.15
  108.8 98.6 %all_to_all.45 = f32[32,8,2,2,8,128]{5,4,3,2,1,0:T(8,128)S(1)} all-to-all(f32[32,8,2,2,8,128]{5,4,3,2,1,0:T(8,128)} %bitcast.14), channel_id=1, replica_groups=mesh['gz'=16,'gy'=2] {'gz','gy'}, dimensions={0} | all-to-all | bytes 8388608 | tf_op jit(solution)/shard_map/all_to_all | solution.py:544
  207.4 0.0 copy-done.11
  207.4 0.0 copy-done.12
  207.4 0.0 copy-done.13
  207.4 0.0 copy-done.15
  207.4 13.8 %blur.2 = f32[16,2,8,2,2,8,128]{6,5,4,3,2,1,0:T(8,128)S(1)} custom-call(f32[16,2,8,2,2,8,128]{6,5,4,3,2,1,0:T(8,128)} %bitcast.got_ref, f32[16,2,8,2,2,8,128]{6,5,4,3,2,1,0:T(8,128)S(1)} %bitcast.10, bf16[2,2,256,512]{3,2,1,0:T(8,128)(2,1)S(1)} %copy-done.11, bf16[2,256,256]{2,1,0:T(8,128)(2,1)S(1)} %copy-done.13, bf16[2,256,256]{2,1,0:T(8,128)(2,1)S(1)} %copy-done.15, ...), custom_call_target="tpu_custom_call" | custom-call | flops 9663676416 | bytes 15204352 | tf_op jit(solution)/shard_map/blur/pallas_call | solution.py:532
  221.2 0.0 copy-start.1
  221.2 0.0 copy-start.4
  221.3 0.0 copy-start.6
  221.3 97.2 %all_to_all.46.got_ref = f32[32,8,2,2,8,128]{5,4,3,2,1,0:T(8,128)S(1)} all-to-all(f32[32,8,2,2,8,128]{5,4,3,2,1,0:T(8,128)S(1)} %bitcast.19), channel_id=1, replica_groups=mesh['gz'=16,'gy'=2] {'gz','gy'}, dimensions={0} | all-to-all | bytes 8388608 | tf_op jit(solution)/shard_map/all_to_all | solution.py:544
  318.5 0.0 copy-done.1
  318.5 0.0 copy-done.4
  318.5 0.0 copy-done.6
  318.5 5.8 ratio.2
  324.3 0.0 copy-start.10
  324.3 0.0 copy-start.14
  324.3 97.4 %all_to_all.47 = f32[32,8,2,2,8,128]{5,4,3,2,1,0:T(8,128)S(1)} all-to-all(f32[32,8,2,2,8,128]{5,4,3,2,1,0:T(8,128)S(1)} %ratio.2), channel_id=1, replica_groups=mesh['gz'=16,'gy'=2] {'gz','gy'}, dimensions={0} | all-to-all | bytes 8388608 | tf_op jit(solution)/shard_map/all_to_all | solution.py:544
  421.7 0.0 copy-done.10
  421.7 0.0 copy-done.14
  421.7 14.9 %adjoint.2 = f32[16,2,8,2,2,8,128]{6,5,4,3,2,1,0:T(8,128)S(1)} custom-call(f32[16,2,8,2,2,8,128]{6,5,4,3,2,1,0:T(8,128)S(1)} %bitcast.20, f32[16,2,8,2,2,8,128]{6,5,4,3,2,1,0:T(8,128)S(1)} %bitcast.11, bf16[2,2,256,512]{3,2,1,0:T(8,128)(2,1)S(1)} %copy-done.11, bf16[2,256,256]{2,1,0:T(8,128)(2,1)S(1)} %copy-done.13, bf16[2,256,256]{2,1,0:T(8,128)(2,1)S(1)} %copy-done.14, ...), custom_call_target="tpu_custom_call" | custom-call | flops 9663676416 | bytes 16252928 | tf_op jit(solution)/shard_map/adjoint/pallas_call | solution.py:532
  436.5 0.0 copy-start.7
  436.6 97.2 %all_to_all.48.got_ref = f32[32,8,2,2,8,128]{5,4,3,2,1,0:T(8,128)S(1)} all-to-all(f32[32,8,2,2,8,128]{5,4,3,2,1,0:T(8,128)S(1)} %bitcast.21), channel_id=1, replica_groups=mesh['gz'=16,'gy'=2] {'gz','gy'}, dimensions={0} | all-to-all | bytes 8388608 | tf_op jit(solution)/shard_map/all_to_all | solution.py:544
  533.7 0.0 copy-done.7
  533.7 6.0 correct.1
  539.8 97.6 %all_to_all.49 = f32[32,8,2,2,8,128]{5,4,3,2,1,0:T(8,128)S(1)} all-to-all(f32[32,8,2,2,8,128]{5,4,3,2,1,0:T(8,128)S(1)} %get-tuple-element.13), channel_id=1, replica_groups=mesh['gz'=16,'gy'=2] {'gz','gy'}, dimensions={0} | all-to-all | bytes 8388608 | tf_op jit(solution)/shard_map/all_to_all | solution.py:544
  637.3 11.6 %blur.3 = f32[16,2,8,2,2,8,128]{6,5,4,3,2,1,0:T(8,128)S(1)} custom-call(f32[16,2,8,2,2,8,128]{6,5,4,3,2,1,0:T(8,128)S(1)} %bitcast.17, f32[16,2,8,2,2,8,128]{6,5,4,3,2,1,0:T(8,128)S(1)} %bitcast.12, bf16[2,2,256,512]{3,2,1,0:T(8,128)(2,1)S(1)} %copy-done.11, bf16[2,256,256]{2,1,0:T(8,128)(2,1)S(1)} %copy-done.13, bf16[2,256,256]{2,1,0:T(8,128)(2,1)S(1)} %copy-done.15, ...), custom_call_target="tpu_custom_call" | custom-call | flops 9663676416 | bytes 15204352 | tf_op jit(solution)/shard_map/blur/pallas_call | solution.py:532
  649.0 97.2 %all_to_all.50.got_ref = f32[32,8,2,2,8,128]{5,4,3,2,1,0:T(8,128)S(1)} all-to-all(f32[32,8,2,2,8,128]{5,4,3,2,1,0:T(8,128)S(1)} %bitcast.18), channel_id=1, replica_groups=mesh['gz'=16,'gy'=2] {'gz','gy'}, dimensions={0} | all-to-all | bytes 8388608 | tf_op jit(solution)/shard_map/all_to_all | solution.py:544
  746.1 5.8 ratio.3
  752.0 97.3 %all_to_all.51 = f32[32,8,2,2,8,128]{5,4,3,2,1,0:T(8,128)S(1)} all-to-all(f32[32,8,2,2,8,128]{5,4,3,2,1,0:T(8,128)S(1)} %ratio.3), channel_id=1, replica_groups=mesh['gz'=16,'gy'=2] {'gz','gy'}, dimensions={0} | all-to-all | bytes 8388608 | tf_op jit(solution)/shard_map/all_to_all | solution.py:544
  849.3 14.8 %adjoint.3 = f32[16,2,8,2,2,8,128]{6,5,4,3,2,1,0:T(8,128)S(1)} custom-call(f32[16,2,8,2,2,8,128]{6,5,4,3,2,1,0:T(8,128)S(1)} %bitcast.15, f32[16,2,8,2,2,8,128]{6,5,4,3,2,1,0:T(8,128)S(1)} %bitcast.13, bf16[2,2,256,512]{3,2,1,0:T(8,128)(2,1)S(1)} %copy-done.11, bf16[2,256,256]{2,1,0:T(8,128)(2,1)S(1)} %copy-done.13, bf16[2,256,256]{2,1,0:T(8,128)(2,1)S(1)} %copy-done.14, ...), custom_call_target="tpu_custom_call" | custom-call | flops 9663676416 | bytes 16252928 | tf_op jit(solution)/shard_map/adjoint/pallas_call | solution.py:532
  864.2 97.2 %all_to_all.52.got_ref = f32[32,8,2,2,8,128]{5,4,3,2,1,0:T(8,128)S(1)} all-to-all(f32[32,8,2,2,8,128]{5,4,3,2,1,0:T(8,128)S(1)} %bitcast.16), channel_id=1, replica_groups=mesh['gz'=16,'gy'=2] {'gz','gy'}, dimensions={0} | all-to-all | bytes 8388608 | tf_op jit(solution)/shard_map/all_to_all | solution.py:544
  961.3 6.0 last.1
Async XLA Ops:
  0.0 2.2 copy-start
  2.2 1.0 copy-start.3
  5.6 2.0 copy-start.2
  7.6 7.4 copy-start.8
  7.6 7.4 copy-start.16
  7.6 101.2 %all-to-all-start = ((f32[32,8,2,2,8,128]{5,4,3,2,1,0:T(8,128)}), f32[32,8,2,2,8,128]{5,4,3,2,1,0:T(8,128)}, u32[]{:S(2)}, u32[]{:S(2)}) async-start(f32[32,8,2,2,8,128]{5,4,3,2,1,0:T(8,128)} %copy-done.2), calls=%async_computation | async-start | bytes 8388608 | tf_op jit(solution)/shard_map/all_to_all | solution.py:544
  15.1 1.6 copy-start.9
  22.7 2.0 copy-start.5
  108.8 98.6 %copy-start.11 = (bf16[2,2,256,512]{3,2,1,0:T(8,128)(2,1)S(1)}, bf16[2,2,256,512]{3,2,1,0:T(8,128)(2,1)}, u32[]{:S(2)}) copy-start(bf16[2,2,256,512]{3,2,1,0:T(8,128)(2,1)} %constant.23.clone.refs_1_) | copy-start | bytes 3145732
  108.8 98.6 %copy-start.12 = (bf16[2,2,256,512]{3,2,1,0:T(8,128)(2,1)S(1)}, bf16[2,2,256,512]{3,2,1,0:T(8,128)(2,1)}, u32[]{:S(2)}) copy-start(bf16[2,2,256,512]{3,2,1,0:T(8,128)(2,1)} %constant.24.clone.refs_4_) | copy-start | bytes 3145732
  108.8 98.6 %copy-start.13 = (bf16[2,256,256]{2,1,0:T(8,128)(2,1)S(1)}, bf16[2,256,256]{2,1,0:T(8,128)(2,1)}, u32[]{:S(2)}) copy-start(bf16[2,256,256]{2,1,0:T(8,128)(2,1)} %constant.26.clone.refs_2_) | copy-start | bytes 786436
  108.8 98.6 %copy-start.15 = (bf16[2,256,256]{2,1,0:T(8,128)(2,1)S(1)}, bf16[2,256,256]{2,1,0:T(8,128)(2,1)}, u32[]{:S(2)}) copy-start(bf16[2,256,256]{2,1,0:T(8,128)(2,1)} %constant.27.clone.refs_3_) | copy-start | bytes 786436
  221.2 97.2 %copy-start.1 = (f32[8,256,512]{2,1,0:T(8,128)S(1)}, f32[8,256,512]{2,1,0:T(8,128)}, u32[]{:S(2)}) copy-start(f32[8,256,512]{2,1,0:T(8,128)} %measured_ref.3) | copy-start | bytes 12582916
  221.2 97.2 %copy-start.4 = (bf16[2,2,256,256]{3,2,1,0:T(8,128)(2,1)S(1)}, bf16[2,2,256,256]{3,2,1,0:T(8,128)(2,1)}, u32[]{:S(2)}) copy-start(bf16[2,2,256,256]{3,2,1,0:T(8,128)(2,1)} %constant.20.clone.xa_ref) | copy-start | bytes 1572868
  221.3 97.2 %copy-start.6 = (bf16[2,2,256,256]{3,2,1,0:T(8,128)(2,1)S(1)}, bf16[2,2,256,256]{3,2,1,0:T(8,128)(2,1)}, u32[]{:S(2)}) copy-start(bf16[2,2,256,256]{3,2,1,0:T(8,128)(2,1)} %constant.21.clone.xb_ref) | copy-start | bytes 1572868
  324.3 97.4 %copy-start.10 = (bf16[2,512,1024]{2,1,0:T(8,128)(2,1)S(1)}, bf16[2,512,1024]{2,1,0:T(8,128)(2,1)}, u32[]{:S(2)}) copy-start(bf16[2,512,1024]{2,1,0:T(8,128)(2,1)} %constant.25.clone.refs_4_) | copy-start | bytes 6291460
  324.3 97.4 %copy-start.14 = (bf16[2,256,256]{2,1,0:T(8,128)(2,1)S(1)}, bf16[2,256,256]{2,1,0:T(8,128)(2,1)}, u32[]{:S(2)}) copy-start(bf16[2,256,256]{2,1,0:T(8,128)(2,1)} %constant.28.clone.refs_3_) | copy-start | bytes 786436
  436.5 97.2 %copy-start.7 = (bf16[2,512,512]{2,1,0:T(8,128)(2,1)S(1)}, bf16[2,512,512]{2,1,0:T(8,128)(2,1)}, u32[]{:S(2)}) copy-start(bf16[2,512,512]{2,1,0:T(8,128)(2,1)} %constant.22.clone.xb_ref) | copy-start | bytes 3145732

commit v5 on v4

--- a/solution.py
+++ b/solution.py
@@ -237,19 +237,35 @@
     return two_terms(np.stack(ahead)), two_terms(sharp), two_terms(soft)
 
 
+def y_order(length, rest):
+    quarter = length // 4
+    return 4 * ((np.arange(quarter) + (rest % 2) * (quarter // 2)) % quarter) + rest
+
+
 def y_tables(length):
-    half = length // 2
+    quarter = length // 4
     where = np.arange(length)
-    ahead, sharp, soft = [], [], []
-    for odd in range(2):
-        k = 2 * np.arange(half) + odd
-        angle = phase_np(where, k, length)
+    ahead, sharp, soft, edges = [], [], [], []
+    weights = gauss_weights_np()
+    for rest in range(4):
+        angle = phase_np(where, y_order(length, rest), length)
         cosine, sine = np.cos(angle), np.sin(angle)
-        ahead.append(np.concatenate((cosine[:half], sine[:half]), axis=1))
-        cosine, sine = cosine.T / length, sine.T / length
-        sharp.append(np.concatenate((cosine[:, :half], sine[:, :half]), axis=1))
-        soft.append(np.concatenate((smooth_np(cosine, 1), smooth_np(sine, 1)), axis=1))
-    return two_terms(np.stack(ahead)), two_terms(np.stack(sharp)), two_terms(np.concatenate(soft))
+        ahead.append(np.concatenate((cosine[:quarter], sine[:quarter]), axis=1))
+        exact, round_trip, edge = [], [], []
+        for table in (cosine.T / length, sine.T / length):
+            around = sum(
+                weights[j] * np.roll(table, RADIUS - j, axis=1) for j in range(2 * RADIUS + 1)
+            )
+            over = around - smooth_np(table, 1)
+            exact.append(table[:, :quarter])
+            round_trip.append(around[:, :quarter])
+            edge += [over[:, : quarter // 2], over[:, -(quarter // 2) :]]
+        sharp.append(np.concatenate(exact, axis=1))
+        soft.append(np.concatenate(round_trip, axis=1))
+        edges.append(np.concatenate(edge, axis=1))
+    return [two_terms(np.stack(t)) for t in (ahead, sharp, soft)] + [
+        two_terms(np.concatenate(edges))
+    ]
 
 
 def z_tables(length):
@@ -264,9 +280,18 @@
     return two_terms(ahead), two_terms(sharp), two_terms(soft)
 
 
-def parity_pick(length):
-    order = np.concatenate((np.arange(0, length, 2), np.arange(1, length, 2)))
-    return np.eye(length, dtype=np.float32)[:, order].astype(jnp.bfloat16)
+def pick_of(order):
+    return np.eye(len(order), dtype=np.float32)[:, np.asarray(order)].astype(jnp.bfloat16)
+
+
+def pick_x_table(length):
+    return pick_of(np.concatenate((np.arange(0, length, 2), np.arange(1, length, 2))))
+
+
+def pick_y_tables(length):
+    by_rest = [np.arange(rest, length, 4) for rest in range(4)]
+    orders = ((0, 1, 2, 3), (1, 0, 3, 2))
+    return np.stack([pick_of(np.concatenate([by_rest[r] for r in order])) for order in orders])
 
 
 def dot(left, right):
@@ -431,13 +456,6 @@
                 ]
 
 
-def plane_of(ref, k, part, tiles):
-    pieces = [
-        ref[:, g, k, part, tile].reshape(-1, LANES) for g in range(ref.shape[1]) for tile in tiles
-    ]
-    return jnp.concatenate(pieces, axis=1)
-
-
 def turned_ahead(both):
     rows, half = both.shape[0] // 2, both.shape[1] // 2
     return (
@@ -460,65 +478,88 @@
         gain_planes(adjoint, at_once, step * at_once, got_ref, *refs)
 
 
+def quarters_of(ref, k, part):
+    _, y_devs, _, _, tiles, _, _ = ref.shape
+    return [ref[:, g, k, part, t].reshape(-1, LANES) for g in range(y_devs) for t in range(tiles)]
+
+
+def gains_of(ref, k, part):
+    first, second, third, fourth = quarters_of(ref, k, part)
+    low = lax.broadcasted_iota(jnp.int32, first.shape, 1) < LANES // 2
+    pairs = ((first, third), (third, first), (second, fourth), (fourth, second))
+    return jnp.concatenate([jnp.where(low, a, b) for a, b in pairs], axis=1)
+
+
 def gain_planes(
-    adjoint, share, base, got_ref, gain_ref, ya_ref, za_ref, zb_ref, yb_ref, send_ref
+    adjoint, share, base, got_ref, gain_ref, ya_ref, za_ref, zb_ref, yb_ref, *rest_refs
 ):
+    send_ref = rest_refs[-1]
     z_devs, y_devs, _, _, tiles, z_local, _ = got_ref.shape
-    rows = 2 * z_devs * z_local
-    half = y_devs * tiles * LANES // 2
+    z_len = z_devs * z_local
+    rows = 2 * z_len
 
     def by_kx(values):
         return [values[k * rows : (k + 1) * rows] for k in range(share)]
 
-    values = jnp.concatenate(
-        [plane_of(got_ref, base + k, part, range(tiles)) for k in range(share) for part in range(2)],
-        axis=0,
-    )
-    left, right = values[:, :half], values[:, half:]
-    evens = by_kx(times_table(left + right, ya_ref[0, 0], ya_ref[1, 0]))
-    odds = by_kx(times_table(left - right, ya_ref[0, 1], ya_ref[1, 1]))
+    inputs = [[], [], [], []]
+    for k in range(share):
+        real, imag = (quarters_of(got_ref, base + k, part) for part in range(2))
+        even_real, even_imag = real[0] + real[2], imag[0] + imag[2]
+        odd_real, odd_imag = real[1] + real[3], imag[1] + imag[3]
+        inputs[0] += [even_real + odd_real, even_imag + odd_imag]
+        inputs[2] += [even_real - odd_real, even_imag - odd_imag]
+        even_real, even_imag = real[0] - real[2], imag[0] - imag[2]
+        odd_real, odd_imag = real[1] - real[3], imag[1] - imag[3]
+        inputs[1] += [even_real + odd_imag, even_imag - odd_real]
+        inputs[3] += [even_real - odd_imag, even_imag + odd_real]
+    turned = [
+        by_kx(times_table(jnp.concatenate(inputs[r], axis=0), ya_ref[0, r], ya_ref[1, r]))
+        for r in range(4)
+    ]
     planes = []
     for k in range(share):
-        even, odd = turned_ahead(evens[k]), turned_ahead(odds[k])
+        pairs = [turned_ahead(turned[r][k]) for r in range(4)]
         values = jnp.concatenate(
-            [jnp.concatenate((even[part], odd[part]), axis=1) for part in range(2)], axis=0
+            [jnp.concatenate([pair[part] for pair in pairs], axis=1) for part in range(2)], axis=0
         )
         values = table_times(za_ref[0], za_ref[1], values)
-        real, imag = values[: rows // 2], values[rows // 2 :]
-        gain_real, gain_imag = [
-            jnp.concatenate(
-                (
-                    plane_of(gain_ref, base + k, part, range(tiles // 2)),
-                    plane_of(gain_ref, base + k, part, range(tiles // 2, tiles)),
-                ),
-                axis=1,
-            )
-            for part in range(2)
-        ]
+        real, imag = values[:z_len], values[z_len:]
+        gain_real, gain_imag = (gains_of(gain_ref, base + k, part) for part in range(2))
         if adjoint:
-            turned = (real * gain_real + imag * gain_imag, imag * gain_real - real * gain_imag)
+            both = (real * gain_real + imag * gain_imag, imag * gain_real - real * gain_imag)
         else:
-            turned = (real * gain_real - imag * gain_imag, real * gain_imag + imag * gain_real)
-        planes.append(table_times(zb_ref[0], zb_ref[1], jnp.concatenate(turned, axis=0)))
+            both = (real * gain_real - imag * gain_imag, real * gain_imag + imag * gain_real)
+        planes.append(table_times(zb_ref[0], zb_ref[1], jnp.concatenate(both, axis=0)))
     values = jnp.concatenate(planes, axis=0)
+    turned = [
+        by_kx(times_table(values[:, r * LANES : (r + 1) * LANES], yb_ref[0, r], yb_ref[1, r]))
+        for r in range(4)
+    ]
     if adjoint:
-        boths = by_kx(times_table(values, yb_ref[0], yb_ref[1]))
-    else:
-        evens = by_kx(times_table(values[:, :half], yb_ref[0, 0], yb_ref[1, 0]))
-        odds = by_kx(times_table(values[:, half:], yb_ref[0, 1], yb_ref[1, 1]))
+        edge_ref = rest_refs[0]
+        edges = by_kx(times_table(values, edge_ref[0], edge_ref[1]))
     for k in range(share):
+        pairs = [turned_back(turned[r][k]) for r in range(4)]
+        even_real, even_imag = (pairs[0][part] + pairs[2][part] for part in range(2))
+        odd_real, odd_imag = (pairs[1][part] + pairs[3][part] for part in range(2))
+        outs = [None] * 4
+        outs[0] = [even_real + odd_real, even_imag + odd_imag]
+        outs[2] = [even_real - odd_real, even_imag - odd_imag]
+        even_real, even_imag = (pairs[0][part] - pairs[2][part] for part in range(2))
+        odd_real, odd_imag = (pairs[1][part] - pairs[3][part] for part in range(2))
+        outs[1] = [even_real - odd_imag, even_imag + odd_real]
+        outs[3] = [even_real + odd_imag, even_imag - odd_real]
         if adjoint:
-            parts = turned_back(boths[k])
-        else:
-            even, odd = turned_back(evens[k]), turned_back(odds[k])
-            parts = [jnp.concatenate((a + b, a - b), axis=1) for a, b in zip(even, odd)]
+            over = turned_back(edges[k])
+            low = lax.broadcasted_iota(jnp.int32, over[0].shape, 1) < LANES // 2
+            for part in range(2):
+                outs[0][part] = outs[0][part] - jnp.where(low, over[part], 0.0)
+                outs[3][part] = outs[3][part] - jnp.where(low, 0.0, over[part])
         for part in range(2):
-            for g in range(y_devs):
-                for tile in range(tiles):
-                    low = (g * tiles + tile) * LANES
-                    send_ref[:, g, base + k, part, tile] = parts[part][:, low : low + LANES].reshape(
-                        z_devs, z_local, LANES
-                    )
+            for j in range(4):
+                send_ref[:, j // tiles, base + k, part, j % tiles] = outs[j][part].reshape(
+                    z_devs, z_local, LANES
+                )
 
 
 KX_AT_ONCE = 4
@@ -551,9 +592,12 @@
     z_len, y_len, kx_len = z_local * z_devs, y_local * y_devs, x_len // 2
     tiles, share = y_local // LANES, kx_len // devs
     xa, xb, xs = (jnp.asarray(t) for t in x_tables(x_len))
-    ya, yb, ys = (jnp.asarray(t) for t in y_tables(y_len))
+    ya, yb, ys, edges = (jnp.asarray(t) for t in y_tables(y_len))
     za, zb, zs = (jnp.asarray(t) for t in z_tables(z_len))
-    pick_x, pick_y = (jnp.asarray(parity_pick(n)) for n in (kx_len, y_local))
+    pick_x = jnp.asarray(pick_x_table(kx_len))
+    pick_y = lax.dynamic_index_in_dim(
+        jnp.asarray(pick_y_tables(y_local)), lax.axis_index("gy"), 0, keepdims=False
+    )
 
     spectrum = jax.ShapeDtypeStruct((devs, share, 2, tiles, z_local, LANES), jnp.float32)
     volume = jax.ShapeDtypeStruct(measured.shape, jnp.float32)
@@ -579,13 +623,13 @@
     def filtered(got, gains, adjoint):
         return call(
             functools.partial(gain_kernel, adjoint, at_once),
-            (got.reshape(planes), gains.reshape(planes), ya, za, *((zs, ys) if adjoint else (zb, yb))),
+            (got.reshape(planes), gains.reshape(planes), ya, za, *((zs, ys, edges) if adjoint else (zb, yb))),
             jax.ShapeDtypeStruct(planes, jnp.float32),
             3 * 8 * share * z_len * y_len * (2 * z_len + y_len),
             "adjoint" if adjoint else "blur",
         ).reshape(spectrum.shape)
 
-    def arranged(transfer_real, transfer_imag):
+    def arranged(pick_x):
         return call(
             arrange_kernel, (transfer_real, transfer_imag, pick_x, pick_y),
             jax.ShapeDtypeStruct((kx_len, *spectrum.shape[2:]), jnp.float32),
@@ -593,11 +637,9 @@
         ).reshape(spectrum.shape)
 
     send = first(measured)
-    send, transfer_real, transfer_imag = lax.optimization_barrier(
-        (send, transfer_real, transfer_imag)
-    )
+    send, pick_x = lax.optimization_barrier((send, pick_x))
     send = exchange(send)
-    gains = exchange(arranged(transfer_real, transfer_imag))
+    gains = exchange(arranged(pick_x))
     estimate = measured
     for iteration in range(ITERS):
         send = ratio(exchange(filtered(send, gains, False)), measured)
@@ -614,7 +656,8 @@
     return (
         z_len % LANES == 0
         and z_len // z_devs == SUBLANES
-        and y_len % (2 * LANES * y_devs) == 0
+        and y_devs == 2
+        and y_len == 4 * LANES
         and x_len % (4 * LANES) == 0
         and x_len // 2 == SUBLANES * z_devs * y_devs
     )

time: 974 us -> 966 us (level)
  Pallas kernels: 87.2 us -> 77 us
    pallas_call x10, Pallas kernels: 87.2 us -> 77 us  [call(): pl.pallas_call(kernel, in_specs=[spec] * len(arrays), out_specs=jax.tree....]
where the time goes in v5:
time: 966 us; the launch traced here: 957 us
  blocking collectives  779 us (81%)
  waiting for transfers between devices  84 us (9%)
  Pallas kernels  77 us (8%)
    all_to_all x8, blocking collectives, exchange(): lax.all_to_all(values, ('gz', 'gy'), split_axis=0, concat_axis=0, tiled=T...  779 us
    all_to_all x1, waiting for transfers between devices, exchange(): lax.all_to_all(values, ('gz', 'gy'), split_axis=0, concat_axis=0, tiled=T...  84 us
    pallas_call x10, Pallas kernels, call(): pl.pallas_call(kernel, in_specs=[spec] * len(arrays), out_specs=jax.tree....  77 us
  transfers between devices with their start and end apart: 1, of which 1 were waited for; matrix products, arithmetic and copies ran while one was open for 0% of the time, Pallas kernels for 1%

profile of v5, /device:TPU:0, one launch (start us, length us, event | category | flops | bytes accessed | tf_op | source)
XLA Modules:
  0.0 957.3 jit_solution(13490826164394457756)
XLA Ops:
  0.0 0.0 copy-start
  0.0 2.2 copy-done
  2.2 0.0 copy-start.3
  2.2 1.0 copy-done.3
  3.2 2.4 first.1
  5.6 0.0 copy-start.2
  5.6 2.0 copy-done.2
  7.6 0.0 copy-start.18
  7.6 0.0 copy-start.8
  7.6 0.0 copy-start.17
  7.6 7.4 all-to-all-start
  15.1 0.0 copy-done.18
  15.1 0.0 copy-done.8
  15.1 0.0 copy-done.17
  15.1 0.0 copy-start.9
  15.2 1.6 copy-done.9
  16.7 6.0 arrange.1
  22.8 0.0 copy-start.5
  22.8 2.0 copy-done.5
  24.8 84.0 %all-to-all-done = f32[32,8,2,2,8,128]{5,4,3,2,1,0:T(8,128)} async-done(((f32[32,8,2,2,8,128]{5,4,3,2,1,0:T(8,128)}), f32[32,8,2,2,8,128]{5,4,3,2,1,0:T(8,128)}, u32[]{:S(2)}, u32[]{:S(2)}) %all-to-all-start) | async-done | bytes 4194336 | tf_op jit(solution)/shard_map/all_to_all | solution.py:585
  108.8 0.0 copy-start.10
  108.8 0.0 copy-start.13
  108.8 0.0 copy-start.14
  108.8 0.0 copy-start.16
  108.8 98.4 %all_to_all.45 = f32[32,8,2,2,8,128]{5,4,3,2,1,0:T(8,128)S(1)} all-to-all(f32[32,8,2,2,8,128]{5,4,3,2,1,0:T(8,128)} %bitcast.16), channel_id=1, replica_groups=mesh['gz'=16,'gy'=2] {'gz','gy'}, dimensions={0} | all-to-all | bytes 8388608 | tf_op jit(solution)/shard_map/all_to_all | solution.py:585
  207.2 0.0 copy-done.10
  207.2 0.0 copy-done.13
  207.2 0.0 copy-done.14
  207.3 0.0 copy-done.16
  207.3 11.8 %blur.2 = f32[16,2,8,2,2,8,128]{6,5,4,3,2,1,0:T(8,128)S(1)} custom-call(f32[16,2,8,2,2,8,128]{6,5,4,3,2,1,0:T(8,128)} %bitcast.got_ref, f32[16,2,8,2,2,8,128]{6,5,4,3,2,1,0:T(8,128)S(1)} %bitcast.12, bf16[2,4,128,256]{3,2,1,0:T(8,128)(2,1)S(1)} %copy-done.10, bf16[2,256,256]{2,1,0:T(8,128)(2,1)S(1)} %copy-done.14, bf16[2,256,256]{2,1,0:T(8,128)(2,1)S(1)} %copy-done.16, ...), custom_call_target="tpu_custom_call" | custom-call | flops 9663676416 | bytes 14155776 | tf_op jit(solution)/shard_map/blur/pallas_call | solution.py:573
  219.1 0.0 copy-start.1
  219.1 0.0 copy-start.4
  219.1 0.0 copy-start.6
  219.1 97.2 %all_to_all.46.got_ref = f32[32,8,2,2,8,128]{5,4,3,2,1,0:T(8,128)S(1)} all-to-all(f32[32,8,2,2,8,128]{5,4,3,2,1,0:T(8,128)S(1)} %bitcast.21), channel_id=1, replica_groups=mesh['gz'=16,'gy'=2] {'gz','gy'}, dimensions={0} | all-to-all | bytes 8388608 | tf_op jit(solution)/shard_map/all_to_all | solution.py:585
  316.3 0.0 copy-done.1
  316.3 0.0 copy-done.4
  316.3 0.0 copy-done.6
  316.3 5.8 ratio.2
  322.1 0.0 copy-start.11
  322.1 0.0 copy-start.12
  322.1 0.0 copy-start.15
  322.1 97.2 %all_to_all.47 = f32[32,8,2,2,8,128]{5,4,3,2,1,0:T(8,128)S(1)} all-to-all(f32[32,8,2,2,8,128]{5,4,3,2,1,0:T(8,128)S(1)} %ratio.2), channel_id=1, replica_groups=mesh['gz'=16,'gy'=2] {'gz','gy'}, dimensions={0} | all-to-all | bytes 8388608 | tf_op jit(solution)/shard_map/all_to_all | solution.py:585
  419.3 0.0 copy-done.11
  419.3 0.0 copy-done.12
  419.3 0.0 copy-done.15
  419.3 11.8 %adjoint.2 = f32[16,2,8,2,2,8,128]{6,5,4,3,2,1,0:T(8,128)S(1)} custom-call(f32[16,2,8,2,2,8,128]{6,5,4,3,2,1,0:T(8,128)S(1)} %bitcast.22, f32[16,2,8,2,2,8,128]{6,5,4,3,2,1,0:T(8,128)S(1)} %bitcast.13, bf16[2,4,128,256]{3,2,1,0:T(8,128)(2,1)S(1)} %copy-done.10, bf16[2,256,256]{2,1,0:T(8,128)(2,1)S(1)} %copy-done.14, bf16[2,256,256]{2,1,0:T(8,128)(2,1)S(1)} %copy-done.15, ...), custom_call_target="tpu_custom_call" | custom-call | flops 9663676416 | bytes 14680064 | tf_op jit(solution)/shard_map/adjoint/pallas_call | solution.py:573
  431.1 0.0 copy-start.7
  431.1 97.6 %all_to_all.48.got_ref = f32[32,8,2,2,8,128]{5,4,3,2,1,0:T(8,128)S(1)} all-to-all(f32[32,8,2,2,8,128]{5,4,3,2,1,0:T(8,128)S(1)} %bitcast.23), channel_id=1, replica_groups=mesh['gz'=16,'gy'=2] {'gz','gy'}, dimensions={0} | all-to-all | bytes 8388608 | tf_op jit(solution)/shard_map/all_to_all | solution.py:585
  528.7 0.0 copy-done.7
  528.7 6.0 correct.1
  534.7 97.2 %all_to_all.49 = f32[32,8,2,2,8,128]{5,4,3,2,1,0:T(8,128)S(1)} all-to-all(f32[32,8,2,2,8,128]{5,4,3,2,1,0:T(8,128)S(1)} %get-tuple-element.11), channel_id=1, replica_groups=mesh['gz'=16,'gy'=2] {'gz','gy'}, dimensions={0} | all-to-all | bytes 8388608 | tf_op jit(solution)/shard_map/all_to_all | solution.py:585
  631.9 9.6 %blur.3 = f32[16,2,8,2,2,8,128]{6,5,4,3,2,1,0:T(8,128)S(1)} custom-call(f32[16,2,8,2,2,8,128]{6,5,4,3,2,1,0:T(8,128)S(1)} %bitcast.19, f32[16,2,8,2,2,8,128]{6,5,4,3,2,1,0:T(8,128)S(1)} %bitcast.14, bf16[2,4,128,256]{3,2,1,0:T(8,128)(2,1)S(1)} %copy-done.10, bf16[2,256,256]{2,1,0:T(8,128)(2,1)S(1)} %copy-done.14, bf16[2,256,256]{2,1,0:T(8,128)(2,1)S(1)} %copy-done.16, ...), custom_call_target="tpu_custom_call" | custom-call | flops 9663676416 | bytes 14155776 | tf_op jit(solution)/shard_map/blur/pallas_call | solution.py:573
  641.5 97.3 %all_to_all.50.got_ref = f32[32,8,2,2,8,128]{5,4,3,2,1,0:T(8,128)S(1)} all-to-all(f32[32,8,2,2,8,128]{5,4,3,2,1,0:T(8,128)S(1)} %bitcast.20), channel_id=1, replica_groups=mesh['gz'=16,'gy'=2] {'gz','gy'}, dimensions={0} | all-to-all | bytes 8388608 | tf_op jit(solution)/shard_map/all_to_all | solution.py:585
  738.8 5.8 ratio.3
  744.6 97.2 %all_to_all.51 = f32[32,8,2,2,8,128]{5,4,3,2,1,0:T(8,128)S(1)} all-to-all(f32[32,8,2,2,8,128]{5,4,3,2,1,0:T(8,128)S(1)} %ratio.3), channel_id=1, replica_groups=mesh['gz'=16,'gy'=2] {'gz','gy'}, dimensions={0} | all-to-all | bytes 8388608 | tf_op jit(solution)/shard_map/all_to_all | solution.py:585
  841.8 11.8 %adjoint.3 = f32[16,2,8,2,2,8,128]{6,5,4,3,2,1,0:T(8,128)S(1)} custom-call(f32[16,2,8,2,2,8,128]{6,5,4,3,2,1,0:T(8,128)S(1)} %bitcast.17, f32[16,2,8,2,2,8,128]{6,5,4,3,2,1,0:T(8,128)S(1)} %bitcast.15, bf16[2,4,128,256]{3,2,1,0:T(8,128)(2,1)S(1)} %copy-done.10, bf16[2,256,256]{2,1,0:T(8,128)(2,1)S(1)} %copy-done.14, bf16[2,256,256]{2,1,0:T(8,128)(2,1)S(1)} %copy-done.15, ...), custom_call_target="tpu_custom_call" | custom-call | flops 9663676416 | bytes 14680064 | tf_op jit(solution)/shard_map/adjoint/pallas_call | solution.py:573
  853.6 97.4 %all_to_all.52.got_ref = f32[32,8,2,2,8,128]{5,4,3,2,1,0:T(8,128)S(1)} all-to-all(f32[32,8,2,2,8,128]{5,4,3,2,1,0:T(8,128)S(1)} %bitcast.18), channel_id=1, replica_groups=mesh['gz'=16,'gy'=2] {'gz','gy'}, dimensions={0} | all-to-all | bytes 8388608 | tf_op jit(solution)/shard_map/all_to_all | solution.py:585
  951.0 6.0 last.1
  (1 shorter events, 0.0 us)
Async XLA Ops:
  0.0 2.2 copy-start
  2.2 1.0 copy-start.3
  5.6 2.0 copy-start.2
  7.6 7.4 copy-start.18
  7.6 7.5 copy-start.8
  7.6 7.5 copy-start.17
  7.6 101.2 %all-to-all-start = ((f32[32,8,2,2,8,128]{5,4,3,2,1,0:T(8,128)}), f32[32,8,2,2,8,128]{5,4,3,2,1,0:T(8,128)}, u32[]{:S(2)}, u32[]{:S(2)}) async-start(f32[32,8,2,2,8,128]{5,4,3,2,1,0:T(8,128)} %copy-done.2), calls=%async_computation | async-start | bytes 8388608 | tf_op jit(solution)/shard_map/all_to_all | solution.py:585
  15.1 1.6 copy-start.9
  22.8 2.0 copy-start.5
  108.8 98.4 %copy-start.10 = (bf16[2,4,128,256]{3,2,1,0:T(8,128)(2,1)S(1)}, bf16[2,4,128,256]{3,2,1,0:T(8,128)(2,1)}, u32[]{:S(2)}) copy-start(bf16[2,4,128,256]{3,2,1,0:T(8,128)(2,1)} %constant.37.clone.refs_1_) | copy-start | bytes 1572868
  108.8 98.4 %copy-start.13 = (bf16[2,4,128,256]{3,2,1,0:T(8,128)(2,1)S(1)}, bf16[2,4,128,256]{3,2,1,0:T(8,128)(2,1)}, u32[]{:S(2)}) copy-start(bf16[2,4,128,256]{3,2,1,0:T(8,128)(2,1)} %constant.38.clone.refs_4_) | copy-start | bytes 1572868
  108.8 98.4 %copy-start.14 = (bf16[2,256,256]{2,1,0:T(8,128)(2,1)S(1)}, bf16[2,256,256]{2,1,0:T(8,128)(2,1)}, u32[]{:S(2)}) copy-start(bf16[2,256,256]{2,1,0:T(8,128)(2,1)} %constant.41.clone.refs_2_) | copy-start | bytes 786436
  108.8 98.4 %copy-start.16 = (bf16[2,256,256]{2,1,0:T(8,128)(2,1)S(1)}, bf16[2,256,256]{2,1,0:T(8,128)(2,1)}, u32[]{:S(2)}) copy-start(bf16[2,256,256]{2,1,0:T(8,128)(2,1)} %constant.42.clone.refs_3_) | copy-start | bytes 786436
  219.1 97.2 %copy-start.1 = (f32[8,256,512]{2,1,0:T(8,128)S(1)}, f32[8,256,512]{2,1,0:T(8,128)}, u32[]{:S(2)}) copy-start(f32[8,256,512]{2,1,0:T(8,128)} %measured_ref.3) | copy-start | bytes 12582916
  219.1 97.2 %copy-start.4 = (bf16[2,2,256,256]{3,2,1,0:T(8,128)(2,1)S(1)}, bf16[2,2,256,256]{3,2,1,0:T(8,128)(2,1)}, u32[]{:S(2)}) copy-start(bf16[2,2,256,256]{3,2,1,0:T(8,128)(2,1)} %constant.34.clone.xa_ref) | copy-start | bytes 1572868
  219.1 97.2 %copy-start.6 = (bf16[2,2,256,256]{3,2,1,0:T(8,128)(2,1)S(1)}, bf16[2,2,256,256]{3,2,1,0:T(8,128)(2,1)}, u32[]{:S(2)}) copy-start(bf16[2,2,256,256]{3,2,1,0:T(8,128)(2,1)} %constant.35.clone.xb_ref) | copy-start | bytes 1572868
  322.1 97.2 %copy-start.11 = (bf16[2,512,256]{2,1,0:T(8,128)(2,1)S(1)}, bf16[2,512,256]{2,1,0:T(8,128)(2,1)}, u32[]{:S(2)}) copy-start(bf16[2,512,256]{2,1,0:T(8,128)(2,1)} %constant.40.clone.refs_5_) | copy-start | bytes 1572868
  322.1 97.2 %copy-start.12 = (bf16[2,4,128,256]{3,2,1,0:T(8,128)(2,1)S(1)}, bf16[2,4,128,256]{3,2,1,0:T(8,128)(2,1)}, u32[]{:S(2)}) copy-start(bf16[2,4,128,256]{3,2,1,0:T(8,128)(2,1)} %constant.39.clone.refs_4_) | copy-start | bytes 1572868
  322.1 97.2 %copy-start.15 = (bf16[2,256,256]{2,1,0:T(8,128)(2,1)S(1)}, bf16[2,256,256]{2,1,0:T(8,128)(2,1)}, u32[]{:S(2)}) copy-start(bf16[2,256,256]{2,1,0:T(8,128)(2,1)} %constant.43.clone.refs_3_) | copy-start | bytes 786436
  431.1 97.6 %copy-start.7 = (bf16[2,512,512]{2,1,0:T(8,128)(2,1)S(1)}, bf16[2,512,512]{2,1,0:T(8,128)(2,1)}, u32[]{:S(2)}) copy-start(bf16[2,512,512]{2,1,0:T(8,128)(2,1)} %constant.36.clone.xb_ref) | copy-start | bytes 3145732

commit v6 on v5

--- a/solution.py
+++ b/solution.py
@@ -390,7 +390,7 @@
 
 def halves(volume_ref, tile):
     half = volume_ref.shape[2] // 2
-    rows = slice(tile * LANES, (tile + 1) * LANES)
+    rows = pl.ds(pl.multiple_of(tile * LANES, LANES), LANES)
     return (
         volume_ref[:, rows, :half].reshape(-1, half),
         volume_ref[:, rows, half:].reshape(-1, half),
@@ -399,20 +399,22 @@
 
 def store_halves(volume_ref, tile, left, right):
     half = volume_ref.shape[2] // 2
-    rows = slice(tile * LANES, (tile + 1) * LANES)
+    rows = pl.ds(pl.multiple_of(tile * LANES, LANES), LANES)
     shape = (volume_ref.shape[0], LANES, half)
     volume_ref[:, rows, :half] = left.reshape(shape)
     volume_ref[:, rows, half:] = right.reshape(shape)
 
 
 def first_kernel(volume_ref, xa_ref, send_ref):
-    for tile in range(send_ref.shape[3]):
+    @pl.loop(0, send_ref.shape[3])
+    def _(tile):
         left, right = halves(volume_ref, tile)
         lines_ahead(left, right, send_ref, tile, xa_ref)
 
 
 def ratio_kernel(got_ref, measured_ref, xb_ref, xa_ref, send_ref):
-    for tile in range(got_ref.shape[3]):
+    @pl.loop(0, got_ref.shape[3])
+    def _(tile):
         left, right = lines_back_sharp(got_ref, tile, xb_ref)
         over_left, over_right = halves(measured_ref, tile)
         left = over_left / jnp.maximum(left, FLOOR)
@@ -421,7 +423,8 @@
 
 
 def correct_kernel(got_ref, estimate_ref, xb_ref, xa_ref, send_ref, out_ref):
-    for tile in range(got_ref.shape[3]):
+    @pl.loop(0, got_ref.shape[3])
+    def _(tile):
         left, right = lines_back_soft(got_ref, tile, xb_ref)
         old_left, old_right = halves(estimate_ref, tile)
         left, right = old_left * left, old_right * right
@@ -430,7 +433,8 @@
 
 
 def last_kernel(got_ref, estimate_ref, xb_ref, out_ref):
-    for tile in range(got_ref.shape[3]):
+    @pl.loop(0, got_ref.shape[3])
+    def _(tile):
         left, right = lines_back_soft(got_ref, tile, xb_ref)
         old_left, old_right = halves(estimate_ref, tile)
         store_halves(out_ref, tile, old_left * left, old_right * right)
@@ -446,8 +450,10 @@
     z_len, _, kx_len = real_ref.shape
     tiles = send_ref.shape[2]
     flat = send_ref.reshape(kx_len * 2 * tiles * z_len, LANES)
-    for part, ref in enumerate((real_ref, imag_ref)):
-        for z in range(z_len):
+
+    @pl.loop(0, z_len)
+    def _(z):
+        for part, ref in enumerate((real_ref, imag_ref)):
             values = picked(picked(ref[z], pick_x_ref[...]).T, pick_y_ref[...])
             for tile in range(tiles):
                 start = (part * tiles + tile) * z_len + z

time: 966 us -> 958 us (level)
  no operation moved by 1% of the time
where the time goes in v6:
time: 958 us; the launch traced here: 957 us
  blocking collectives  779 us (81%)
  waiting for transfers between devices  81.4 us (8%)
  Pallas kernels  80.8 us (8%)
    all_to_all x8, blocking collectives, exchange(): lax.all_to_all(values, ('gz', 'gy'), split_axis=0, concat_axis=0, tiled=T...  779 us
    all_to_all x1, waiting for transfers between devices, exchange(): lax.all_to_all(values, ('gz', 'gy'), split_axis=0, concat_axis=0, tiled=T...  81.4 us
    pallas_call x10, Pallas kernels, call(): pl.pallas_call(kernel, in_specs=[spec] * len(arrays), out_specs=jax.tree....  80.8 us
  transfers between devices with their start and end apart: 1, of which 1 were waited for; matrix products, arithmetic and copies ran while one was open for 0% of the time, Pallas kernels for 1%

profile of v6, /device:TPU:0, one launch (start us, length us, event | category | flops | bytes accessed | tf_op | source)
XLA Modules:
  0.0 957.4 jit_solution(17924242308962493163)
XLA Ops:
  0.0 0.0 copy-start
  0.0 2.2 copy-done
  2.2 0.0 copy-start.3
  2.2 1.0 copy-done.3
  3.2 2.6 first.1
  5.8 0.0 copy-start.2
  5.8 2.0 copy-done.2
  7.8 0.0 copy-start.18
  7.8 0.0 copy-start.8
  7.8 0.0 copy-start.17
  7.8 7.4 all-to-all-start
  15.3 0.0 copy-done.18
  15.3 0.0 copy-done.8
  15.3 0.0 copy-done.17
  15.3 0.0 copy-start.9
  15.3 1.6 copy-done.9
  16.9 8.7 arrange.1
  25.6 0.0 copy-start.5
  25.6 2.0 copy-done.5
  27.6 81.4 %all-to-all-done = f32[32,8,2,2,8,128]{5,4,3,2,1,0:T(8,128)} async-done(((f32[32,8,2,2,8,128]{5,4,3,2,1,0:T(8,128)}), f32[32,8,2,2,8,128]{5,4,3,2,1,0:T(8,128)}, u32[]{:S(2)}, u32[]{:S(2)}) %all-to-all-start) | async-done | bytes 4194336 | tf_op jit(solution)/shard_map/all_to_all | solution.py:591
  109.0 0.0 copy-start.10
  109.0 0.0 copy-start.13
  109.0 0.0 copy-start.14
  109.0 0.0 copy-start.16
  109.0 98.4 %all_to_all.45 = f32[32,8,2,2,8,128]{5,4,3,2,1,0:T(8,128)S(1)} all-to-all(f32[32,8,2,2,8,128]{5,4,3,2,1,0:T(8,128)} %bitcast.16), channel_id=1, replica_groups=mesh['gz'=16,'gy'=2] {'gz','gy'}, dimensions={0} | all-to-all | bytes 8388608 | tf_op jit(solution)/shard_map/all_to_all | solution.py:591
  207.4 0.0 copy-done.10
  207.4 0.0 copy-done.13
  207.4 0.0 copy-done.14
  207.4 0.0 copy-done.16
  207.4 11.8 %blur.2 = f32[16,2,8,2,2,8,128]{6,5,4,3,2,1,0:T(8,128)S(1)} custom-call(f32[16,2,8,2,2,8,128]{6,5,4,3,2,1,0:T(8,128)} %bitcast.got_ref, f32[16,2,8,2,2,8,128]{6,5,4,3,2,1,0:T(8,128)S(1)} %bitcast.12, bf16[2,4,128,256]{3,2,1,0:T(8,128)(2,1)S(1)} %copy-done.10, bf16[2,256,256]{2,1,0:T(8,128)(2,1)S(1)} %copy-done.14, bf16[2,256,256]{2,1,0:T(8,128)(2,1)S(1)} %copy-done.16, ...), custom_call_target="tpu_custom_call" | custom-call | flops 9663676416 | bytes 14155776 | tf_op jit(solution)/shard_map/blur/pallas_call | solution.py:579
  219.2 0.0 copy-start.1
  219.2 0.0 copy-start.4
  219.3 0.0 copy-start.6
  219.3 97.2 %all_to_all.46.got_ref = f32[32,8,2,2,8,128]{5,4,3,2,1,0:T(8,128)S(1)} all-to-all(f32[32,8,2,2,8,128]{5,4,3,2,1,0:T(8,128)S(1)} %bitcast.21), channel_id=1, replica_groups=mesh['gz'=16,'gy'=2] {'gz','gy'}, dimensions={0} | all-to-all | bytes 8388608 | tf_op jit(solution)/shard_map/all_to_all | solution.py:591
  316.4 0.0 copy-done.1
  316.4 0.0 copy-done.4
  316.4 0.0 copy-done.6
  316.4 6.1 ratio.2
  322.6 0.0 copy-start.11
  322.6 0.0 copy-start.12
  322.6 0.0 copy-start.15
  322.6 97.2 %all_to_all.47 = f32[32,8,2,2,8,128]{5,4,3,2,1,0:T(8,128)S(1)} all-to-all(f32[32,8,2,2,8,128]{5,4,3,2,1,0:T(8,128)S(1)} %ratio.2), channel_id=1, replica_groups=mesh['gz'=16,'gy'=2] {'gz','gy'}, dimensions={0} | all-to-all | bytes 8388608 | tf_op jit(solution)/shard_map/all_to_all | solution.py:591
  419.8 0.0 copy-done.11
  419.8 0.0 copy-done.12
  419.8 0.0 copy-done.15
  419.8 11.8 %adjoint.2 = f32[16,2,8,2,2,8,128]{6,5,4,3,2,1,0:T(8,128)S(1)} custom-call(f32[16,2,8,2,2,8,128]{6,5,4,3,2,1,0:T(8,128)S(1)} %bitcast.22, f32[16,2,8,2,2,8,128]{6,5,4,3,2,1,0:T(8,128)S(1)} %bitcast.13, bf16[2,4,128,256]{3,2,1,0:T(8,128)(2,1)S(1)} %copy-done.10, bf16[2,256,256]{2,1,0:T(8,128)(2,1)S(1)} %copy-done.14, bf16[2,256,256]{2,1,0:T(8,128)(2,1)S(1)} %copy-done.15, ...), custom_call_target="tpu_custom_call" | custom-call | flops 9663676416 | bytes 14680064 | tf_op jit(solution)/shard_map/adjoint/pallas_call | solution.py:579
  431.6 0.0 copy-start.7
  431.6 97.2 %all_to_all.48.got_ref = f32[32,8,2,2,8,128]{5,4,3,2,1,0:T(8,128)S(1)} all-to-all(f32[32,8,2,2,8,128]{5,4,3,2,1,0:T(8,128)S(1)} %bitcast.23), channel_id=1, replica_groups=mesh['gz'=16,'gy'=2] {'gz','gy'}, dimensions={0} | all-to-all | bytes 8388608 | tf_op jit(solution)/shard_map/all_to_all | solution.py:591
  528.8 0.0 copy-done.7
  528.8 6.2 correct.1
  535.0 97.2 %all_to_all.49 = f32[32,8,2,2,8,128]{5,4,3,2,1,0:T(8,128)S(1)} all-to-all(f32[32,8,2,2,8,128]{5,4,3,2,1,0:T(8,128)S(1)} %get-tuple-element.11), channel_id=1, replica_groups=mesh['gz'=16,'gy'=2] {'gz','gy'}, dimensions={0} | all-to-all | bytes 8388608 | tf_op jit(solution)/shard_map/all_to_all | solution.py:591
  632.1 9.6 %blur.3 = f32[16,2,8,2,2,8,128]{6,5,4,3,2,1,0:T(8,128)S(1)} custom-call(f32[16,2,8,2,2,8,128]{6,5,4,3,2,1,0:T(8,128)S(1)} %bitcast.19, f32[16,2,8,2,2,8,128]{6,5,4,3,2,1,0:T(8,128)S(1)} %bitcast.14, bf16[2,4,128,256]{3,2,1,0:T(8,128)(2,1)S(1)} %copy-done.10, bf16[2,256,256]{2,1,0:T(8,128)(2,1)S(1)} %copy-done.14, bf16[2,256,256]{2,1,0:T(8,128)(2,1)S(1)} %copy-done.16, ...), custom_call_target="tpu_custom_call" | custom-call | flops 9663676416 | bytes 14155776 | tf_op jit(solution)/shard_map/blur/pallas_call | solution.py:579
  641.8 97.2 %all_to_all.50.got_ref = f32[32,8,2,2,8,128]{5,4,3,2,1,0:T(8,128)S(1)} all-to-all(f32[32,8,2,2,8,128]{5,4,3,2,1,0:T(8,128)S(1)} %bitcast.20), channel_id=1, replica_groups=mesh['gz'=16,'gy'=2] {'gz','gy'}, dimensions={0} | all-to-all | bytes 8388608 | tf_op jit(solution)/shard_map/all_to_all | solution.py:591
  738.9 6.1 ratio.3
  745.0 97.2 %all_to_all.51 = f32[32,8,2,2,8,128]{5,4,3,2,1,0:T(8,128)S(1)} all-to-all(f32[32,8,2,2,8,128]{5,4,3,2,1,0:T(8,128)S(1)} %ratio.3), channel_id=1, replica_groups=mesh['gz'=16,'gy'=2] {'gz','gy'}, dimensions={0} | all-to-all | bytes 8388608 | tf_op jit(solution)/shard_map/all_to_all | solution.py:591
  842.2 11.8 %adjoint.3 = f32[16,2,8,2,2,8,128]{6,5,4,3,2,1,0:T(8,128)S(1)} custom-call(f32[16,2,8,2,2,8,128]{6,5,4,3,2,1,0:T(8,128)S(1)} %bitcast.17, f32[16,2,8,2,2,8,128]{6,5,4,3,2,1,0:T(8,128)S(1)} %bitcast.15, bf16[2,4,128,256]{3,2,1,0:T(8,128)(2,1)S(1)} %copy-done.10, bf16[2,256,256]{2,1,0:T(8,128)(2,1)S(1)} %copy-done.14, bf16[2,256,256]{2,1,0:T(8,128)(2,1)S(1)} %copy-done.15, ...), custom_call_target="tpu_custom_call" | custom-call | flops 9663676416 | bytes 14680064 | tf_op jit(solution)/shard_map/adjoint/pallas_call | solution.py:579
  854.0 97.2 %all_to_all.52.got_ref = f32[32,8,2,2,8,128]{5,4,3,2,1,0:T(8,128)S(1)} all-to-all(f32[32,8,2,2,8,128]{5,4,3,2,1,0:T(8,128)S(1)} %bitcast.18), channel_id=1, replica_groups=mesh['gz'=16,'gy'=2] {'gz','gy'}, dimensions={0} | all-to-all | bytes 8388608 | tf_op jit(solution)/shard_map/all_to_all | solution.py:591
  951.2 6.2 last.1
  (1 shorter events, 0.0 us)
Async XLA Ops:
  0.0 2.2 copy-start
  2.2 1.0 copy-start.3
  5.8 2.0 copy-start.2
  7.8 7.4 copy-start.18
  7.8 7.5 copy-start.8
  7.8 7.5 copy-start.17
  7.8 101.2 %all-to-all-start = ((f32[32,8,2,2,8,128]{5,4,3,2,1,0:T(8,128)}), f32[32,8,2,2,8,128]{5,4,3,2,1,0:T(8,128)}, u32[]{:S(2)}, u32[]{:S(2)}) async-start(f32[32,8,2,2,8,128]{5,4,3,2,1,0:T(8,128)} %copy-done.2), calls=%async_computation | async-start | bytes 8388608 | tf_op jit(solution)/shard_map/all_to_all | solution.py:591
  15.3 1.6 copy-start.9
  25.6 2.0 copy-start.5
  109.0 98.4 %copy-start.10 = (bf16[2,4,128,256]{3,2,1,0:T(8,128)(2,1)S(1)}, bf16[2,4,128,256]{3,2,1,0:T(8,128)(2,1)}, u32[]{:S(2)}) copy-start(bf16[2,4,128,256]{3,2,1,0:T(8,128)(2,1)} %constant.37.clone.refs_1_) | copy-start | bytes 1572868
  109.0 98.4 %copy-start.13 = (bf16[2,4,128,256]{3,2,1,0:T(8,128)(2,1)S(1)}, bf16[2,4,128,256]{3,2,1,0:T(8,128)(2,1)}, u32[]{:S(2)}) copy-start(bf16[2,4,128,256]{3,2,1,0:T(8,128)(2,1)} %constant.38.clone.refs_4_) | copy-start | bytes 1572868
  109.0 98.4 %copy-start.14 = (bf16[2,256,256]{2,1,0:T(8,128)(2,1)S(1)}, bf16[2,256,256]{2,1,0:T(8,128)(2,1)}, u32[]{:S(2)}) copy-start(bf16[2,256,256]{2,1,0:T(8,128)(2,1)} %constant.41.clone.refs_2_) | copy-start | bytes 786436
  109.0 98.4 %copy-start.16 = (bf16[2,256,256]{2,1,0:T(8,128)(2,1)S(1)}, bf16[2,256,256]{2,1,0:T(8,128)(2,1)}, u32[]{:S(2)}) copy-start(bf16[2,256,256]{2,1,0:T(8,128)(2,1)} %constant.42.clone.refs_3_) | copy-start | bytes 786436
  219.2 97.2 %copy-start.1 = (f32[8,256,512]{2,1,0:T(8,128)S(1)}, f32[8,256,512]{2,1,0:T(8,128)}, u32[]{:S(2)}) copy-start(f32[8,256,512]{2,1,0:T(8,128)} %measured_ref.3) | copy-start | bytes 12582916
  219.2 97.2 %copy-start.4 = (bf16[2,2,256,256]{3,2,1,0:T(8,128)(2,1)S(1)}, bf16[2,2,256,256]{3,2,1,0:T(8,128)(2,1)}, u32[]{:S(2)}) copy-start(bf16[2,2,256,256]{3,2,1,0:T(8,128)(2,1)} %constant.34.clone.xa_ref) | copy-start | bytes 1572868
  219.3 97.2 %copy-start.6 = (bf16[2,2,256,256]{3,2,1,0:T(8,128)(2,1)S(1)}, bf16[2,2,256,256]{3,2,1,0:T(8,128)(2,1)}, u32[]{:S(2)}) copy-start(bf16[2,2,256,256]{3,2,1,0:T(8,128)(2,1)} %constant.35.clone.xb_ref) | copy-start | bytes 1572868
  322.6 97.2 %copy-start.11 = (bf16[2,512,256]{2,1,0:T(8,128)(2,1)S(1)}, bf16[2,512,256]{2,1,0:T(8,128)(2,1)}, u32[]{:S(2)}) copy-start(bf16[2,512,256]{2,1,0:T(8,128)(2,1)} %constant.40.clone.refs_5_) | copy-start | bytes 1572868
  322.6 97.2 %copy-start.12 = (bf16[2,4,128,256]{3,2,1,0:T(8,128)(2,1)S(1)}, bf16[2,4,128,256]{3,2,1,0:T(8,128)(2,1)}, u32[]{:S(2)}) copy-start(bf16[2,4,128,256]{3,2,1,0:T(8,128)(2,1)} %constant.39.clone.refs_4_) | copy-start | bytes 1572868
  322.6 97.2 %copy-start.15 = (bf16[2,256,256]{2,1,0:T(8,128)(2,1)S(1)}, bf16[2,256,256]{2,1,0:T(8,128)(2,1)}, u32[]{:S(2)}) copy-start(bf16[2,256,256]{2,1,0:T(8,128)(2,1)} %constant.43.clone.refs_3_) | copy-start | bytes 786436
  431.6 97.2 %copy-start.7 = (bf16[2,512,512]{2,1,0:T(8,128)(2,1)S(1)}, bf16[2,512,512]{2,1,0:T(8,128)(2,1)}, u32[]{:S(2)}) copy-start(bf16[2,512,512]{2,1,0:T(8,128)(2,1)} %constant.36.clone.xb_ref) | copy-start | bytes 3145732

commit v7 on v6

--- a/solution.py
+++ b/solution.py
@@ -405,11 +405,30 @@
     volume_ref[:, rows, half:] = right.reshape(shape)
 
 
-def first_kernel(volume_ref, xa_ref, send_ref):
-    @pl.loop(0, send_ref.shape[3])
+def first_kernel(volume_ref, xa_ref, send_ref, volume_buf, send_buf, in_sems, out_sems):
+    tiles = send_ref.shape[3]
+
+    def copy_in(tile):
+        rows = pl.ds(pl.multiple_of(tile * LANES, LANES), LANES)
+        return pltpu.make_async_copy(volume_ref.at[:, rows], volume_buf.at[tile], in_sems.at[tile])
+
+    def copy_out(tile):
+        return pltpu.make_async_copy(
+            send_buf.at[tile], send_ref.at[:, :, :, pl.ds(tile, 1)], out_sems.at[tile]
+        )
+
+    for tile in range(tiles):
+        copy_in(tile).start()
+
+    @pl.loop(0, tiles)
     def _(tile):
-        left, right = halves(volume_ref, tile)
-        lines_ahead(left, right, send_ref, tile, xa_ref)
+        copy_in(tile).wait()
+        left, right = halves(volume_buf.at[tile], 0)
+        lines_ahead(left, right, send_buf.at[tile], 0, xa_ref)
+        copy_out(tile).start()
+
+    for tile in range(tiles):
+        copy_out(tile).wait()
 
 
 def ratio_kernel(got_ref, measured_ref, xb_ref, xa_ref, send_ref):
@@ -432,34 +451,47 @@
         lines_ahead(left, right, send_ref, tile, xa_ref)
 
 
-def last_kernel(got_ref, estimate_ref, xb_ref, out_ref):
-    @pl.loop(0, got_ref.shape[3])
+def last_kernel(got_ref, estimate_ref, xb_ref, out_ref, out_buf, out_sems):
+    tiles = got_ref.shape[3]
+
+    def copy_out(tile):
+        rows = pl.ds(pl.multiple_of(tile * LANES, LANES), LANES)
+        return pltpu.make_async_copy(out_buf.at[tile], out_ref.at[:, rows], out_sems.at[tile])
+
+    @pl.loop(0, tiles)
     def _(tile):
         left, right = lines_back_soft(got_ref, tile, xb_ref)
         old_left, old_right = halves(estimate_ref, tile)
-        store_halves(out_ref, tile, old_left * left, old_right * right)
+        store_halves(out_buf.at[tile], 0, old_left * left, old_right * right)
+        copy_out(tile).start()
+
+    for tile in range(tiles):
+        copy_out(tile).wait()
 
 
 def picked(values, pick):
     first, second = split_terms(values)
-    rest = values - first.astype(jnp.float32) - second.astype(jnp.float32)
-    return dot(first, pick) + dot(second, pick) + dot(rest.astype(jnp.bfloat16), pick)
+    return dot(
+        jnp.concatenate((first, second), axis=1), jnp.concatenate((pick, pick), axis=0)
+    )
 
 
 def arrange_kernel(real_ref, imag_ref, pick_x_ref, pick_y_ref, send_ref):
-    z_len, _, kx_len = real_ref.shape
-    tiles = send_ref.shape[2]
-    flat = send_ref.reshape(kx_len * 2 * tiles * z_len, LANES)
-
-    @pl.loop(0, z_len)
-    def _(z):
-        for part, ref in enumerate((real_ref, imag_ref)):
-            values = picked(picked(ref[z], pick_x_ref[...]).T, pick_y_ref[...])
-            for tile in range(tiles):
-                start = (part * tiles + tile) * z_len + z
-                flat[pl.ds(start, kx_len, 2 * tiles * z_len), :] = values[
-                    :, tile * LANES : (tile + 1) * LANES
-                ]
+    devs, _, _, tiles, z_len, _ = send_ref.shape
+
+    @pl.loop(0, 2)
+    def _(part):
+        planes = []
+        for z in range(z_len):
+            values = jnp.where(part == 0, real_ref[z], imag_ref[z])
+            planes.append(picked(picked(values, pick_x_ref[...]).T, pick_y_ref[...]))
+        for tile in range(tiles):
+            blocks = [
+                plane[:, tile * LANES : (tile + 1) * LANES].reshape(devs, SUBLANES, LANES)
+                for plane in planes
+            ]
+            for i, block in enumerate(swapped(blocks)):
+                send_ref[:, i, part, tile] = block
 
 
 def turned_ahead(both):
@@ -570,18 +602,20 @@
 
 KX_AT_ONCE = 4
 VMEM_BYTES = 32 * 2**20
-
-
-def call(kernel, arrays, outs, flops, name):
+ALL_VMEM_BYTES = 59 * 2**20
+
+
+def call(kernel, arrays, outs, flops, name, specs=(), out_spec=None, scratch=(), vmem=None):
     leaves = (*arrays, *jax.tree.leaves(outs))
     moved = sum(math.prod(a.shape) * a.dtype.itemsize for a in leaves)
     spec = pl.BlockSpec(memory_space=pltpu.VMEM)
     return pl.pallas_call(
         kernel,
-        in_specs=[spec] * len(arrays),
-        out_specs=jax.tree.map(lambda _: spec, outs),
+        in_specs=[*specs, *[spec] * (len(arrays) - len(specs))],
+        out_specs=out_spec or jax.tree.map(lambda _: spec, outs),
         out_shape=outs,
-        compiler_params=pltpu.CompilerParams(vmem_limit_bytes=VMEM_BYTES),
+        scratch_shapes=scratch,
+        compiler_params=pltpu.CompilerParams(vmem_limit_bytes=vmem or VMEM_BYTES),
         cost_estimate=pl.CostEstimate(flops=flops, bytes_accessed=moved, transcendentals=0),
         name=name,
     )(*arrays)
@@ -607,10 +641,17 @@
 
     spectrum = jax.ShapeDtypeStruct((devs, share, 2, tiles, z_local, LANES), jnp.float32)
     volume = jax.ShapeDtypeStruct(measured.shape, jnp.float32)
+    far = pl.BlockSpec(memory_space=pltpu.HBM)
+    sems = pltpu.SemaphoreType.DMA((tiles,))
+    volume_tiles = pltpu.VMEM((tiles, z_local, LANES, x_len), jnp.float32)
+    spectrum_tiles = pltpu.VMEM((tiles, devs, share, 2, 1, z_local, LANES), jnp.float32)
     line_flops = 3 * z_local * y_local * x_len * x_len
 
     def first(values):
-        return call(first_kernel, (values, xa), spectrum, line_flops, "first")
+        return call(
+            first_kernel, (values, xa), spectrum, line_flops, "first", (far,), far,
+            (volume_tiles, spectrum_tiles, sems, sems), ALL_VMEM_BYTES,
+        )
 
     def ratio(got, values):
         return call(ratio_kernel, (got, values, xb, xa), spectrum, 2 * line_flops, "ratio")
@@ -621,7 +662,10 @@
         )
 
     def last(got, values):
-        return call(last_kernel, (got, values, xs), volume, 2 * line_flops, "last")
+        return call(
+            last_kernel, (got, values, xs), volume, 2 * line_flops, "last", (), far,
+            (volume_tiles, sems),
+        )
 
     planes = (z_devs, y_devs, *spectrum.shape[1:])
     at_once = KX_AT_ONCE if share % KX_AT_ONCE == 0 else 1
@@ -638,9 +682,9 @@
     def arranged(pick_x):
         return call(
             arrange_kernel, (transfer_real, transfer_imag, pick_x, pick_y),
-            jax.ShapeDtypeStruct((kx_len, *spectrum.shape[2:]), jnp.float32),
+            spectrum,
             3 * 4 * z_local * y_local * kx_len * (y_local + kx_len), "arrange",
-        ).reshape(spectrum.shape)
+        )
 
     send = first(measured)
     send, pick_x = lax.optimization_barrier((send, pick_x))

time: 958 us -> 956 us (level)
  transfers between devices with their start and end apart: 1 -> 1, of which waited for: 1 -> 1; matrix products, arithmetic and copies ran while one was open for 0% -> 0% of each run, Pallas kernels for 1% -> 0%
where the time goes in v7:
time: 956 us
  blocking collectives  779 us (81%)
  waiting for transfers between devices  86.4 us (9%)
  Pallas kernels  79 us (8%)
    all_to_all x8, blocking collectives, exchange(): lax.all_to_all(values, ('gz', 'gy'), split_axis=0, concat_axis=0, tiled=T...  779 us
    all_to_all x1, waiting for transfers between devices, exchange(): lax.all_to_all(values, ('gz', 'gy'), split_axis=0, concat_axis=0, tiled=T...  86.4 us
    pallas_call x10, Pallas kernels, call(): pl.pallas_call(kernel, in_specs=[*specs, *[spec] * (len(arrays) - len(spe...  79 us
  transfers between devices with their start and end apart: 1, of which 1 were waited for; matrix products, arithmetic and copies ran while one was open for 0% of the time, Pallas kernels for 0%

profile of v7, /device:TPU:0, one launch (start us, length us, event | category | flops | bytes accessed | tf_op | source)
XLA Modules:
  0.0 955.5 jit_solution(2139766015739594046)
XLA Ops:
  0.0 6.4 first.1
  6.4 0.0 copy-start.15
  6.4 0.0 copy-start.5
  6.5 0.0 copy-start.14
  6.5 7.4 all-to-all-start
  13.9 0.0 copy-done.15
  13.9 0.0 copy-done.5
  14.0 0.0 copy-done.14
  14.0 0.0 copy-start.6
  14.0 1.6 copy-done.6
  15.6 3.6 arrange.1
  19.2 0.0 copy-start.2
  19.2 2.0 copy-done.2
  21.2 0.0 copy-start.7
  21.2 0.0 copy-start.10
  21.2 0.0 copy-start.11
  21.2 0.0 copy-start.13
  21.2 86.4 %all-to-all-done = f32[32,8,2,2,8,128]{5,4,3,2,1,0:T(8,128)} async-done(((f32[32,8,2,2,8,128]{5,4,3,2,1,0:T(8,128)}), f32[32,8,2,2,8,128]{5,4,3,2,1,0:T(8,128)}, u32[]{:S(2)}, u32[]{:S(2)}) %all-to-all-start) | async-done | bytes 4194336 | tf_op jit(solution)/shard_map/all_to_all | solution.py:625
  107.6 98.4 %all_to_all.45 = f32[32,8,2,2,8,128]{5,4,3,2,1,0:T(8,128)S(1)} all-to-all(f32[32,8,2,2,8,128]{5,4,3,2,1,0:T(8,128)} %copy-done.2), channel_id=1, replica_groups=mesh['gz'=16,'gy'=2] {'gz','gy'}, dimensions={0} | all-to-all | bytes 8388608 | tf_op jit(solution)/shard_map/all_to_all | solution.py:625
  206.0 0.0 copy-done.7
  206.0 0.0 copy-done.10
  206.1 0.0 copy-done.11
  206.1 0.0 copy-done.13
  206.1 11.8 %blur.2 = f32[16,2,8,2,2,8,128]{6,5,4,3,2,1,0:T(8,128)S(1)} custom-call(f32[16,2,8,2,2,8,128]{6,5,4,3,2,1,0:T(8,128)} %bitcast.got_ref, f32[16,2,8,2,2,8,128]{6,5,4,3,2,1,0:T(8,128)S(1)} %bitcast.11, bf16[2,4,128,256]{3,2,1,0:T(8,128)(2,1)S(1)} %copy-done.7, bf16[2,256,256]{2,1,0:T(8,128)(2,1)S(1)} %copy-done.11, bf16[2,256,256]{2,1,0:T(8,128)(2,1)S(1)} %copy-done.13, ...), custom_call_target="tpu_custom_call" | custom-call | flops 9663676416 | bytes 14155776 | tf_op jit(solution)/shard_map/blur/pallas_call | solution.py:612
  217.9 0.0 copy-start
  217.9 0.0 copy-start.1
  217.9 0.0 copy-start.3
  217.9 97.2 %all_to_all.46.got_ref = f32[32,8,2,2,8,128]{5,4,3,2,1,0:T(8,128)S(1)} all-to-all(f32[32,8,2,2,8,128]{5,4,3,2,1,0:T(8,128)S(1)} %bitcast.19), channel_id=1, replica_groups=mesh['gz'=16,'gy'=2] {'gz','gy'}, dimensions={0} | all-to-all | bytes 8388608 | tf_op jit(solution)/shard_map/all_to_all | solution.py:625
  315.1 0.0 copy-done
  315.1 0.0 copy-done.1
  315.1 0.0 copy-done.3
  315.1 6.1 ratio.2
  321.2 0.0 copy-start.8
  321.2 0.0 copy-start.9
  321.2 0.0 copy-start.12
  321.2 97.2 %all_to_all.47 = f32[32,8,2,2,8,128]{5,4,3,2,1,0:T(8,128)S(1)} all-to-all(f32[32,8,2,2,8,128]{5,4,3,2,1,0:T(8,128)S(1)} %ratio.2), channel_id=1, replica_groups=mesh['gz'=16,'gy'=2] {'gz','gy'}, dimensions={0} | all-to-all | bytes 8388608 | tf_op jit(solution)/shard_map/all_to_all | solution.py:625
  418.4 0.0 copy-done.8
  418.4 0.0 copy-done.9
  418.4 0.0 copy-done.12
  418.4 11.8 %adjoint.2 = f32[16,2,8,2,2,8,128]{6,5,4,3,2,1,0:T(8,128)S(1)} custom-call(f32[16,2,8,2,2,8,128]{6,5,4,3,2,1,0:T(8,128)S(1)} %bitcast.20, f32[16,2,8,2,2,8,128]{6,5,4,3,2,1,0:T(8,128)S(1)} %bitcast.12, bf16[2,4,128,256]{3,2,1,0:T(8,128)(2,1)S(1)} %copy-done.7, bf16[2,256,256]{2,1,0:T(8,128)(2,1)S(1)} %copy-done.11, bf16[2,256,256]{2,1,0:T(8,128)(2,1)S(1)} %copy-done.12, ...), custom_call_target="tpu_custom_call" | custom-call | flops 9663676416 | bytes 14680064 | tf_op jit(solution)/shard_map/adjoint/pallas_call | solution.py:612
  430.2 0.0 copy-start.4
  430.2 97.2 %all_to_all.48.got_ref = f32[32,8,2,2,8,128]{5,4,3,2,1,0:T(8,128)S(1)} all-to-all(f32[32,8,2,2,8,128]{5,4,3,2,1,0:T(8,128)S(1)} %bitcast.21), channel_id=1, replica_groups=mesh['gz'=16,'gy'=2] {'gz','gy'}, dimensions={0} | all-to-all | bytes 8388608 | tf_op jit(solution)/shard_map/all_to_all | solution.py:625
  527.4 0.0 copy-done.4
  527.4 6.2 correct.1
  533.6 97.2 %all_to_all.49 = f32[32,8,2,2,8,128]{5,4,3,2,1,0:T(8,128)S(1)} all-to-all(f32[32,8,2,2,8,128]{5,4,3,2,1,0:T(8,128)S(1)} %get-tuple-element.11), channel_id=1, replica_groups=mesh['gz'=16,'gy'=2] {'gz','gy'}, dimensions={0} | all-to-all | bytes 8388608 | tf_op jit(solution)/shard_map/all_to_all | solution.py:625
  630.8 9.6 %blur.3 = f32[16,2,8,2,2,8,128]{6,5,4,3,2,1,0:T(8,128)S(1)} custom-call(f32[16,2,8,2,2,8,128]{6,5,4,3,2,1,0:T(8,128)S(1)} %bitcast.17, f32[16,2,8,2,2,8,128]{6,5,4,3,2,1,0:T(8,128)S(1)} %bitcast.13, bf16[2,4,128,256]{3,2,1,0:T(8,128)(2,1)S(1)} %copy-done.7, bf16[2,256,256]{2,1,0:T(8,128)(2,1)S(1)} %copy-done.11, bf16[2,256,256]{2,1,0:T(8,128)(2,1)S(1)} %copy-done.13, ...), custom_call_target="tpu_custom_call" | custom-call | flops 9663676416 | bytes 14155776 | tf_op jit(solution)/shard_map/blur/pallas_call | solution.py:612
  640.4 97.2 %all_to_all.50.got_ref = f32[32,8,2,2,8,128]{5,4,3,2,1,0:T(8,128)S(1)} all-to-all(f32[32,8,2,2,8,128]{5,4,3,2,1,0:T(8,128)S(1)} %bitcast.18), channel_id=1, replica_groups=mesh['gz'=16,'gy'=2] {'gz','gy'}, dimensions={0} | all-to-all | bytes 8388608 | tf_op jit(solution)/shard_map/all_to_all | solution.py:625
  737.6 6.1 ratio.3
  743.7 97.2 %all_to_all.51 = f32[32,8,2,2,8,128]{5,4,3,2,1,0:T(8,128)S(1)} all-to-all(f32[32,8,2,2,8,128]{5,4,3,2,1,0:T(8,128)S(1)} %ratio.3), channel_id=1, replica_groups=mesh['gz'=16,'gy'=2] {'gz','gy'}, dimensions={0} | all-to-all | bytes 8388608 | tf_op jit(solution)/shard_map/all_to_all | solution.py:625
  840.8 11.8 %adjoint.3 = f32[16,2,8,2,2,8,128]{6,5,4,3,2,1,0:T(8,128)S(1)} custom-call(f32[16,2,8,2,2,8,128]{6,5,4,3,2,1,0:T(8,128)S(1)} %bitcast.15, f32[16,2,8,2,2,8,128]{6,5,4,3,2,1,0:T(8,128)S(1)} %bitcast.14, bf16[2,4,128,256]{3,2,1,0:T(8,128)(2,1)S(1)} %copy-done.7, bf16[2,256,256]{2,1,0:T(8,128)(2,1)S(1)} %copy-done.11, bf16[2,256,256]{2,1,0:T(8,128)(2,1)S(1)} %copy-done.12, ...), custom_call_target="tpu_custom_call" | custom-call | flops 9663676416 | bytes 14680064 | tf_op jit(solution)/shard_map/adjoint/pallas_call | solution.py:612
  852.6 97.2 %all_to_all.52.got_ref = f32[32,8,2,2,8,128]{5,4,3,2,1,0:T(8,128)S(1)} all-to-all(f32[32,8,2,2,8,128]{5,4,3,2,1,0:T(8,128)S(1)} %bitcast.16), channel_id=1, replica_groups=mesh['gz'=16,'gy'=2] {'gz','gy'}, dimensions={0} | all-to-all | bytes 8388608 | tf_op jit(solution)/shard_map/all_to_all | solution.py:625
  949.8 5.5 last.1
  (1 shorter events, 0.0 us)
Async XLA Ops:
  6.4 7.5 copy-start.15
  6.4 7.5 copy-start.5
  6.5 7.5 copy-start.14
  6.5 101.2 %all-to-all-start = ((f32[32,8,2,2,8,128]{5,4,3,2,1,0:T(8,128)}), f32[32,8,2,2,8,128]{5,4,3,2,1,0:T(8,128)}, u32[]{:S(2)}, u32[]{:S(2)}) async-start(f32[32,8,2,2,8,128]{5,4,3,2,1,0:T(8,128)} %first.1), calls=%async_computation | async-start | bytes 8388608 | tf_op jit(solution)/shard_map/all_to_all | solution.py:625
  14.0 1.6 copy-start.6
  19.2 2.0 copy-start.2
  21.2 184.9 %copy-start.7 = (bf16[2,4,128,256]{3,2,1,0:T(8,128)(2,1)S(1)}, bf16[2,4,128,256]{3,2,1,0:T(8,128)(2,1)}, u32[]{:S(2)}) copy-start(bf16[2,4,128,256]{3,2,1,0:T(8,128)(2,1)} %constant.37.clone.refs_1_) | copy-start | bytes 1572868
  21.2 184.9 %copy-start.10 = (bf16[2,4,128,256]{3,2,1,0:T(8,128)(2,1)S(1)}, bf16[2,4,128,256]{3,2,1,0:T(8,128)(2,1)}, u32[]{:S(2)}) copy-start(bf16[2,4,128,256]{3,2,1,0:T(8,128)(2,1)} %constant.38.clone.refs_4_) | copy-start | bytes 1572868
  21.2 184.9 %copy-start.11 = (bf16[2,256,256]{2,1,0:T(8,128)(2,1)S(1)}, bf16[2,256,256]{2,1,0:T(8,128)(2,1)}, u32[]{:S(2)}) copy-start(bf16[2,256,256]{2,1,0:T(8,128)(2,1)} %constant.41.clone.refs_2_) | copy-start | bytes 786436
  21.2 184.9 %copy-start.13 = (bf16[2,256,256]{2,1,0:T(8,128)(2,1)S(1)}, bf16[2,256,256]{2,1,0:T(8,128)(2,1)}, u32[]{:S(2)}) copy-start(bf16[2,256,256]{2,1,0:T(8,128)(2,1)} %constant.42.clone.refs_3_) | copy-start | bytes 786436
  217.9 97.2 %copy-start = (f32[8,256,512]{2,1,0:T(8,128)S(1)}, f32[8,256,512]{2,1,0:T(8,128)}, u32[]{:S(2)}) copy-start(f32[8,256,512]{2,1,0:T(8,128)} %measured_ref.3) | copy-start | bytes 12582916
  217.9 97.2 %copy-start.1 = (bf16[2,2,256,256]{3,2,1,0:T(8,128)(2,1)S(1)}, bf16[2,2,256,256]{3,2,1,0:T(8,128)(2,1)}, u32[]{:S(2)}) copy-start(bf16[2,2,256,256]{3,2,1,0:T(8,128)(2,1)} %constant.34.clone.xa_ref) | copy-start | bytes 1572868
  217.9 97.2 %copy-start.3 = (bf16[2,2,256,256]{3,2,1,0:T(8,128)(2,1)S(1)}, bf16[2,2,256,256]{3,2,1,0:T(8,128)(2,1)}, u32[]{:S(2)}) copy-start(bf16[2,2,256,256]{3,2,1,0:T(8,128)(2,1)} %constant.35.clone.xb_ref) | copy-start | bytes 1572868
  321.2 97.2 %copy-start.8 = (bf16[2,512,256]{2,1,0:T(8,128)(2,1)S(1)}, bf16[2,512,256]{2,1,0:T(8,128)(2,1)}, u32[]{:S(2)}) copy-start(bf16[2,512,256]{2,1,0:T(8,128)(2,1)} %constant.40.clone.refs_5_) | copy-start | bytes 1572868
  321.2 97.2 %copy-start.9 = (bf16[2,4,128,256]{3,2,1,0:T(8,128)(2,1)S(1)}, bf16[2,4,128,256]{3,2,1,0:T(8,128)(2,1)}, u32[]{:S(2)}) copy-start(bf16[2,4,128,256]{3,2,1,0:T(8,128)(2,1)} %constant.39.clone.refs_4_) | copy-start | bytes 1572868
  321.2 97.2 %copy-start.12 = (bf16[2,256,256]{2,1,0:T(8,128)(2,1)S(1)}, bf16[2,256,256]{2,1,0:T(8,128)(2,1)}, u32[]{:S(2)}) copy-start(bf16[2,256,256]{2,1,0:T(8,128)(2,1)} %constant.43.clone.refs_3_) | copy-start | bytes 786436
  430.2 97.2 %copy-start.4 = (bf16[2,512,512]{2,1,0:T(8,128)(2,1)S(1)}, bf16[2,512,512]{2,1,0:T(8,128)(2,1)}, u32[]{:S(2)}) copy-start(bf16[2,512,512]{2,1,0:T(8,128)(2,1)} %constant.36.clone.xb_ref) | copy-start | bytes 3145732

commit v8 on v7

--- a/solution.py
+++ b/solution.py
@@ -405,8 +405,11 @@
     volume_ref[:, rows, half:] = right.reshape(shape)
 
 
-def first_kernel(volume_ref, xa_ref, send_ref, volume_buf, send_buf, in_sems, out_sems):
+def first_kernel(
+    volume_ref, table_ref, send_ref, volume_buf, send_buf, xa_ref, in_sems, out_sems, table_sem
+):
     tiles = send_ref.shape[3]
+    copy_table = pltpu.make_async_copy(table_ref, xa_ref, table_sem)
 
     def copy_in(tile):
         rows = pl.ds(pl.multiple_of(tile * LANES, LANES), LANES)
@@ -417,8 +420,10 @@
             send_buf.at[tile], send_ref.at[:, :, :, pl.ds(tile, 1)], out_sems.at[tile]
         )
 
+    copy_table.start()
     for tile in range(tiles):
         copy_in(tile).start()
+    copy_table.wait()
 
     @pl.loop(0, tiles)
     def _(tile):
@@ -602,7 +607,7 @@
 
 KX_AT_ONCE = 4
 VMEM_BYTES = 32 * 2**20
-ALL_VMEM_BYTES = 59 * 2**20
+FIRST_VMEM_BYTES = 59 * 2**20
 
 
 def call(kernel, arrays, outs, flops, name, specs=(), out_spec=None, scratch=(), vmem=None):
@@ -649,8 +654,12 @@
 
     def first(values):
         return call(
-            first_kernel, (values, xa), spectrum, line_flops, "first", (far,), far,
-            (volume_tiles, spectrum_tiles, sems, sems), ALL_VMEM_BYTES,
+            first_kernel, (values, xa), spectrum, line_flops, "first", (far, far), far,
+            (
+                volume_tiles, spectrum_tiles, pltpu.VMEM(xa.shape, xa.dtype), sems, sems,
+                pltpu.SemaphoreType.DMA,
+            ),
+            FIRST_VMEM_BYTES,
         )
 
     def ratio(got, values):

time: 956 us -> 955 us (level)
  no operation moved by 1% of the time
where the time goes in v8:
time: 955 us
  blocking collectives  779 us (82%)
  waiting for transfers between devices  86.4 us (9%)
  Pallas kernels  78 us (8%)
    all_to_all x8, blocking collectives, exchange(): lax.all_to_all(values, ('gz', 'gy'), split_axis=0, concat_axis=0, tiled=T...  779 us
    all_to_all x1, waiting for transfers between devices, exchange(): lax.all_to_all(values, ('gz', 'gy'), split_axis=0, concat_axis=0, tiled=T...  86.4 us
    pallas_call x10, Pallas kernels, call(): pl.pallas_call(kernel, in_specs=[*specs, *[spec] * (len(arrays) - len(spe...  78 us
  transfers between devices with their start and end apart: 1, of which 1 were waited for; matrix products, arithmetic and copies ran while one was open for 0% of the time, Pallas kernels for 0%

profile of v8, /device:TPU:0, one launch (start us, length us, event | category | flops | bytes accessed | tf_op | source)
XLA Modules:
  0.0 954.6 jit_solution(17153336152476528354)
XLA Ops:
  0.0 5.5 first.1
  5.5 0.0 copy-start.15
  5.5 0.0 copy-start.5
  5.5 0.0 copy-start.14
  5.5 7.4 all-to-all-start
  13.0 0.0 copy-done.15
  13.0 0.0 copy-done.5
  13.0 0.0 copy-done.14
  13.0 0.0 copy-start.6
  13.0 1.6 copy-done.6
  14.6 3.6 arrange.1
  18.3 0.0 copy-start.2
  18.3 2.0 copy-done.2
  20.2 0.0 copy-start.7
  20.2 0.0 copy-start.10
  20.2 0.0 copy-start.11
  20.3 0.0 copy-start.13
  20.3 86.4 %all-to-all-done = f32[32,8,2,2,8,128]{5,4,3,2,1,0:T(8,128)} async-done(((f32[32,8,2,2,8,128]{5,4,3,2,1,0:T(8,128)}), f32[32,8,2,2,8,128]{5,4,3,2,1,0:T(8,128)}, u32[]{:S(2)}, u32[]{:S(2)}) %all-to-all-start) | async-done | bytes 4194336 | tf_op jit(solution)/shard_map/all_to_all | solution.py:630
  106.7 98.4 %all_to_all.45 = f32[32,8,2,2,8,128]{5,4,3,2,1,0:T(8,128)S(1)} all-to-all(f32[32,8,2,2,8,128]{5,4,3,2,1,0:T(8,128)} %copy-done.2), channel_id=1, replica_groups=mesh['gz'=16,'gy'=2] {'gz','gy'}, dimensions={0} | all-to-all | bytes 8388608 | tf_op jit(solution)/shard_map/all_to_all | solution.py:630
  205.1 0.0 copy-done.7
  205.1 0.0 copy-done.10
  205.1 0.0 copy-done.11
  205.1 0.0 copy-done.13
  205.1 11.8 %blur.2 = f32[16,2,8,2,2,8,128]{6,5,4,3,2,1,0:T(8,128)S(1)} custom-call(f32[16,2,8,2,2,8,128]{6,5,4,3,2,1,0:T(8,128)} %bitcast.got_ref, f32[16,2,8,2,2,8,128]{6,5,4,3,2,1,0:T(8,128)S(1)} %bitcast.11, bf16[2,4,128,256]{3,2,1,0:T(8,128)(2,1)S(1)} %copy-done.7, bf16[2,256,256]{2,1,0:T(8,128)(2,1)S(1)} %copy-done.11, bf16[2,256,256]{2,1,0:T(8,128)(2,1)S(1)} %copy-done.13, ...), custom_call_target="tpu_custom_call" | custom-call | flops 9663676416 | bytes 14155776 | tf_op jit(solution)/shard_map/blur/pallas_call | solution.py:617
  216.9 0.0 copy-start
  216.9 0.0 copy-start.1
  216.9 0.0 copy-start.3
  217.0 97.2 %all_to_all.46.got_ref = f32[32,8,2,2,8,128]{5,4,3,2,1,0:T(8,128)S(1)} all-to-all(f32[32,8,2,2,8,128]{5,4,3,2,1,0:T(8,128)S(1)} %bitcast.19), channel_id=1, replica_groups=mesh['gz'=16,'gy'=2] {'gz','gy'}, dimensions={0} | all-to-all | bytes 8388608 | tf_op jit(solution)/shard_map/all_to_all | solution.py:630
  314.1 0.0 copy-done
  314.1 0.0 copy-done.1
  314.1 0.0 copy-done.3
  314.1 6.1 ratio.2
  320.3 0.0 copy-start.8
  320.3 0.0 copy-start.9
  320.3 0.0 copy-start.12
  320.3 97.2 %all_to_all.47 = f32[32,8,2,2,8,128]{5,4,3,2,1,0:T(8,128)S(1)} all-to-all(f32[32,8,2,2,8,128]{5,4,3,2,1,0:T(8,128)S(1)} %ratio.2), channel_id=1, replica_groups=mesh['gz'=16,'gy'=2] {'gz','gy'}, dimensions={0} | all-to-all | bytes 8388608 | tf_op jit(solution)/shard_map/all_to_all | solution.py:630
  417.5 0.0 copy-done.8
  417.5 0.0 copy-done.9
  417.5 0.0 copy-done.12
  417.5 11.8 %adjoint.2 = f32[16,2,8,2,2,8,128]{6,5,4,3,2,1,0:T(8,128)S(1)} custom-call(f32[16,2,8,2,2,8,128]{6,5,4,3,2,1,0:T(8,128)S(1)} %bitcast.20, f32[16,2,8,2,2,8,128]{6,5,4,3,2,1,0:T(8,128)S(1)} %bitcast.12, bf16[2,4,128,256]{3,2,1,0:T(8,128)(2,1)S(1)} %copy-done.7, bf16[2,256,256]{2,1,0:T(8,128)(2,1)S(1)} %copy-done.11, bf16[2,256,256]{2,1,0:T(8,128)(2,1)S(1)} %copy-done.12, ...), custom_call_target="tpu_custom_call" | custom-call | flops 9663676416 | bytes 14680064 | tf_op jit(solution)/shard_map/adjoint/pallas_call | solution.py:617
  429.3 0.0 copy-start.4
  429.3 97.2 %all_to_all.48.got_ref = f32[32,8,2,2,8,128]{5,4,3,2,1,0:T(8,128)S(1)} all-to-all(f32[32,8,2,2,8,128]{5,4,3,2,1,0:T(8,128)S(1)} %bitcast.21), channel_id=1, replica_groups=mesh['gz'=16,'gy'=2] {'gz','gy'}, dimensions={0} | all-to-all | bytes 8388608 | tf_op jit(solution)/shard_map/all_to_all | solution.py:630
  526.4 0.0 copy-done.4
  526.4 6.2 correct.1
  532.6 97.2 %all_to_all.49 = f32[32,8,2,2,8,128]{5,4,3,2,1,0:T(8,128)S(1)} all-to-all(f32[32,8,2,2,8,128]{5,4,3,2,1,0:T(8,128)S(1)} %get-tuple-element.11), channel_id=1, replica_groups=mesh['gz'=16,'gy'=2] {'gz','gy'}, dimensions={0} | all-to-all | bytes 8388608 | tf_op jit(solution)/shard_map/all_to_all | solution.py:630
  629.8 9.6 %blur.3 = f32[16,2,8,2,2,8,128]{6,5,4,3,2,1,0:T(8,128)S(1)} custom-call(f32[16,2,8,2,2,8,128]{6,5,4,3,2,1,0:T(8,128)S(1)} %bitcast.17, f32[16,2,8,2,2,8,128]{6,5,4,3,2,1,0:T(8,128)S(1)} %bitcast.13, bf16[2,4,128,256]{3,2,1,0:T(8,128)(2,1)S(1)} %copy-done.7, bf16[2,256,256]{2,1,0:T(8,128)(2,1)S(1)} %copy-done.11, bf16[2,256,256]{2,1,0:T(8,128)(2,1)S(1)} %copy-done.13, ...), custom_call_target="tpu_custom_call" | custom-call | flops 9663676416 | bytes 14155776 | tf_op jit(solution)/shard_map/blur/pallas_call | solution.py:617
  639.4 97.2 %all_to_all.50.got_ref = f32[32,8,2,2,8,128]{5,4,3,2,1,0:T(8,128)S(1)} all-to-all(f32[32,8,2,2,8,128]{5,4,3,2,1,0:T(8,128)S(1)} %bitcast.18), channel_id=1, replica_groups=mesh['gz'=16,'gy'=2] {'gz','gy'}, dimensions={0} | all-to-all | bytes 8388608 | tf_op jit(solution)/shard_map/all_to_all | solution.py:630
  736.6 6.1 ratio.3
  742.7 97.2 %all_to_all.51 = f32[32,8,2,2,8,128]{5,4,3,2,1,0:T(8,128)S(1)} all-to-all(f32[32,8,2,2,8,128]{5,4,3,2,1,0:T(8,128)S(1)} %ratio.3), channel_id=1, replica_groups=mesh['gz'=16,'gy'=2] {'gz','gy'}, dimensions={0} | all-to-all | bytes 8388608 | tf_op jit(solution)/shard_map/all_to_all | solution.py:630
  839.9 11.8 %adjoint.3 = f32[16,2,8,2,2,8,128]{6,5,4,3,2,1,0:T(8,128)S(1)} custom-call(f32[16,2,8,2,2,8,128]{6,5,4,3,2,1,0:T(8,128)S(1)} %bitcast.15, f32[16,2,8,2,2,8,128]{6,5,4,3,2,1,0:T(8,128)S(1)} %bitcast.14, bf16[2,4,128,256]{3,2,1,0:T(8,128)(2,1)S(1)} %copy-done.7, bf16[2,256,256]{2,1,0:T(8,128)(2,1)S(1)} %copy-done.11, bf16[2,256,256]{2,1,0:T(8,128)(2,1)S(1)} %copy-done.12, ...), custom_call_target="tpu_custom_call" | custom-call | flops 9663676416 | bytes 14680064 | tf_op jit(solution)/shard_map/adjoint/pallas_call | solution.py:617
  851.7 97.2 %all_to_all.52.got_ref = f32[32,8,2,2,8,128]{5,4,3,2,1,0:T(8,128)S(1)} all-to-all(f32[32,8,2,2,8,128]{5,4,3,2,1,0:T(8,128)S(1)} %bitcast.16), channel_id=1, replica_groups=mesh['gz'=16,'gy'=2] {'gz','gy'}, dimensions={0} | all-to-all | bytes 8388608 | tf_op jit(solution)/shard_map/all_to_all | solution.py:630
  948.8 5.5 last.1
  (1 shorter events, 0.0 us)
Async XLA Ops:
  5.5 7.5 copy-start.15
  5.5 7.5 copy-start.5
  5.5 7.5 copy-start.14
  5.5 101.2 %all-to-all-start = ((f32[32,8,2,2,8,128]{5,4,3,2,1,0:T(8,128)}), f32[32,8,2,2,8,128]{5,4,3,2,1,0:T(8,128)}, u32[]{:S(2)}, u32[]{:S(2)}) async-start(f32[32,8,2,2,8,128]{5,4,3,2,1,0:T(8,128)} %first.1), calls=%async_computation | async-start | bytes 8388608 | tf_op jit(solution)/shard_map/all_to_all | solution.py:630
  13.0 1.6 copy-start.6
  18.3 2.0 copy-start.2
  20.2 184.9 %copy-start.7 = (bf16[2,4,128,256]{3,2,1,0:T(8,128)(2,1)S(1)}, bf16[2,4,128,256]{3,2,1,0:T(8,128)(2,1)}, u32[]{:S(2)}) copy-start(bf16[2,4,128,256]{3,2,1,0:T(8,128)(2,1)} %constant.37.clone.refs_1_) | copy-start | bytes 1572868
  20.2 184.9 %copy-start.10 = (bf16[2,4,128,256]{3,2,1,0:T(8,128)(2,1)S(1)}, bf16[2,4,128,256]{3,2,1,0:T(8,128)(2,1)}, u32[]{:S(2)}) copy-start(bf16[2,4,128,256]{3,2,1,0:T(8,128)(2,1)} %constant.38.clone.refs_4_) | copy-start | bytes 1572868
  20.2 184.9 %copy-start.11 = (bf16[2,256,256]{2,1,0:T(8,128)(2,1)S(1)}, bf16[2,256,256]{2,1,0:T(8,128)(2,1)}, u32[]{:S(2)}) copy-start(bf16[2,256,256]{2,1,0:T(8,128)(2,1)} %constant.41.clone.refs_2_) | copy-start | bytes 786436
  20.3 184.9 %copy-start.13 = (bf16[2,256,256]{2,1,0:T(8,128)(2,1)S(1)}, bf16[2,256,256]{2,1,0:T(8,128)(2,1)}, u32[]{:S(2)}) copy-start(bf16[2,256,256]{2,1,0:T(8,128)(2,1)} %constant.42.clone.refs_3_) | copy-start | bytes 786436
  216.9 97.2 %copy-start = (f32[8,256,512]{2,1,0:T(8,128)S(1)}, f32[8,256,512]{2,1,0:T(8,128)}, u32[]{:S(2)}) copy-start(f32[8,256,512]{2,1,0:T(8,128)} %measured_ref.3) | copy-start | bytes 12582916
  216.9 97.2 %copy-start.1 = (bf16[2,2,256,256]{3,2,1,0:T(8,128)(2,1)S(1)}, bf16[2,2,256,256]{3,2,1,0:T(8,128)(2,1)}, u32[]{:S(2)}) copy-start(bf16[2,2,256,256]{3,2,1,0:T(8,128)(2,1)} %constant.34.clone.table_ref.xa_ref) | copy-start | bytes 1572868
  216.9 97.2 %copy-start.3 = (bf16[2,2,256,256]{3,2,1,0:T(8,128)(2,1)S(1)}, bf16[2,2,256,256]{3,2,1,0:T(8,128)(2,1)}, u32[]{:S(2)}) copy-start(bf16[2,2,256,256]{3,2,1,0:T(8,128)(2,1)} %constant.35.clone.xb_ref) | copy-start | bytes 1572868
  320.3 97.2 %copy-start.8 = (bf16[2,512,256]{2,1,0:T(8,128)(2,1)S(1)}, bf16[2,512,256]{2,1,0:T(8,128)(2,1)}, u32[]{:S(2)}) copy-start(bf16[2,512,256]{2,1,0:T(8,128)(2,1)} %constant.40.clone.refs_5_) | copy-start | bytes 1572868
  320.3 97.2 %copy-start.9 = (bf16[2,4,128,256]{3,2,1,0:T(8,128)(2,1)S(1)}, bf16[2,4,128,256]{3,2,1,0:T(8,128)(2,1)}, u32[]{:S(2)}) copy-start(bf16[2,4,128,256]{3,2,1,0:T(8,128)(2,1)} %constant.39.clone.refs_4_) | copy-start | bytes 1572868
  320.3 97.2 %copy-start.12 = (bf16[2,256,256]{2,1,0:T(8,128)(2,1)S(1)}, bf16[2,256,256]{2,1,0:T(8,128)(2,1)}, u32[]{:S(2)}) copy-start(bf16[2,256,256]{2,1,0:T(8,128)(2,1)} %constant.43.clone.refs_3_) | copy-start | bytes 786436
  429.3 97.2 %copy-start.4 = (bf16[2,512,512]{2,1,0:T(8,128)(2,1)S(1)}, bf16[2,512,512]{2,1,0:T(8,128)(2,1)}, u32[]{:S(2)}) copy-start(bf16[2,512,512]{2,1,0:T(8,128)(2,1)} %constant.36.clone.xb_ref) | copy-start | bytes 3145732
